TPU v7x, 32 devices: a whole 2x2x4 slice. The times are simulated.
32 devices in a mesh: dp: 16 (over z, x, core), seq: 2 (over y).
Axes of the slice: x: 2, y: 2, z: 4, core: 2. Of those that a mesh axis runs over, the one named last changes fastest.
Arguments:
- features: bfloat16 [16, 1024, 768], P('dp', 'seq'), may hold values from -2.5 to 2.5
- w_first: bfloat16 [2304, 768], P('dp'), may hold values from -0.125 to 0.125
- w_second: bfloat16 [2304, 768], P('dp'), may hold values from -0.125 to 0.125
- cotangent: bfloat16 [16, 1024, 768], P('dp', 'seq'), may hold values from -2.5 to 2.5
Outputs:
- tower_out: bfloat16 [16, 1024, 768], P('dp', 'seq')
- grad_input: bfloat16 [16, 1024, 768], P('dp', 'seq')
- grad_first: float32 [2304, 768], P('dp')
- grad_second: float32 [2304, 768], P('dp')
All inputs are finite; a program needn't handle non-finite values.
Results may differ from a plain program's by a relative error of at most 0.014.
Values may be sent and summed in bfloat16 or wider, within the bound.
No kernel may reach another device: no remote copies, remote signals or barrier semaphores. Data moves between devices by JAX's collectives and lax.ppermute only.
A program may use at most 128 MiB of HBM per device.

v0:
```python
import math

import jax
import jax.numpy as jnp
from jax import lax
from jax.sharding import PartitionSpec as P


def padded_2(block, sides, width):
    for axis, dim in sides:
        count = lax.axis_size(axis)
        forward = [(i, i + 1) for i in range(count - 1)]
        backward = [(target, source) for source, target in forward]
        low = lax.ppermute(
            lax.slice_in_dim(block, block.shape[dim] - width, None, axis=dim), axis, forward
        )
        high = lax.ppermute(lax.slice_in_dim(block, 0, width, axis=dim), axis, backward)
        block = jnp.concatenate([low, block, high], axis=dim)
    return block


def gelu_value(values):
    return values * 0.5 * (1.0 + lax.erf(values * 0.7071067811865476))


def gelu_slope(values):
    cumulative = 0.5 * (1.0 + lax.erf(values * 0.7071067811865476))
    density = jnp.exp(-0.5 * values * values) * 0.3989422804014327
    return cumulative + values * density


def stack_taps(padded, dilation, row_count):
    return jnp.concatenate(
        [padded[tap_index * dilation : tap_index * dilation + row_count] for tap_index in range(3)],
        axis=1,
    )


def spread_taps(product, dilation, row_count, channels):
    summed = product[2 * dilation : 2 * dilation + row_count, 0:channels]
    for tap_index in (1, 2):
        offset = (2 - tap_index) * dilation
        summed = (
            summed
            + product[
                offset : offset + row_count, tap_index * channels : (tap_index + 1) * channels
            ]
        )
    return summed


def forward_rim(values, depth):
    return padded_2(values, (("seq", 0),), depth)


def backward_rim(values, depth):
    return padded_2(values, (("seq", 0),), depth)


def forward_product(stacked, weight):
    return jnp.dot(
        stacked,
        lax.all_gather(weight, "dp", axis=0, tiled=True),
        preferred_element_type=jnp.float32,
    )


def backward_product(padded, weight):
    return lax.dot_general(
        padded,
        lax.all_gather(weight, "dp", axis=0, tiled=True),
        (((1,), (1,)), ((), ())),
        preferred_element_type=jnp.float32,
    )


def reduce_grad(stacked, upstream, grad_scale):
    owned = lax.psum_scatter(
        lax.dot_general(
            stacked, upstream, (((0,), (0,)), ((), ())), preferred_element_type=jnp.float32
        )
        * grad_scale,
        "dp",
        scatter_dimension=0,
        tiled=True,
    )
    result = lax.psum(owned, "seq")
    return result


def shards(features, w_first, w_second, cotangent):
    f32 = jnp.float32
    source = features[0]
    upstream = cotangent[0]
    row_count = source.shape[0]
    channels = source.shape[1]
    grad_scale = 1.0 / math.sqrt(row_count * lax.axis_size("seq") * lax.axis_size("dp"))
    act_first = gelu_value(source.astype(f32)).astype(jnp.bfloat16)
    stack_first = stack_taps(forward_rim(act_first, 4), 4, row_count)
    hidden = (source.astype(f32) + forward_product(stack_first, w_first)).astype(jnp.bfloat16)
    act_second = gelu_value(hidden.astype(f32)).astype(jnp.bfloat16)
    stack_second = stack_taps(forward_rim(act_second, 8), 8, row_count)
    tower = (hidden.astype(f32) + forward_product(stack_second, w_second)).astype(jnp.bfloat16)
    grad_second = reduce_grad(stack_second, upstream, grad_scale)
    padded_upstream = backward_rim(upstream, 8)
    product = backward_product(padded_upstream, w_second)
    grad_hidden = (
        upstream.astype(f32)
        + spread_taps(product, 8, row_count, channels) * gelu_slope(hidden.astype(f32))
    ).astype(jnp.bfloat16)
    padded_hidden = backward_rim(grad_hidden, 4)
    grad_first = reduce_grad(stack_first, grad_hidden, grad_scale)
    product = backward_product(padded_hidden, w_first)
    grad_input = (
        grad_hidden.astype(f32)
        + spread_taps(product, 4, row_count, channels) * gelu_slope(source.astype(f32))
    ).astype(jnp.bfloat16)
    return (tower[None], grad_input[None], grad_first, grad_second)


def solution(mesh):
    return jax.shard_map(
        shards,
        mesh=mesh,
        in_specs=(P("dp", "seq", None), P("dp", None), P("dp", None), P("dp", "seq", None)),
        out_specs=(P("dp", "seq", None), P("dp", "seq", None), P("dp", None), P("dp", None)),
        check_vma=False,
    )
```

profile of v0, /device:TPU:0, one launch (start us, length us, event | category | flops | bytes accessed | tf_op | source)
XLA Modules:
  0.0 353.8 jit_solution(2352449634978029814)
XLA Ops:
  7.2 0.7 all-gather.5.cloned.1.call-update
  7.9 0.7 all-gather.3.cloned.1.call-update
  8.7 0.7 slice_bitcast_fusion.1
  9.4 4.9 %collective-permute-start.4 = (bf16[8,768]{1,0:T(8,128)(2,1)S(1)}, bf16[8,768]{1,0:T(8,128)(2,1)S(1)}, u32[]{:S(2)}, u32[]{:S(2)}) collective-permute-start(bf16[8,768]{1,0:T(8,128)(2,1)S(1)} %get-tuple-element.10), channel_id=1, source_target_pairs={{0,1},{2,3},{4,5},{6,7},{8,9},{10,11},{12,13},{14,15},{16,17},{18,... | collective-permute-start | bytes 36872 | tf_op jit(solution)/shard_map/ppermute | solution.py:14
  14.3 1.3 collective-permute-start.5
  15.6 1.5 fusion.16
  17.1 4.5 %collective-permute-start = (bf16[4,768]{1,0:T(4,128)(2,1)S(1)}, bf16[4,768]{1,0:T(4,128)(2,1)S(1)}, u32[]{:S(2)}, u32[]{:S(2)}) collective-permute-start(bf16[4,768]{1,0:T(4,128)(2,1)S(1)} %get-tuple-element.14), channel_id=1, source_target_pairs={{0,1},{2,3},{4,5},{6,7},{8,9},{10,11},{12,13},{14,15},{16,17},{18,... | collective-permute-start | bytes 18440 | tf_op jit(solution)/shard_map/ppermute | solution.py:14
  21.6 1.3 collective-permute-start.1
  23.0 37.2 %all-gather.5.cloned.1.call-done = bf16[2304,768]{1,0:T(8,128)(2,1)} async-done(((bf16[144,768]{1,0:T(8,128)(2,1)}), bf16[2304,768]{1,0:T(8,128)(2,1)}) %all-gather.5.cloned.1.call-update) | async-done | bytes 3538960 | tf_op jit(solution)/shard_map/all_gather | solution.py:63
  60.2 6.6 %fusion.27 = f32[528,2304]{1,0:T(8,128)} fusion(bf16[2304,768]{1,0:T(8,128)(2,1)} %all-gather.5.cloned.1.call-done, bf16[8,768]{1,0:T(8,128)(2,1)S(1)} %collective-permute-done.5, bf16[512,768]{1,0:T(8,128)(2,1)} %bitcast.29, bf16[8,768]{1,0:T(8,128)(2,1)S(1)} %collective-permute-done.4), kind=kOutput, calls=%fused_computation.49 | convolution fusion | flops 1870995456 | bytes 9216000 | tf_op jit(solution)/shard_map/dot_general | solution.py:69
  66.8 41.9 %all-gather.3.cloned.1.call-done = bf16[2304,768]{1,0:T(8,128)(2,1)} async-done(((bf16[144,768]{1,0:T(8,128)(2,1)}), bf16[2304,768]{1,0:T(8,128)(2,1)}) %all-gather.3.cloned.1.call-update) | async-done | bytes 3538960 | tf_op jit(solution)/shard_map/all_gather | solution.py:63
  108.7 8.0 %fusion.14 = (bf16[512,768]{1,0:T(8,128)(2,1)S(1)}, bf16[512,768]{1,0:T(8,128)(2,1)}, bf16[512,768]{1,0:T(8,128)(2,1)}) fusion(f32[528,2304]{1,0:T(8,128)} %fusion.27, bf16[1,512,768]{2,1,0:T(8,128)(2,1)S(1)} %copy-done.1, bf16[2304,768]{1,0:T(8,128)(2,1)} %all-gather.3.cloned.1.call-done, bf16[4,768]{1,0:T(4,128)(2,1)S(1)} %collective-permute-done.1, ...), kind=kOutput, calls=%fused_computation.32 | convolution fusion | flops 1831993344 | bytes 12988416 | tf_op jit(solution)/shard_map/dot_general | solution.py:61
  116.8 5.3 %convolution_multiply_fusion.1 = f32[2304,768]{1,0:T(8,128)} fusion(bf16[512,768]{1,0:T(8,128)(2,1)S(1)} %get-tuple-element.8, bf16[4,768]{1,0:T(4,128)(2,1)S(1)} %collective-permute-done.1, bf16[512,768]{1,0:T(8,128)(2,1)S(1)} %fusion.16, bf16[4,768]{1,0:T(4,128)(2,1)S(1)} %collective-permute-done), kind=kOutput, calls=%fused_computation.1 | convolution fusion | flops 1825505280 | bytes 8663040 | tf_op jit(solution)/shard_map/dot_general | solution.py:79
  122.0 0.0 reduce-scatter.5.cloned.1.call-start
  122.1 1.1 copy-done.2
  123.1 3.4 collective-permute-start.2
  126.5 1.3 collective-permute-start.3
  127.8 0.1 collective-permute-done.2
  127.9 4.2 %collective-permute-done.3 = bf16[8,768]{1,0:T(8,128)(2,1)S(1)} collective-permute-done((bf16[8,768]{1,0:T(8,128)(2,1)S(1)}, bf16[8,768]{1,0:T(8,128)(2,1)S(1)}, u32[]{:S(2)}, u32[]{:S(2)}) %collective-permute-start.3) | collective-permute-done | bytes 12320 | tf_op jit(solution)/shard_map/ppermute | solution.py:17
  132.1 5.2 %convolution_multiply_fusion = f32[2304,768]{1,0:T(8,128)} fusion(bf16[8,768]{1,0:T(8,128)(2,1)S(1)} %collective-permute-done.3, bf16[512,768]{1,0:T(8,128)(2,1)S(1)} %copy-done.2, bf16[8,768]{1,0:T(8,128)(2,1)S(1)} %collective-permute-done.2, bf16[1,512,768]{2,1,0:T(8,128)(2,1)S(1)} %copy-done.1), kind=kOutput, calls=%fused_computation | convolution fusion | flops 1825505280 | bytes 8675328 | tf_op jit(solution)/shard_map/dot_general | solution.py:79
  137.3 0.0 all-reduce.3.cloned.1.call-start
  137.3 1.6 collective-permute-start.6
  139.0 1.3 collective-permute-start.7
  140.3 4.2 %collective-permute-done.7 = bf16[4,768]{1,0:T(4,128)(2,1)S(1)} collective-permute-done((bf16[4,768]{1,0:T(4,128)(2,1)S(1)}, bf16[4,768]{1,0:T(4,128)(2,1)S(1)}, u32[]{:S(2)}, u32[]{:S(2)}) %collective-permute-start.7) | collective-permute-done | bytes 6176 | tf_op jit(solution)/shard_map/ppermute | solution.py:17
  144.5 6.2 %fusion.33 = f32[520,2304]{1,0:T(8,128)} fusion(bf16[2304,768]{1,0:T(8,128)(2,1)} %all-gather.3.cloned.1.call-done, bf16[4,768]{1,0:T(4,128)(2,1)S(1)} %collective-permute-done.7, bf16[512,768]{1,0:T(8,128)(2,1)S(1)} %get-tuple-element.8, bf16[4,768]{1,0:T(4,128)(2,1)S(1)} %collective-permute-done.6), kind=kOutput, calls=%fused_computation.55 | convolution fusion | flops 1842647040 | bytes 9129984 | tf_op jit(solution)/shard_map/dot_general | solution.py:69
  150.7 60.5 %reduce-scatter.3.cloned.1.call-done = f32[144,768]{1,0:T(8,128)} async-done(((f32[2304,768]{1,0:T(8,128)}), f32[144,768]{1,0:T(8,128)}) %reduce-scatter.3.cloned.1.call-update) | async-done | bytes 442384 | tf_op jit(solution)/shard_map/reduce_scatter | solution.py:78
  211.2 94.0 %reduce-scatter.5.cloned.1.call-done = f32[144,768]{1,0:T(8,128)} async-done(((f32[2304,768]{1,0:T(8,128)}), f32[144,768]{1,0:T(8,128)}) %reduce-scatter.5.cloned.1.call-update) | async-done | bytes 442384 | tf_op jit(solution)/shard_map/reduce_scatter | solution.py:78
  305.3 3.8 %fusion.39 = bf16[1,512,768]{2,1,0:T(8,128)(2,1)} fusion(bf16[1,512,768]{2,1,0:T(8,128)(2,1)S(1)} %copy-done, f32[520,2304]{1,0:T(8,128)} %fusion.33, bf16[512,768]{1,0:T(8,128)(2,1)S(1)} %get-tuple-element.8), kind=kLoop, calls=%fused_computation.61 | loop fusion | flops 5898240 | bytes 7077888 | tf_op jit(solution)/shard_map/broadcast_in_dim | solution.py:118
  309.1 4.4 %fusion.26 = bf16[1,512,768]{2,1,0:T(8,128)(2,1)} fusion(bf16[2304,768]{1,0:T(8,128)(2,1)S(1)} %copy-done.3, bf16[512,768]{1,0:T(8,128)(2,1)S(1)} %copy-done.4, bf16[8,768]{1,0:T(8,128)(2,1)S(1)} %collective-permute-done.3, bf16[512,768]{1,0:T(8,128)(2,1)S(1)} %copy-done.2, bf16[8,768]{1,0:T(8,128)(2,1)S(1)} %collective-permute-done.2), kind=kOutput, calls=%fused_computation.48 | convolution fusion | flops 1824915456 | bytes 5922816 | tf_op jit(solution)/shard_map/dot_general | solution.py:61
  313.5 30.1 %all-reduce.3.cloned.1.call-done = (f32[144,768]{1,0:T(8,128)}, f32[144,768]{1,0:T(8,128)}) async-done(((f32[144,768]{1,0:T(8,128)}, f32[144,768]{1,0:T(8,128)}), (f32[144,768]{1,0:T(8,128)}, f32[144,768]{1,0:T(8,128)})) %all-reduce.3.cloned.1.call-update) | async-done | bytes 884752 | tf_op jit(solution)/shard_map/psum | solution.py:87
  343.6 1.8 copy.10
  345.4 1.8 copy.11
  (23 shorter events, 0.2 us)
Async XLA Ops:
  7.2 53.0 %all-gather.5.cloned.1.call-start = ((), (), s32[]{:S(2)}) async-start(), calls=%async_computation.3 | async-start | bytes 3760128 | tf_op jit(solution)/shard_map/all_gather | solution.py:63
  7.9 100.8 %all-gather.3.cloned.1.call-start = ((), (), s32[]{:S(2)}) async-start(), calls=%async_computation.2 | async-start | bytes 3760128 | tf_op jit(solution)/shard_map/all_gather | solution.py:63
  8.6 202.6 %reduce-scatter.3.cloned.1.call-start = ((), (), s32[]{:S(2)}) async-start(), calls=%async_computation.4 | async-start | bytes 7520256 | tf_op jit(solution)/shard_map/reduce_scatter | solution.py:78
  9.4 13.5 %collective-permute-start.4 = (bf16[8,768]{1,0:T(8,128)(2,1)S(1)}, bf16[8,768]{1,0:T(8,128)(2,1)S(1)}, u32[]{:S(2)}, u32[]{:S(2)}) collective-permute-start(bf16[8,768]{1,0:T(8,128)(2,1)S(1)} %get-tuple-element.10), channel_id=1, source_target_pairs={{0,1},{2,3},{4,5},{6,7},{8,9},{10,11},{12,13},{14,15},{16,17},{18,... | collective-permute-start | bytes 36872 | tf_op jit(solution)/shard_map/ppermute | solution.py:14
  14.3 8.7 %collective-permute-start.5 = (bf16[8,768]{1,0:T(8,128)(2,1)S(1)}, bf16[8,768]{1,0:T(8,128)(2,1)S(1)}, u32[]{:S(2)}, u32[]{:S(2)}) collective-permute-start(bf16[8,768]{1,0:T(8,128)(2,1)S(1)} %get-tuple-element.11), channel_id=1, source_target_pairs={{1,0},{3,2},{5,4},{7,6},{9,8},{11,10},{13,12},{15,14},{17,16},{19,... | collective-permute-start | bytes 36872 | tf_op jit(solution)/shard_map/ppermute | solution.py:17
  17.1 49.8 %collective-permute-start = (bf16[4,768]{1,0:T(4,128)(2,1)S(1)}, bf16[4,768]{1,0:T(4,128)(2,1)S(1)}, u32[]{:S(2)}, u32[]{:S(2)}) collective-permute-start(bf16[4,768]{1,0:T(4,128)(2,1)S(1)} %get-tuple-element.14), channel_id=1, source_target_pairs={{0,1},{2,3},{4,5},{6,7},{8,9},{10,11},{12,13},{14,15},{16,17},{18,... | collective-permute-start | bytes 18440 | tf_op jit(solution)/shard_map/ppermute | solution.py:14
  21.6 45.2 %collective-permute-start.1 = (bf16[4,768]{1,0:T(4,128)(2,1)S(1)}, bf16[4,768]{1,0:T(4,128)(2,1)S(1)}, u32[]{:S(2)}, u32[]{:S(2)}) collective-permute-start(bf16[4,768]{1,0:T(4,128)(2,1)S(1)} %get-tuple-element.15), channel_id=1, source_target_pairs={{1,0},{3,2},{5,4},{7,6},{9,8},{11,10},{13,12},{15,14},{17,16},{19,... | collective-permute-start | bytes 18440 | tf_op jit(solution)/shard_map/ppermute | solution.py:17
  60.2 48.5 %copy-start = (bf16[1,512,768]{2,1,0:T(8,128)(2,1)S(1)}, bf16[1,512,768]{2,1,0:T(8,128)(2,1)}, u32[]{:S(2)}) copy-start(bf16[1,512,768]{2,1,0:T(8,128)(2,1)} %param.4) | copy-start | bytes 2359300
  60.2 48.5 %copy-start.1 = (bf16[1,512,768]{2,1,0:T(8,128)(2,1)S(1)}, bf16[1,512,768]{2,1,0:T(8,128)(2,1)}, u32[]{:S(2)}) copy-start(bf16[1,512,768]{2,1,0:T(8,128)(2,1)} %param.7) | copy-start | bytes 2359300
  122.0 1.1 copy-start.2
  122.0 183.2 %reduce-scatter.5.cloned.1.call-start = ((), (), s32[]{:S(2)}) async-start(), calls=%async_computation.5 | async-start | bytes 7520256 | tf_op jit(solution)/shard_map/reduce_scatter | solution.py:78
  123.1 4.8 %collective-permute-start.2 = (bf16[8,768]{1,0:T(8,128)(2,1)S(1)}, bf16[8,768]{1,0:T(8,128)(2,1)S(1)}, u32[]{:S(2)}, u32[]{:S(2)}) collective-permute-start(bf16[8,768]{1,0:T(8,128)(2,1)S(1)} %get-tuple-element.12), channel_id=1, source_target_pairs={{0,1},{2,3},{4,5},{6,7},{8,9},{10,11},{12,13},{14,15},{16,17},{18,... | collective-permute-start | bytes 36872 | tf_op jit(solution)/shard_map/ppermute | solution.py:14
  126.5 5.6 %collective-permute-start.3 = (bf16[8,768]{1,0:T(8,128)(2,1)S(1)}, bf16[8,768]{1,0:T(8,128)(2,1)S(1)}, u32[]{:S(2)}, u32[]{:S(2)}) collective-permute-start(bf16[8,768]{1,0:T(8,128)(2,1)S(1)} %get-tuple-element.13), channel_id=1, source_target_pairs={{1,0},{3,2},{5,4},{7,6},{9,8},{11,10},{13,12},{15,14},{17,16},{19,... | collective-permute-start | bytes 36872 | tf_op jit(solution)/shard_map/ppermute | solution.py:17
  137.3 206.4 %all-reduce.3.cloned.1.call-start = ((), (), s32[]{:S(2)}) async-start(), calls=%async_computation.6 | async-start | bytes 1769472 | tf_op jit(solution)/shard_map/psum | solution.py:87
  137.3 3.0 collective-permute-start.6
  139.0 5.5 %collective-permute-start.7 = (bf16[4,768]{1,0:T(4,128)(2,1)S(1)}, bf16[4,768]{1,0:T(4,128)(2,1)S(1)}, u32[]{:S(2)}, u32[]{:S(2)}) collective-permute-start(bf16[4,768]{1,0:T(4,128)(2,1)S(1)} %get-tuple-element.7), channel_id=1, source_target_pairs={{1,0},{3,2},{5,4},{7,6},{9,8},{11,10},{13,12},{15,14},{17,16},{19,... | collective-permute-start | bytes 18440 | tf_op jit(solution)/shard_map/ppermute | solution.py:17
  305.3 3.8 %copy-start.3 = (bf16[2304,768]{1,0:T(8,128)(2,1)S(1)}, bf16[2304,768]{1,0:T(8,128)(2,1)}, u32[]{:S(2)}) copy-start(bf16[2304,768]{1,0:T(8,128)(2,1)} %all-gather.5.cloned.1.call-done) | copy-start | bytes 10616836
  305.3 3.8 %copy-start.4 = (bf16[512,768]{1,0:T(8,128)(2,1)S(1)}, bf16[512,768]{1,0:T(8,128)(2,1)}, u32[]{:S(2)}) copy-start(bf16[512,768]{1,0:T(8,128)(2,1)} %get-tuple-element.16) | copy-start | bytes 2359300
Sparse Core Ops, SparseCore 0:
  10.3 49.8 all-gather.4
  62.5 46.1 all-gather.2
  122.2 89.0 reduce-scatter.2
  215.6 89.5 reduce-scatter.4
  307.5 36.1 all-reduce.2
where the time goes:
time: 354 us
  waiting for transfers between devices  274 us (77%)
  matrix products  35.7 us (10%)
  starting transfers between devices  19.8 us (6%)
  between operations  13.9 us (4%)
  local copies, waits for them, and re-layouts  5.44 us (2%)
  other arithmetic  5.24 us (1%)
    reduce_scatter x2, waiting for transfers between devices, reduce_grad(): lax.psum_scatter(lax.dot_general(stacked, upstream, (((0,), (0,)), ((), (...  154 us
    all_gather x2, waiting for transfers between devices, forward_product(): lax.all_gather(weight, 'dp', axis=0, tiled=True)  79.1 us
    psum x1, waiting for transfers between devices, reduce_grad(): result = lax.psum(owned, 'seq')  30.1 us
    ppermute x4, starting transfers between devices, padded_2(): lax.ppermute(lax.slice_in_dim(block, block.shape[dim] - width, None, axis...  14.4 us
    dot_general x2, matrix products, backward_product(): lax.dot_general(padded, lax.all_gather(weight, 'dp', axis=0, tiled=True),...  12.9 us
    dot_general x2, matrix products, forward_product(): jnp.dot(stacked, lax.all_gather(weight, 'dp', axis=0, tiled=True), prefer...  12.5 us
    dot_general x2, matrix products, reduce_grad(): lax.dot_general(stacked, upstream, (((0,), (0,)), ((), ())), preferred_el...  10.4 us
    ppermute x4, waiting for transfers between devices, padded_2(): lax.ppermute(lax.slice_in_dim(block, 0, width, axis=dim), axis, backward)  8.4 us
  transfers between devices with their start and end apart: 13, of which 8 were waited for; matrix products, arithmetic and copies ran while one was open for 8% of the time, Pallas kernels for 0%

commit v1 on v0

v1 whole, which is shorter than its diff:
```python
import math

import jax
import jax.numpy as jnp
from jax import lax
from jax.sharding import PartitionSpec as P

F32 = jnp.float32
BF16 = jnp.bfloat16
HALO = 16
EDGE = 8


def gelu_value(values):
    return values * 0.5 * (1.0 + lax.erf(values * 0.7071067811865476))


def gelu_slope(values):
    cumulative = 0.5 * (1.0 + lax.erf(values * 0.7071067811865476))
    density = jnp.exp(-0.5 * values * values) * 0.3989422804014327
    return cumulative + values * density


def after(value, *others):
    return lax.optimization_barrier((value,) + others)[0]


def shards(features, w_first, w_second, cotangent):
    parts = lax.axis_size("dp")
    seqs = lax.axis_size("seq")
    place, me_y = lax.axis_index("dp"), lax.axis_index("seq")
    depth = parts // 4
    core, me_x, me_z = place % 2, (place // 2) % 2, place // 4
    h = me_y % 2
    rows, channels = features.shape[1], features.shape[2]
    block = w_first.shape[0]
    half = channels // 2
    grad_scale = 1.0 / math.sqrt(rows * seqs * parts)

    core_pairs = [(i, i ^ 1) for i in range(parts)]
    x_pairs = [(i, i ^ 2) for i in range(parts)]
    y_pairs = [(i, i ^ 1) for i in range(seqs)]

    def turn(step):
        return [(i, (i - 4 * step) % parts) for i in range(parts)]

    def by_core(mine, theirs, axis):
        first = jnp.where(core == 0, mine, theirs)
        second = jnp.where(core == 0, theirs, mine)
        return jnp.concatenate([first, second], axis=axis)

    def half_of(array, index, axis):
        return lax.dynamic_slice_in_dim(array, index * half, half, axis=axis)

    def take(array, index, axis):
        return lax.dynamic_index_in_dim(array, index, axis, keepdims=False)

    both = jnp.stack([w_first, w_second])
    given = lax.ppermute(half_of(both, 1 - core, 2), "dp", core_pairs)
    kept = half_of(both, core, 2)
    pair = jnp.stack(
        [jnp.where(core == 0, kept, given), jnp.where(core == 0, given, kept)], axis=1
    )

    joined = jnp.concatenate([features[0], cotangent[0]], axis=1)
    if seqs == 2:
        rim = jnp.where(h == 0, joined[rows - HALO :], joined[:HALO])
        rim = lax.ppermute(rim, "seq", y_pairs)
        none = jnp.zeros_like(rim)
        low, high = jnp.where(h == 0, none, rim), jnp.where(h == 0, rim, none)
    else:
        onward = [(i, i + 1) for i in range(seqs - 1)]
        back = [(i + 1, i) for i in range(seqs - 1)]
        low = lax.ppermute(joined[rows - HALO :], "seq", onward)
        high = lax.ppermute(joined[:HALO], "seq", back)

    def gather(which, x_pair, *others):
        piece = after(lax.dynamic_index_in_dim(pair[which], h, 0, keepdims=False), *others)
        turned = jnp.stack(
            [lax.ppermute(piece, "dp", turn(step)) for step in range(1, depth)]
        )
        from_x = lax.ppermute(turned, "dp", x_pairs)
        from_y = lax.ppermute(turned, "seq", y_pairs)
        by_y = lax.ppermute(from_x[: depth // 2], "seq", y_pairs)
        by_x = lax.ppermute(from_y[depth // 2 :], "dp", x_pairs)

        return pair[which], x_pair[which], turned, from_x, from_y, by_y, by_x

    def assemble(own, across, turned, from_x, from_y, by_y, by_x):
        both_in = jnp.concatenate([by_y, by_x], axis=0)

        def on(flag, here, there, axis):
            return jnp.stack(
                [jnp.where(flag == 0, here, there), jnp.where(flag == 0, there, here)], axis=axis
            )

        near, far = on(h, turned, from_y, 1), on(h, from_x, both_in, 1)
        near = jnp.concatenate([own[None], near], axis=0)
        far = jnp.concatenate([across[None], far], axis=0)
        lines = on(me_x, near, far, 1)
        lines = jnp.concatenate([lines, lines], axis=0)
        lines = lax.dynamic_slice_in_dim(lines, (depth - me_z) % depth, depth, axis=0)
        return lines.reshape(parts * block, half)

    x_pair = lax.ppermute(after(pair, low, high), "dp", x_pairs)
    first_pieces = gather(0, x_pair, low, high)
    second_pieces = gather(1, x_pair, first_pieces[2])

    extended = after(jnp.concatenate([low, joined, high], axis=0), first_pieces[2])
    partner = lax.ppermute(extended, "dp", core_pairs)
    pairs = jnp.stack([extended, partner])
    features_two, cot_two = pairs[..., :channels], pairs[..., channels:]
    act_first = gelu_value(features_two.astype(F32)).astype(BF16)
    wide = rows + 2 * EDGE

    def shifted(array, offset, count):
        return lax.slice_in_dim(array, offset, offset + count, axis=1)

    stack_first = jnp.concatenate(
        [shifted(act_first, HALO - EDGE + (tap - 1) * 4, wide) for tap in range(3)], axis=2
    )
    cot_halves = [half_of(cot_two, core, 2), half_of(cot_two, 1 - core, 2)]
    stack_cot = jnp.concatenate(
        [
            shifted(side, HALO - EDGE - (tap - 1) * 8, wide)
            for tap in range(3)
            for side in cot_halves
        ],
        axis=2,
    )
    cot_base = shifted(cot_halves[0], HALO - EDGE, wide)
    row = lax.broadcasted_iota(jnp.int32, (1, wide, 1), 1)
    valid = (row >= jnp.where(me_y == 0, EDGE, 0)) & (
        row < jnp.where(me_y == seqs - 1, wide - EDGE, wide)
    )
    slope_first = gelu_slope(features[0].astype(F32))

    first_base = shifted(half_of(features_two, core, 2), HALO - EDGE, wide)
    first_mine = assemble(*first_pieces)
    first_theirs = lax.ppermute(first_mine, "dp", core_pairs)
    hidden = (
        first_base.astype(F32) + jnp.dot(stack_first, first_mine, preferred_element_type=F32)
    ).astype(BF16)
    act_mine = jnp.where(valid, gelu_value(hidden.astype(F32)), 0.0).astype(BF16)
    act_theirs = lax.ppermute(act_mine, "dp", core_pairs)[::-1]
    act_second = by_core(act_mine, act_theirs, 2)
    stack_second = jnp.concatenate(
        [shifted(act_second, EDGE + (tap - 1) * 8, rows) for tap in range(3)], axis=2
    )

    def gradient(stacked, upstream):
        return (
            lax.dot_general(
                stacked.reshape(2 * rows, 3 * channels),
                upstream.reshape(2 * rows, half),
                (((0,), (0,)), ((), ())),
                preferred_element_type=F32,
            )
            * grad_scale
        ).astype(BF16)

    def add(left, right):
        return (left.astype(F32) + right.astype(F32)).astype(BF16)

    def plane_sum(grad):
        grad = grad.reshape(depth, 2, 2, block, half)
        cut = depth // 2
        one, two = grad[:cut], grad[cut:]
        one_in = lax.ppermute(take(one, 1 - me_x, 1), "dp", x_pairs)
        two_in = lax.ppermute(take(two, 1 - h, 2), "seq", y_pairs)
        return add(take(one, me_x, 1), one_in), add(take(two, h, 2), two_in)

    def plane_rest(one, two):
        one_in = lax.ppermute(take(one, 1 - h, 1), "seq", y_pairs)
        two_in = lax.ppermute(take(two, 1 - me_x, 1), "dp", x_pairs)
        one = add(take(one, h, 1), one_in)
        two = add(take(two, me_x, 1), two_in)
        return jnp.concatenate([one, two], axis=0)

    def line_sum(summed):
        total = take(summed, me_z, 0).astype(F32)
        for step in range(1, depth):
            out = take(summed, (me_z - step) % depth, 0)
            total = total + lax.ppermute(out, "dp", turn(step)).astype(F32)
        return total

    def finish(totals):
        if seqs > 2:
            groups = [[i for i in range(seqs) if i % 2 == k] for k in range(2)]
            totals = lax.psum(totals, "seq", axis_index_groups=groups)
        mine = totals.astype(BF16)
        theirs = lax.ppermute(mine, "seq", y_pairs)
        rows_two = jnp.stack(
            [jnp.where(h == 0, mine, theirs), jnp.where(h == 0, theirs, mine)], axis=0
        )
        kept = take(rows_two, core, 0)
        given = lax.ppermute(take(rows_two, 1 - core, 0), "dp", core_pairs)
        return by_core(kept, given, 2).astype(F32)

    grad_second = gradient(stack_second, shifted(cot_halves[0], HALO, rows))
    second_mine = assemble(*(after(piece, grad_second) for piece in second_pieces))
    second_theirs = lax.ppermute(second_mine, "dp", core_pairs)
    half_second = plane_sum(grad_second)
    plane_second = plane_rest(*half_second)

    slope = gelu_slope(hidden.astype(F32))
    blocks = jnp.stack(
        [take(side.reshape(3, 2, half, half), core, 1) for side in (second_mine, second_theirs)],
        axis=1,
    )
    spread = jnp.dot(
        after(stack_cot, *half_second),
        blocks.transpose(0, 1, 3, 2).reshape(3 * channels, half),
        preferred_element_type=F32,
    )
    grad_mine = jnp.where(valid, cot_base.astype(F32) + spread * slope, 0.0).astype(BF16)
    grad_first = gradient(shifted(stack_first, EDGE, rows), shifted(grad_mine, EDGE, rows))
    plane_first = plane_rest(*plane_sum(after(grad_first, plane_second)))

    tower_mine = (
        shifted(hidden, EDGE, rows).astype(F32)
        + jnp.dot(stack_second, second_mine, preferred_element_type=F32)
    ).astype(BF16)
    sent = jnp.concatenate([tower_mine[1], grad_mine[1]], axis=0)
    came = lax.ppermute(sent, "dp", core_pairs)
    tower = by_core(tower_mine[0], came[:rows], 1)
    grad_hidden = by_core(grad_mine[0], came[rows:], 1)

    w_first_whole = by_core(first_mine, first_theirs, 1).reshape(3, channels, channels)
    spread = None
    for tap in range(3):
        offset = EDGE - (tap - 1) * 4
        product = lax.dot_general(
            grad_hidden, w_first_whole[tap], (((1,), (1,)), ((), ())), preferred_element_type=F32
        )[offset : offset + rows]
        spread = product if spread is None else spread + product
    grad_input = (
        grad_hidden[EDGE : EDGE + rows].astype(F32) + spread * slope_first
    ).astype(BF16)

    done = finish(jnp.stack([line_sum(plane_first), line_sum(plane_second)]))
    return (tower[None], grad_input[None], done[0], done[1])


def solution(mesh):
    return jax.shard_map(
        shards,
        mesh=mesh,
        in_specs=(P("dp", "seq", None), P("dp", None), P("dp", None), P("dp", "seq", None)),
        out_specs=(P("dp", "seq", None), P("dp", "seq", None), P("dp", None), P("dp", None)),
        check_vma=False,
    )
```

time: 354 us -> 160 us (0.45)
  waiting for transfers between devices: 274 us -> 53.3 us
  starting transfers between devices: 19.8 us -> 45.7 us
  other arithmetic: 5.24 us -> 20.7 us
  between operations: 13.9 us -> 1.59 us
  matrix products: 35.7 us -> 24.9 us
  local copies, waits for them, and re-layouts: 5.44 us -> 13.3 us
    reduce_scatter x2 -> x0, waiting for transfers between devices: 154 us -> none  [reduce_grad(): lax.psum_scatter(lax.dot_general(stacked, upstream, (((0,), (0,)), ((), (...]
    all_gather x2 -> x0, waiting for transfers between devices: 79.1 us -> none  [forward_product(): lax.all_gather(weight, 'dp', axis=0, tiled=True)]
    ppermute x8 -> x38, waiting for transfers between devices: 8.52 us -> 53.3 us  [the longest x2 12 us: plane_sum(): one_in = lax.ppermute(take(one, 1 - me_x, 1), 'dp', x_pairs)]
    psum x1 -> x0, waiting for transfers between devices: 30.1 us -> none  [reduce_grad(): result = lax.psum(owned, 'seq')]
    ppermute x8 -> x38, starting transfers between devices: 19.6 us -> 45.7 us  [the longest x6 11.6 us: gather(): lax.ppermute(piece, 'dp', turn(step))]
    dot_general x6 -> x8, matrix products: 35.7 us -> 24.9 us  [the longest x2 8.31 us: gradient(): lax.dot_general(stacked.reshape(2 * rows, 3 * channels), upstream.reshape...]
    another operation x0 -> x15, other arithmetic: none -> 8.33 us  [the longest x4 2.36 us: on(): jnp.stack([jnp.where(flag == 0, here, there), jnp.where(flag == 0, there,...]
    select_n x0 -> x9, other arithmetic: none -> 4.78 us  [the longest x2 2.73 us: by_core(): second = jnp.where(core == 0, theirs, mine)]
  transfers between devices with their start and end apart: 13 -> 38, of which waited for: 8 -> 20; matrix products, arithmetic and copies ran while one was open for 8% -> 33% of each run, Pallas kernels for 0% -> 0%
where the time goes in v1:
time: 160 us; the launch traced here: 159 us
  waiting for transfers between devices  53.3 us (33%)
  starting transfers between devices  45.7 us (29%)
  matrix products  24.9 us (16%)
  other arithmetic  20.7 us (13%)
  local copies, waits for them, and re-layouts  13.3 us (8%)
    ppermute x2, waiting for transfers between devices, plane_sum(): one_in = lax.ppermute(take(one, 1 - me_x, 1), 'dp', x_pairs)  12 us
    ppermute x6, starting transfers between devices, gather(): lax.ppermute(piece, 'dp', turn(step))  11.6 us
    ppermute x2, waiting for transfers between devices, plane_rest(): one_in = lax.ppermute(take(one, 1 - h, 1), 'seq', y_pairs)  10.6 us
    ppermute x6, waiting for transfers between devices, gather(): lax.ppermute(piece, 'dp', turn(step))  9.53 us
    ppermute x6, starting transfers between devices, line_sum(): total = total + lax.ppermute(out, 'dp', turn(step)).astype(F32)  8.81 us
    dot_general x2, matrix products, gradient(): lax.dot_general(stacked.reshape(2 * rows, 3 * channels), upstream.reshape...  8.31 us
    dot_general x1, matrix products, shards(): jnp.dot(after(stack_cot, *half_second), blocks.transpose(0, 1, 3, 2).resh...  6.47 us
    ppermute x6, waiting for transfers between devices, line_sum(): total = total + lax.ppermute(out, 'dp', turn(step)).astype(F32)  5.36 us
  transfers between devices with their start and end apart: 38, of which 20 were waited for; matrix products, arithmetic and copies ran while one was open for 33% of the time, Pallas kernels for 0%

profile of v1, /device:TPU:0, one launch (start us, length us, event | category | flops | bytes accessed | tf_op | source)
XLA Modules:
  0.0 159.5 jit_solution(8691744294609550318)
XLA Ops:
  1.6 3.0 %collective-permute-start = (bf16[16,1536]{1,0:T(8,128)(2,1)S(1)}, bf16[16,1536]{1,0:T(8,128)(2,1)S(1)}, u32[]{:S(2)}, u32[]{:S(2)}) collective-permute-start(bf16[16,1536]{1,0:T(8,128)(2,1)S(1)} %fusion.118), channel_id=1, source_target_pairs={{0,1},{1,0},{2,3},{3,2},{4,5},{5,4},{6,7},{7,6},{8,9},{9,8},{10,11... | collective-permute-start | bytes 147464 | tf_op jit(solution)/shard_map/ppermute | solution.py:68
  4.6 1.7 %fusion.90 = bf16[2,144,384]{2,1,0:T(8,128)(2,1)} fusion(s32[]{:T(128)S(6)} %select_n.317, bf16[1,144,768]{2,1,0:T(8,128)(2,1)} %bitcast.228, bf16[1,144,768]{2,1,0:T(8,128)(2,1)} %bitcast.230), kind=kLoop, calls=%fused_computation.212 | loop fusion | flops 442368 | bytes 663556 | tf_op jit(solution)/shard_map/stack | solution.py:58
  9.4 1.6 %collective-permute-start.4 = (bf16[144,384]{1,0:T(8,128)(2,1)S(1)}, bf16[144,384]{1,0:T(8,128)(2,1)S(1)}, u32[]{:S(2)}, u32[]{:S(2)}) collective-permute-start(bf16[144,384]{1,0:T(8,128)(2,1)S(1)} %dynamic-slice_bitcast_fusion.6), channel_id=1, source_target_pairs={{0,8},{2,10},{4,12},{6,14},{8,16},{10,18},{12,20},{14,22},{16,24},... | collective-permute-start | bytes 331784 | tf_op jit(solution)/shard_map/ppermute | solution.py:80
  11.0 2.6 %collective-permute-start.3 = (bf16[144,384]{1,0:T(8,128)(2,1)S(1)}, bf16[144,384]{1,0:T(8,128)(2,1)S(1)}, u32[]{:S(2)}, u32[]{:S(2)}) collective-permute-start(bf16[144,384]{1,0:T(8,128)(2,1)S(1)} %dynamic-slice_bitcast_fusion.6), channel_id=1, source_target_pairs={{0,16},{2,18},{4,20},{6,22},{8,24},{10,26},{12,28},{14,30},{16,0},... | collective-permute-start | bytes 331784 | tf_op jit(solution)/shard_map/ppermute | solution.py:80
  15.6 1.6 %collective-permute-done.4 = bf16[144,384]{1,0:T(8,128)(2,1)S(1)} collective-permute-done((bf16[144,384]{1,0:T(8,128)(2,1)S(1)}, bf16[144,384]{1,0:T(8,128)(2,1)S(1)}, u32[]{:S(2)}, u32[]{:S(2)}) %collective-permute-start.4) | collective-permute-done | bytes 110624 | tf_op jit(solution)/shard_map/ppermute | solution.py:80
  17.2 4.0 %collective-permute-done.3 = bf16[144,384]{1,0:T(8,128)(2,1)S(1)} collective-permute-done((bf16[144,384]{1,0:T(8,128)(2,1)S(1)}, bf16[144,384]{1,0:T(8,128)(2,1)S(1)}, u32[]{:S(2)}, u32[]{:S(2)}) %collective-permute-start.3) | collective-permute-done | bytes 110624 | tf_op jit(solution)/shard_map/ppermute | solution.py:80
  22.0 2.8 %collective-permute-start.14 = (bf16[144,384]{1,0:T(8,128)(2,1)}, bf16[144,384]{1,0:T(8,128)(2,1)S(1)}, u32[]{:S(2)}, u32[]{:S(2)}) collective-permute-start(bf16[144,384]{1,0:T(8,128)(2,1)} %dynamic-slice_bitcast_fusion.5), channel_id=1, source_target_pairs={{0,8},{2,10},{4,12},{6,14},{8,16},{10,18},{12,20},{14,22},{16,24},... | collective-permute-start | bytes 331784 | tf_op jit(solution)/shard_map/ppermute | solution.py:80
  24.8 1.6 %collective-permute-start.13 = (bf16[144,384]{1,0:T(8,128)(2,1)}, bf16[144,384]{1,0:T(8,128)(2,1)}, u32[]{:S(2)}, u32[]{:S(2)}) collective-permute-start(bf16[144,384]{1,0:T(8,128)(2,1)} %dynamic-slice_bitcast_fusion.5), channel_id=1, source_target_pairs={{0,16},{2,18},{4,20},{6,22},{8,24},{10,26},{12,28},{14,30},{16,0},... | collective-permute-start | bytes 331784 | tf_op jit(solution)/shard_map/ppermute | solution.py:80
  31.5 2.4 %collective-permute-done.13 = bf16[144,384]{1,0:T(8,128)(2,1)} collective-permute-done((bf16[144,384]{1,0:T(8,128)(2,1)}, bf16[144,384]{1,0:T(8,128)(2,1)}, u32[]{:S(2)}, u32[]{:S(2)}) %collective-permute-start.13) | collective-permute-done | bytes 110624 | tf_op jit(solution)/shard_map/ppermute | solution.py:80
  43.2 4.4 %collective-permute-done.7 = bf16[2,2,144,384]{3,2,1,0:T(8,128)(2,1)} collective-permute-done((bf16[2,2,144,384]{3,2,1,0:T(8,128)(2,1)}, bf16[2,2,144,384]{3,2,1,0:T(8,128)(2,1)}, u32[]{:S(2)}, u32[]{:S(2)}) %collective-permute-start.7) | collective-permute-done | bytes 442400 | tf_op jit(solution)/shard_map/ppermute | solution.py:105
  50.1 2.8 %collective-permute-done.16 = bf16[3,144,384]{2,1,0:T(8,128)(2,1)S(1)} collective-permute-done((bf16[3,144,384]{2,1,0:T(8,128)(2,1)S(1)}, bf16[3,144,384]{2,1,0:T(8,128)(2,1)S(1)}, u32[]{:S(2)}, u32[]{:S(2)}) %collective-permute-start.16) | collective-permute-done | bytes 331808 | tf_op jit(solution)/shard_map/ppermute | solution.py:82
  52.9 2.6 %collective-permute-start.17 = (bf16[2,144,384]{2,1,0:T(8,128)(2,1)S(1)}, bf16[2,144,384]{2,1,0:T(8,128)(2,1)S(1)}, u32[]{:S(2)}, u32[]{:S(2)}) collective-permute-start(bf16[2,144,384]{2,1,0:T(8,128)(2,1)S(1)} %slice.236), channel_id=1, source_target_pairs={{0,1},{1,0},{2,3},{3,2},{4,5},{5,4},{6,7},{7,6},{8,9},{9,8},{10,11... | collective-permute-start | bytes 663560 | tf_op jit(solution)/shard_map/ppermute | solution.py:84
  61.7 3.4 %fusion.37 = (bf16[2,528,384]{2,1,0:T(8,128)(2,1)S(1)}, bf16[2,528,384]{2,1,0:T(8,128)(2,1)S(1)}) fusion(pred[528]{0:T(1024)(128)(4,1)S(1)} %fusion.119, bf16[2304,384,1]{1,0,2:T(8,128)(2,1)S(1)} %bitcast.210, bf16[2,528,768]{2,1,0:T(8,128)(2,1)S(1)} %get-tuple-element.45, bf16[2,528,768]{2,1,0:T(8,128)(2,1)S(1)} %get-tuple-element.46, ...), kind=kOutput, calls=%fused_computation.66 | convolution fusion | flops 1887215616 | bytes 9069080 | tf_op jit(solution)/shard_map/dot_general | solution.py:142
  66.8 2.6 %broadcast_select_fusion = (bf16[2304,384]{1,0:T(8,128)(2,1)}, bf16[2304,384]{1,0:T(8,128)(2,1)}) fusion(bf16[2304,384]{1,0:T(8,128)(2,1)S(1)} %collective-permute-done.23, pred[]{:T(512)S(6)} %eq.22, bf16[4,2,2,144,384]{4,3,2,1,0:T(8,128)(2,1)S(1)} %copy.26), kind=kLoop, calls=%fused_computation.60 | loop fusion | flops 1769472 | bytes 7077889 | tf_op jit(solution)/shard_map/jit(_where)/select_n | solution.py:49
  70.9 4.2 %fusion.20 = bf16[2304,384]{1,0:T(8,128)(2,1)S(1)} fusion(bf16[2,544,384]{2,1,0:T(8,128)(2,1)S(1)} %get-tuple-element.35, bf16[2,528,384]{2,1,0:T(8,128)(2,1)S(1)} %get-tuple-element.50, bf16[2,528,384]{2,1,0:T(8,128)(2,1)S(1)} %get-tuple-element.49, bf16[2,512,768]{2,1,0:T(8,128)(2,1)S(1)} %get-tuple-element.48, bf16[2,512,768]{2,1,0:T(8,128)(2,1)S(1)} %get-tuple-element.47), kind=kOutput, calls=%fused_computation.18 | convolution fusion | flops 1832583168 | bytes 7323648 | tf_op jit(solution)/shard_map/dot_general | solution.py:153
  79.5 2.8 %add_convert_fusion.1 = bf16[2,512,384]{2,1,0:T(8,128)(2,1)S(1)} fusion(bf16[2304,384,1]{1,0,2:T(8,128)(2,1)S(1)} %bitcast.214, bf16[2,528,384]{2,1,0:T(8,128)(2,1)S(1)} %get-tuple-element.90, bf16[2,528,384]{2,1,0:T(8,128)(2,1)S(1)} %get-tuple-element.50, bf16[2,528,384]{2,1,0:T(8,128)(2,1)S(1)} %get-tuple-element.49, ...), kind=kOutput, calls=%fused_computation.87 | convolution fusion | flops 1831993344 | bytes 8110080 | tf_op jit(solution)/shard_map/dot_general | solution.py:222
  82.5 5.2 %collective-permute-done.19 = bf16[2,2,144,384]{3,2,0,1:T(8,128)(2,1)S(1)} collective-permute-done((bf16[2,2,144,384]{3,2,0,1:T(8,128)(2,1)S(1)}, bf16[2,2,144,384]{3,2,0,1:T(8,128)(2,1)S(1)}, u32[]{:S(2)}, u32[]{:S(2)}) %collective-permute-start.19) | collective-permute-done | bytes 442400 | tf_op jit(solution)/shard_map/ppermute | solution.py:169
  88.2 1.6 collective-permute-start.25
  89.8 4.6 %collective-permute-done.24 = bf16[2,144,384]{2,1,0:T(8,128)(2,1)S(1)} collective-permute-done((bf16[2,144,384]{2,1,0:T(8,128)(2,1)S(1)}, bf16[2,144,384]{2,1,0:T(8,128)(2,1)S(1)}, u32[]{:S(2)}, u32[]{:S(2)}) %collective-permute-start.24) | collective-permute-done | bytes 221216 | tf_op jit(solution)/shard_map/ppermute | solution.py:174
  95.1 1.7 %collective-permute-start.34 = (bf16[144,384]{1,0:T(8,128)(2,1)S(1)}, bf16[144,384]{1,0:T(8,128)(2,1)S(1)}, u32[]{:S(2)}, u32[]{:S(2)}) collective-permute-start(bf16[144,384]{1,0:T(8,128)(2,1)S(1)} %get-tuple-element.81), channel_id=1, source_target_pairs={{0,16},{2,18},{4,20},{6,22},{8,24},{10,26},{12,28},{14,30},{16,0},... | collective-permute-start | bytes 331784 | tf_op jit(solution)/shard_map/ppermute | solution.py:184
  96.7 2.6 %collective-permute-start.33 = (bf16[144,384]{1,0:T(8,128)(2,1)S(1)}, bf16[144,384]{1,0:T(8,128)(2,1)S(1)}, u32[]{:S(2)}, u32[]{:S(2)}) collective-permute-start(bf16[144,384]{1,0:T(8,128)(2,1)S(1)} %get-tuple-element.80), channel_id=1, source_target_pairs={{0,24},{2,26},{4,28},{6,30},{8,0},{10,2},{12,4},{14,6},{16,8},{18,... | collective-permute-start | bytes 331784 | tf_op jit(solution)/shard_map/ppermute | solution.py:184
  101.0 3.8 %copy.34 = bf16[3,2,384,384]{3,2,1,0:T(8,128)(2,1)} copy(bf16[3,2,384,384]{2,3,1,0:T(8,128)(2,1)} %maximum_bitcast_fusion) | data formatting | bytes 3538944 | tf_op jit(solution)/shard_map/transpose | solution.py:213
  104.8 6.5 %fusion.46 = bf16[2,528,384]{2,1,0:T(8,128)(2,1)S(1)} fusion(bf16[2,528,384]{2,1,0:T(8,128)(2,1)} %copy-done.22, bf16[2,528,2304]{2,1,0:T(8,128)(2,1)} %copy-done.20, bf16[2304,384,1]{1,0,2:T(8,128)(2,1)} %bitcast.225, pred[528]{0:T(1024)(128)(4,1)S(1)} %fusion.119, bf16[2,544,384]{2,1,0:T(8,128)(2,1)S(1)} %get-tuple-element.35), kind=kOutput, calls=%fused_computation.75 | convolution fusion | flops 1874239488 | bytes 9069072 | tf_op jit(solution)/shard_map/dot_general | solution.py:211
  111.3 4.1 %fusion.21 = bf16[2304,384]{1,0:T(8,128)(2,1)S(1)} fusion(bf16[2,528,768]{2,1,0:T(8,128)(2,1)S(1)} %copy-done.10, bf16[2,528,768]{2,1,0:T(8,128)(2,1)S(1)} %copy-done.12, bf16[2,528,768]{2,1,0:T(8,128)(2,1)S(1)} %copy-done.8, bf16[2,528,384]{2,1,0:T(8,128)(2,1)S(1)} %fusion.46), kind=kOutput, calls=%fused_computation.19 | convolution fusion | flops 1827864576 | bytes 7421952 | tf_op jit(solution)/shard_map/dot_general | solution.py:153
  118.2 6.9 %collective-permute-done.26 = bf16[2,2,144,384]{3,2,0,1:T(8,128)(2,1)S(1)} collective-permute-done((bf16[2,2,144,384]{3,2,0,1:T(8,128)(2,1)S(1)}, bf16[2,2,144,384]{3,2,0,1:T(8,128)(2,1)S(1)}, u32[]{:S(2)}, u32[]{:S(2)}) %collective-permute-start.26) | collective-permute-done | bytes 442400 | tf_op jit(solution)/shard_map/ppermute | solution.py:169
  127.2 6.0 %collective-permute-done.27 = bf16[2,144,384]{2,1,0:T(8,128)(2,1)S(1)} collective-permute-done((bf16[2,144,384]{2,1,0:T(8,128)(2,1)S(1)}, bf16[2,144,384]{2,1,0:T(8,128)(2,1)S(1)}, u32[]{:S(2)}, u32[]{:S(2)}) %collective-permute-start.27) | collective-permute-done | bytes 221216 | tf_op jit(solution)/shard_map/ppermute | solution.py:174
  134.6 4.9 %collective-permute-done.29 = bf16[2,144,384]{2,1,0:T(8,128)(2,1)S(1)} collective-permute-done((bf16[2,144,384]{2,1,0:T(8,128)(2,1)S(1)}, bf16[2,144,384]{2,1,0:T(8,128)(2,1)S(1)}, u32[]{:S(2)}, u32[]{:S(2)}) %collective-permute-start.29) | collective-permute-done | bytes 221216 | tf_op jit(solution)/shard_map/ppermute | solution.py:175
  141.3 2.8 %collective-permute-start.30 = (bf16[144,384]{1,0:T(8,128)(2,1)S(1)}, bf16[144,384]{1,0:T(8,128)(2,1)S(1)}, u32[]{:S(2)}, u32[]{:S(2)}) collective-permute-start(bf16[144,384]{1,0:T(8,128)(2,1)S(1)} %get-tuple-element.77), channel_id=1, source_target_pairs={{0,24},{2,26},{4,28},{6,30},{8,0},{10,2},{12,4},{14,6},{16,8},{18,... | collective-permute-start | bytes 331784 | tf_op jit(solution)/shard_map/ppermute | solution.py:184
  144.3 2.9 %collective-permute-done.32 = bf16[144,384]{1,0:T(8,128)(2,1)S(1)} collective-permute-done((bf16[144,384]{1,0:T(8,128)(2,1)S(1)}, bf16[144,384]{1,0:T(8,128)(2,1)S(1)}, u32[]{:S(2)}, u32[]{:S(2)}) %collective-permute-start.32) | collective-permute-done | bytes 110624 | tf_op jit(solution)/shard_map/ppermute | solution.py:184
  147.2 2.4 %collective-permute-done.31 = bf16[144,384]{1,0:T(8,128)(2,1)S(1)} collective-permute-done((bf16[144,384]{1,0:T(8,128)(2,1)S(1)}, bf16[144,384]{1,0:T(8,128)(2,1)S(1)}, u32[]{:S(2)}, u32[]{:S(2)}) %collective-permute-start.31) | collective-permute-done | bytes 110624 | tf_op jit(solution)/shard_map/ppermute | solution.py:184
  149.8 2.5 %collective-permute-start.36 = (bf16[2,144,384]{2,1,0:T(8,128)(2,1)S(1)}, bf16[2,144,384]{2,1,0:T(8,128)(2,1)S(1)}, u32[]{:S(2)}, u32[]{:S(2)}) collective-permute-start(bf16[2,144,384]{2,1,0:T(8,128)(2,1)S(1)} %pad_maximum_fusion.15), channel_id=1, source_target_pairs={{0,1},{1,0},{2,3},{3,2},{4,5},{5,4},{6,7},{7,6},{8,9},{9,8},{10,11... | collective-permute-start | bytes 663560 | tf_op jit(solution)/shard_map/ppermute | solution.py:192
  154.3 2.3 %fusion.60 = bf16[1,512,768]{2,1,0:T(8,128)(2,1)} fusion(f32[512,768]{1,0:T(8,128)S(1)} %fusion.65, f32[512,768]{1,0:T(8,128)S(1)} %fusion.62, bf16[2304,384]{1,0:T(8,128)(2,1)S(1)} %copy-done.5, bf16[2304,384]{1,0:T(8,128)(2,1)S(1)} %copy-done.6, bf16[528,384]{1,0:T(8,128)(2,1)S(1)} %get-tuple-element.51, bf16[528,384]{1,0:T(8,128)(2,1)S(1)} %get-tuple-element.52, ...), kind=kOutput, calls=%fused_computation.93 | convolution fusion | flops 614989824 | bytes 9879552 | tf_op jit(solution)/shard_map/dot_general | solution.py:233
  (183 shorter events, 52.9 us)
Async XLA Ops:
  9.4 7.8 %collective-permute-start.4 = (bf16[144,384]{1,0:T(8,128)(2,1)S(1)}, bf16[144,384]{1,0:T(8,128)(2,1)S(1)}, u32[]{:S(2)}, u32[]{:S(2)}) collective-permute-start(bf16[144,384]{1,0:T(8,128)(2,1)S(1)} %dynamic-slice_bitcast_fusion.6), channel_id=1, source_target_pairs={{0,8},{2,10},{4,12},{6,14},{8,16},{10,18},{12,20},{14,22},{16,24},... | collective-permute-start | bytes 331784 | tf_op jit(solution)/shard_map/ppermute | solution.py:80
  11.0 10.2 %collective-permute-start.3 = (bf16[144,384]{1,0:T(8,128)(2,1)S(1)}, bf16[144,384]{1,0:T(8,128)(2,1)S(1)}, u32[]{:S(2)}, u32[]{:S(2)}) collective-permute-start(bf16[144,384]{1,0:T(8,128)(2,1)S(1)} %dynamic-slice_bitcast_fusion.6), channel_id=1, source_target_pairs={{0,16},{2,18},{4,20},{6,22},{8,24},{10,26},{12,28},{14,30},{16,0},... | collective-permute-start | bytes 331784 | tf_op jit(solution)/shard_map/ppermute | solution.py:80
  13.6 7.6 %collective-permute-start.2 = (bf16[144,384]{1,0:T(8,128)(2,1)S(1)}, bf16[144,384]{1,0:T(8,128)(2,1)S(1)}, u32[]{:S(2)}, u32[]{:S(2)}) collective-permute-start(bf16[144,384]{1,0:T(8,128)(2,1)S(1)} %dynamic-slice_bitcast_fusion.6), channel_id=1, source_target_pairs={{0,24},{2,26},{4,28},{6,30},{8,0},{10,2},{12,4},{14,6},{16,8},{18,... | collective-permute-start | bytes 331784 | tf_op jit(solution)/shard_map/ppermute | solution.py:80
  22.0 7.9 %collective-permute-start.14 = (bf16[144,384]{1,0:T(8,128)(2,1)}, bf16[144,384]{1,0:T(8,128)(2,1)S(1)}, u32[]{:S(2)}, u32[]{:S(2)}) collective-permute-start(bf16[144,384]{1,0:T(8,128)(2,1)} %dynamic-slice_bitcast_fusion.5), channel_id=1, source_target_pairs={{0,8},{2,10},{4,12},{6,14},{8,16},{10,18},{12,20},{14,22},{16,24},... | collective-permute-start | bytes 331784 | tf_op jit(solution)/shard_map/ppermute | solution.py:80
  24.8 9.1 %collective-permute-start.13 = (bf16[144,384]{1,0:T(8,128)(2,1)}, bf16[144,384]{1,0:T(8,128)(2,1)}, u32[]{:S(2)}, u32[]{:S(2)}) collective-permute-start(bf16[144,384]{1,0:T(8,128)(2,1)} %dynamic-slice_bitcast_fusion.5), channel_id=1, source_target_pairs={{0,16},{2,18},{4,20},{6,22},{8,24},{10,26},{12,28},{14,30},{16,0},... | collective-permute-start | bytes 331784 | tf_op jit(solution)/shard_map/ppermute | solution.py:80
  26.5 14.0 %collective-permute-start.6 = (bf16[3,144,384]{2,1,0:T(8,128)(2,1)}, bf16[3,144,384]{2,1,0:T(8,128)(2,1)}, u32[]{:S(2)}, u32[]{:S(2)}) collective-permute-start(bf16[3,144,384]{2,1,0:T(8,128)(2,1)} %pad_maximum_fusion.13), channel_id=1, source_target_pairs={{0,1},{1,0},{2,3},{3,2},{4,5},{5,4},{6,7},{7,6},{8,9},{9,8},{10,11... | collective-permute-start | bytes 995336 | tf_op jit(solution)/shard_map/ppermute | solution.py:83
  27.0 11.1 %collective-permute-start.8 = (bf16[3,144,384]{2,1,0:T(8,128)(2,1)}, bf16[3,144,384]{2,1,0:T(8,128)(2,1)}, u32[]{:S(2)}, u32[]{:S(2)}) collective-permute-start(bf16[3,144,384]{2,1,0:T(8,128)(2,1)} %pad_maximum_fusion.13), channel_id=1, source_target_pairs={{0,4},{2,6},{4,0},{6,2},{8,12},{10,14},{12,8},{14,10},{16,20},{18,... | collective-permute-start | bytes 995336 | tf_op jit(solution)/shard_map/ppermute | solution.py:82
  29.3 18.2 %collective-permute-start.7 = (bf16[2,2,144,384]{3,2,1,0:T(8,128)(2,1)}, bf16[2,2,144,384]{3,2,1,0:T(8,128)(2,1)}, u32[]{:S(2)}, u32[]{:S(2)}) collective-permute-start(bf16[2,2,144,384]{3,2,1,0:T(8,128)(2,1)} %pad_maximum_fusion.12), channel_id=1, source_target_pairs={{0,4},{2,6},{4,0},{6,2},{8,12},{10,14},{12,8},{14,10},{16,20},{18,... | collective-permute-start | bytes 1327112 | tf_op jit(solution)/shard_map/ppermute | solution.py:105
  33.9 26.1 %collective-permute-start.5 = (bf16[544,1536]{1,0:T(8,128)(2,1)S(1)}, bf16[544,1536]{1,0:T(8,128)(2,1)S(1)}, u32[]{:S(2)}, u32[]{:S(2)}) collective-permute-start(bf16[544,1536]{1,0:T(8,128)(2,1)S(1)} %pad_maximum_fusion.1), channel_id=1, source_target_pairs={{0,2},{2,0},{4,6},{6,4},{8,10},{10,8},{12,14},{14,12},{16,18},{18,... | collective-permute-start | bytes 5013512 | tf_op jit(solution)/shard_map/ppermute | solution.py:110
  36.5 16.4 %collective-permute-start.16 = (bf16[3,144,384]{2,1,0:T(8,128)(2,1)S(1)}, bf16[3,144,384]{2,1,0:T(8,128)(2,1)S(1)}, u32[]{:S(2)}, u32[]{:S(2)}) collective-permute-start(bf16[3,144,384]{2,1,0:T(8,128)(2,1)S(1)} %pad_maximum_fusion.14), channel_id=1, source_target_pairs={{0,4},{2,6},{4,0},{6,2},{8,12},{10,14},{12,8},{14,10},{16,20},{18,... | collective-permute-start | bytes 995336 | tf_op jit(solution)/shard_map/ppermute | solution.py:82
  38.0 17.5 %collective-permute-start.15 = (bf16[3,144,384]{2,1,0:T(8,128)(2,1)S(1)}, bf16[3,144,384]{2,1,0:T(8,128)(2,1)S(1)}, u32[]{:S(2)}, u32[]{:S(2)}) collective-permute-start(bf16[3,144,384]{2,1,0:T(8,128)(2,1)S(1)} %pad_maximum_fusion.14), channel_id=1, source_target_pairs={{0,1},{1,0},{2,3},{3,2},{4,5},{5,4},{6,7},{7,6},{8,9},{9,8},{10,11... | collective-permute-start | bytes 995336 | tf_op jit(solution)/shard_map/ppermute | solution.py:83
  40.5 16.6 %collective-permute-start.9 = (bf16[2,144,384]{2,1,0:T(8,128)(2,1)S(1)}, bf16[2,144,384]{2,1,0:T(8,128)(2,1)S(1)}, u32[]{:S(2)}, u32[]{:S(2)}) collective-permute-start(bf16[2,144,384]{2,1,0:T(8,128)(2,1)S(1)} %slice.225), channel_id=1, source_target_pairs={{0,1},{1,0},{2,3},{3,2},{4,5},{5,4},{6,7},{7,6},{8,9},{9,8},{10,11... | collective-permute-start | bytes 663560 | tf_op jit(solution)/shard_map/ppermute | solution.py:84
  47.5 9.6 %collective-permute-start.10 = (bf16[1,144,384]{2,1,0:T(8,128)(2,1)S(1)}, bf16[1,144,384]{2,1,0:T(8,128)(2,1)S(1)}, u32[]{:S(2)}, u32[]{:S(2)}) collective-permute-start(bf16[1,144,384]{2,1,0:T(8,128)(2,1)S(1)} %slice.226), channel_id=1, source_target_pairs={{0,4},{2,6},{4,0},{6,2},{8,12},{10,14},{12,8},{14,10},{16,20},{18,... | collective-permute-start | bytes 331784 | tf_op jit(solution)/shard_map/ppermute | solution.py:85
  52.9 22.4 %collective-permute-start.17 = (bf16[2,144,384]{2,1,0:T(8,128)(2,1)S(1)}, bf16[2,144,384]{2,1,0:T(8,128)(2,1)S(1)}, u32[]{:S(2)}, u32[]{:S(2)}) collective-permute-start(bf16[2,144,384]{2,1,0:T(8,128)(2,1)S(1)} %slice.236), channel_id=1, source_target_pairs={{0,1},{1,0},{2,3},{3,2},{4,5},{5,4},{6,7},{7,6},{8,9},{9,8},{10,11... | collective-permute-start | bytes 663560 | tf_op jit(solution)/shard_map/ppermute | solution.py:84
  55.5 19.8 %collective-permute-start.18 = (bf16[1,144,384]{2,1,0:T(8,128)(2,1)S(1)}, bf16[1,144,384]{2,1,0:T(8,128)(2,1)S(1)}, u32[]{:S(2)}, u32[]{:S(2)}) collective-permute-start(bf16[1,144,384]{2,1,0:T(8,128)(2,1)S(1)} %slice.237), channel_id=1, source_target_pairs={{0,4},{2,6},{4,0},{6,2},{8,12},{10,14},{12,8},{14,10},{16,20},{18,... | collective-permute-start | bytes 331784 | tf_op jit(solution)/shard_map/ppermute | solution.py:85
  59.9 6.9 %collective-permute-start.23 = (bf16[2304,384]{1,0:T(8,128)(2,1)S(1)}, bf16[2304,384]{1,0:T(8,128)(2,1)S(1)}, u32[]{:S(2)}, u32[]{:S(2)}) collective-permute-start(bf16[2304,384]{1,0:T(8,128)(2,1)S(1)} %bitcast.209), channel_id=1, source_target_pairs={{0,2},{2,0},{4,6},{6,4},{8,10},{10,8},{12,14},{14,12},{16,18},{18,... | collective-permute-start | bytes 5308424 | tf_op jit(solution)/shard_map/ppermute | solution.py:140
  75.5 12.2 %collective-permute-start.19 = (bf16[2,2,144,384]{3,2,0,1:T(8,128)(2,1)S(1)}, bf16[2,2,144,384]{3,2,0,1:T(8,128)(2,1)S(1)}, u32[]{:S(2)}, u32[]{:S(2)}) collective-permute-start(bf16[2,2,144,384]{3,2,0,1:T(8,128)(2,1)S(1)} %bitcast.233), channel_id=1, source_target_pairs={{0,4},{2,6},{4,0},{6,2},{8,12},{10,14},{12,8},{14,10},{16,20},{18,... | collective-permute-start | bytes 1327112 | tf_op jit(solution)/shard_map/ppermute | solution.py:169
  76.2 11.9 %collective-permute-start.20 = (bf16[2,2,144,384]{3,2,1,0:T(8,128)(2,1)S(1)}, bf16[2,2,144,384]{3,2,1,0:T(8,128)(2,1)S(1)}, u32[]{:S(2)}, u32[]{:S(2)}) collective-permute-start(bf16[2,2,144,384]{3,2,1,0:T(8,128)(2,1)S(1)} %dynamic-slice_bitcast_fusion), channel_id=1, source_target_pairs={{0,1},{1,0},{2,3},{3,2},{4,5},{5,4},{6,7},{7,6},{8,9},{9,8},{10,11... | collective-permute-start | bytes 1327112 | tf_op jit(solution)/shard_map/ppermute | solution.py:170
  79.4 19.9 %collective-permute-start.21 = (bf16[2304,384]{1,0:T(8,128)(2,1)S(1)}, bf16[2304,384]{1,0:T(8,128)(2,1)S(1)}, u32[]{:S(2)}, u32[]{:S(2)}) collective-permute-start(bf16[2304,384]{1,0:T(8,128)(2,1)S(1)} %bitcast.213), channel_id=1, source_target_pairs={{0,2},{2,0},{4,6},{6,4},{8,10},{10,8},{12,14},{14,12},{16,18},{18,... | collective-permute-start | bytes 5308424 | tf_op jit(solution)/shard_map/ppermute | solution.py:202
  87.9 6.6 %collective-permute-start.24 = (bf16[2,144,384]{2,1,0:T(8,128)(2,1)S(1)}, bf16[2,144,384]{2,1,0:T(8,128)(2,1)S(1)}, u32[]{:S(2)}, u32[]{:S(2)}) collective-permute-start(bf16[2,144,384]{2,1,0:T(8,128)(2,1)S(1)} %dynamic-slice_bitcast_fusion.4), channel_id=1, source_target_pairs={{0,1},{1,0},{2,3},{3,2},{4,5},{5,4},{6,7},{7,6},{8,9},{9,8},{10,11... | collective-permute-start | bytes 663560 | tf_op jit(solution)/shard_map/ppermute | solution.py:174
  88.2 6.5 %collective-permute-start.25 = (bf16[2,144,384]{2,1,0:T(8,128)(2,1)S(1)}, bf16[2,144,384]{2,1,0:T(8,128)(2,1)S(1)}, u32[]{:S(2)}, u32[]{:S(2)}) collective-permute-start(bf16[2,144,384]{2,1,0:T(8,128)(2,1)S(1)} %dynamic-slice_bitcast_fusion.3), channel_id=1, source_target_pairs={{0,4},{2,6},{4,0},{6,2},{8,12},{10,14},{12,8},{14,10},{16,20},{18,... | collective-permute-start | bytes 663560 | tf_op jit(solution)/shard_map/ppermute | solution.py:175
  94.9 45.1 %collective-permute-start.35 = (bf16[144,384]{1,0:T(8,128)(2,1)S(1)}, bf16[144,384]{1,0:T(8,128)(2,1)S(1)}, u32[]{:S(2)}, u32[]{:S(2)}) collective-permute-start(bf16[144,384]{1,0:T(8,128)(2,1)S(1)} %get-tuple-element.82), channel_id=1, source_target_pairs={{0,8},{2,10},{4,12},{6,14},{8,16},{10,18},{12,20},{14,22},{16,24},... | collective-permute-start | bytes 331784 | tf_op jit(solution)/shard_map/ppermute | solution.py:184
  95.1 46.3 %collective-permute-start.34 = (bf16[144,384]{1,0:T(8,128)(2,1)S(1)}, bf16[144,384]{1,0:T(8,128)(2,1)S(1)}, u32[]{:S(2)}, u32[]{:S(2)}) collective-permute-start(bf16[144,384]{1,0:T(8,128)(2,1)S(1)} %get-tuple-element.81), channel_id=1, source_target_pairs={{0,16},{2,18},{4,20},{6,22},{8,24},{10,26},{12,28},{14,30},{16,0},... | collective-permute-start | bytes 331784 | tf_op jit(solution)/shard_map/ppermute | solution.py:184
  96.7 47.5 %collective-permute-start.33 = (bf16[144,384]{1,0:T(8,128)(2,1)S(1)}, bf16[144,384]{1,0:T(8,128)(2,1)S(1)}, u32[]{:S(2)}, u32[]{:S(2)}) collective-permute-start(bf16[144,384]{1,0:T(8,128)(2,1)S(1)} %get-tuple-element.80), channel_id=1, source_target_pairs={{0,24},{2,26},{4,28},{6,30},{8,0},{10,2},{12,4},{14,6},{16,8},{18,... | collective-permute-start | bytes 331784 | tf_op jit(solution)/shard_map/ppermute | solution.py:184
  115.8 9.3 %collective-permute-start.26 = (bf16[2,2,144,384]{3,2,0,1:T(8,128)(2,1)S(1)}, bf16[2,2,144,384]{3,2,0,1:T(8,128)(2,1)S(1)}, u32[]{:S(2)}, u32[]{:S(2)}) collective-permute-start(bf16[2,2,144,384]{3,2,0,1:T(8,128)(2,1)S(1)} %bitcast.235), channel_id=1, source_target_pairs={{0,4},{2,6},{4,0},{6,2},{8,12},{10,14},{12,8},{14,10},{16,20},{18,... | collective-permute-start | bytes 1327112 | tf_op jit(solution)/shard_map/ppermute | solution.py:169
  117.4 9.0 %collective-permute-start.28 = (bf16[2,2,144,384]{3,2,0,1:T(8,128)(2,1)S(1)}, bf16[2,2,144,384]{3,2,0,1:T(8,128)(2,1)S(1)}, u32[]{:S(2)}, u32[]{:S(2)}) collective-permute-start(bf16[2,2,144,384]{3,2,0,1:T(8,128)(2,1)S(1)} %bitcast.234), channel_id=1, source_target_pairs={{0,1},{1,0},{2,3},{3,2},{4,5},{5,4},{6,7},{7,6},{8,9},{9,8},{10,11... | collective-permute-start | bytes 1327112 | tf_op jit(solution)/shard_map/ppermute | solution.py:170
  125.1 27.2 %collective-permute-start.22 = (bf16[1040,384]{1,0:T(8,128)(2,1)S(1)}, bf16[1040,384]{1,0:T(8,128)(2,1)S(1)}, u32[]{:S(2)}, u32[]{:S(2)}) collective-permute-start(bf16[1040,384]{1,0:T(8,128)(2,1)S(1)} %pad_maximum_fusion.8), channel_id=1, source_target_pairs={{0,2},{2,0},{4,6},{6,4},{8,10},{10,8},{12,14},{14,12},{16,18},{18,... | collective-permute-start | bytes 2396168 | tf_op jit(solution)/shard_map/ppermute | solution.py:225
  126.4 6.7 %collective-permute-start.27 = (bf16[2,144,384]{2,1,0:T(8,128)(2,1)S(1)}, bf16[2,144,384]{2,1,0:T(8,128)(2,1)S(1)}, u32[]{:S(2)}, u32[]{:S(2)}) collective-permute-start(bf16[2,144,384]{2,1,0:T(8,128)(2,1)S(1)} %dynamic-slice_bitcast_fusion.2), channel_id=1, source_target_pairs={{0,1},{1,0},{2,3},{3,2},{4,5},{5,4},{6,7},{7,6},{8,9},{9,8},{10,11... | collective-permute-start | bytes 663560 | tf_op jit(solution)/shard_map/ppermute | solution.py:174
  139.8 7.4 %collective-permute-start.32 = (bf16[144,384]{1,0:T(8,128)(2,1)S(1)}, bf16[144,384]{1,0:T(8,128)(2,1)S(1)}, u32[]{:S(2)}, u32[]{:S(2)}) collective-permute-start(bf16[144,384]{1,0:T(8,128)(2,1)S(1)} %get-tuple-element.79), channel_id=1, source_target_pairs={{0,8},{2,10},{4,12},{6,14},{8,16},{10,18},{12,20},{14,22},{16,24},... | collective-permute-start | bytes 331784 | tf_op jit(solution)/shard_map/ppermute | solution.py:184
  140.1 9.6 %collective-permute-start.31 = (bf16[144,384]{1,0:T(8,128)(2,1)S(1)}, bf16[144,384]{1,0:T(8,128)(2,1)S(1)}, u32[]{:S(2)}, u32[]{:S(2)}) collective-permute-start(bf16[144,384]{1,0:T(8,128)(2,1)S(1)} %get-tuple-element.78), channel_id=1, source_target_pairs={{0,16},{2,18},{4,20},{6,22},{8,24},{10,26},{12,28},{14,30},{16,0},... | collective-permute-start | bytes 331784 | tf_op jit(solution)/shard_map/ppermute | solution.py:184
  141.3 8.3 %collective-permute-start.30 = (bf16[144,384]{1,0:T(8,128)(2,1)S(1)}, bf16[144,384]{1,0:T(8,128)(2,1)S(1)}, u32[]{:S(2)}, u32[]{:S(2)}) collective-permute-start(bf16[144,384]{1,0:T(8,128)(2,1)S(1)} %get-tuple-element.77), channel_id=1, source_target_pairs={{0,24},{2,26},{4,28},{6,30},{8,0},{10,2},{12,4},{14,6},{16,8},{18,... | collective-permute-start | bytes 331784 | tf_op jit(solution)/shard_map/ppermute | solution.py:184
  149.8 6.8 %collective-permute-start.36 = (bf16[2,144,384]{2,1,0:T(8,128)(2,1)S(1)}, bf16[2,144,384]{2,1,0:T(8,128)(2,1)S(1)}, u32[]{:S(2)}, u32[]{:S(2)}) collective-permute-start(bf16[2,144,384]{2,1,0:T(8,128)(2,1)S(1)} %pad_maximum_fusion.15), channel_id=1, source_target_pairs={{0,1},{1,0},{2,3},{3,2},{4,5},{5,4},{6,7},{7,6},{8,9},{9,8},{10,11... | collective-permute-start | bytes 663560 | tf_op jit(solution)/shard_map/ppermute | solution.py:192
  (29 other events, 186.1 us)

commit v2 on v1

--- a/solution.py
+++ b/solution.py
@@ -19,6 +19,10 @@
     cumulative = 0.5 * (1.0 + lax.erf(values * 0.7071067811865476))
     density = jnp.exp(-0.5 * values * values) * 0.3989422804014327
     return cumulative + values * density
+
+
+def together(*values):
+    return lax.optimization_barrier(values)
 
 
 def after(value, *others):
@@ -40,6 +44,7 @@
     core_pairs = [(i, i ^ 1) for i in range(parts)]
     x_pairs = [(i, i ^ 2) for i in range(parts)]
     y_pairs = [(i, i ^ 1) for i in range(seqs)]
+    xy_pairs = [((i ^ 2) * seqs + k, i * seqs + (k ^ 1)) for i in range(parts) for k in range(seqs)]
 
     def turn(step):
         return [(i, (i - 4 * step) % parts) for i in range(parts)]
@@ -74,27 +79,26 @@
         low = lax.ppermute(joined[rows - HALO :], "seq", onward)
         high = lax.ppermute(joined[:HALO], "seq", back)
 
-    def gather(which, x_pair, *others):
+    def along_z(which, *others):
         piece = after(lax.dynamic_index_in_dim(pair[which], h, 0, keepdims=False), *others)
-        turned = jnp.stack(
-            [lax.ppermute(piece, "dp", turn(step)) for step in range(1, depth)]
+        return jnp.stack(
+            together(*(lax.ppermute(piece, "dp", turn(step)) for step in range(1, depth)))
         )
-        from_x = lax.ppermute(turned, "dp", x_pairs)
-        from_y = lax.ppermute(turned, "seq", y_pairs)
-        by_y = lax.ppermute(from_x[: depth // 2], "seq", y_pairs)
-        by_x = lax.ppermute(from_y[depth // 2 :], "dp", x_pairs)
-
-        return pair[which], x_pair[which], turned, from_x, from_y, by_y, by_x
-
-    def assemble(own, across, turned, from_x, from_y, by_y, by_x):
-        both_in = jnp.concatenate([by_y, by_x], axis=0)
-
+
+    def across(turned, *others):
+        given = after(turned, *others)
+        return lax.ppermute(given, "dp", x_pairs), lax.ppermute(given, "seq", y_pairs)
+
+    def corner(turned, *others):
+        return lax.ppermute(after(turned, *others), ("dp", "seq"), xy_pairs)
+
+    def assemble(own, across, turned, from_x, from_y, from_xy):
         def on(flag, here, there, axis):
             return jnp.stack(
                 [jnp.where(flag == 0, here, there), jnp.where(flag == 0, there, here)], axis=axis
             )
 
-        near, far = on(h, turned, from_y, 1), on(h, from_x, both_in, 1)
+        near, far = on(h, turned, from_y, 1), on(h, from_x, from_xy, 1)
         near = jnp.concatenate([own[None], near], axis=0)
         far = jnp.concatenate([across[None], far], axis=0)
         lines = on(me_x, near, far, 1)
@@ -103,10 +107,13 @@
         return lines.reshape(parts * block, half)
 
     x_pair = lax.ppermute(after(pair, low, high), "dp", x_pairs)
-    first_pieces = gather(0, x_pair, low, high)
-    second_pieces = gather(1, x_pair, first_pieces[2])
-
-    extended = after(jnp.concatenate([low, joined, high], axis=0), first_pieces[2])
+    first_turned = along_z(0, low, high)
+    first_across = across(first_turned)
+    first_corner = corner(first_turned)
+    second_turned = along_z(1, first_turned)
+    second_across = across(second_turned, first_corner)
+
+    extended = after(jnp.concatenate([low, joined, high], axis=0), first_turned)
     partner = lax.ppermute(extended, "dp", core_pairs)
     pairs = jnp.stack([extended, partner])
     features_two, cot_two = pairs[..., :channels], pairs[..., channels:]
@@ -119,16 +126,8 @@
     stack_first = jnp.concatenate(
         [shifted(act_first, HALO - EDGE + (tap - 1) * 4, wide) for tap in range(3)], axis=2
     )
-    cot_halves = [half_of(cot_two, core, 2), half_of(cot_two, 1 - core, 2)]
-    stack_cot = jnp.concatenate(
-        [
-            shifted(side, HALO - EDGE - (tap - 1) * 8, wide)
-            for tap in range(3)
-            for side in cot_halves
-        ],
-        axis=2,
-    )
-    cot_base = shifted(cot_halves[0], HALO - EDGE, wide)
+    cot_mine = half_of(cot_two, core, 2)
+    cot_base = shifted(cot_mine, HALO - EDGE, wide)
     row = lax.broadcasted_iota(jnp.int32, (1, wide, 1), 1)
     valid = (row >= jnp.where(me_y == 0, EDGE, 0)) & (
         row < jnp.where(me_y == seqs - 1, wide - EDGE, wide)
@@ -136,12 +135,13 @@
     slope_first = gelu_slope(features[0].astype(F32))
 
     first_base = shifted(half_of(features_two, core, 2), HALO - EDGE, wide)
-    first_mine = assemble(*first_pieces)
+    first_mine = assemble(pair[0], x_pair[0], first_turned, *first_across, first_corner)
     first_theirs = lax.ppermute(first_mine, "dp", core_pairs)
     hidden = (
         first_base.astype(F32) + jnp.dot(stack_first, first_mine, preferred_element_type=F32)
     ).astype(BF16)
     act_mine = jnp.where(valid, gelu_value(hidden.astype(F32)), 0.0).astype(BF16)
+    second_corner = corner(second_turned, act_mine)
     act_theirs = lax.ppermute(act_mine, "dp", core_pairs)[::-1]
     act_second = by_core(act_mine, act_theirs, 2)
     stack_second = jnp.concatenate(
@@ -166,21 +166,27 @@
         grad = grad.reshape(depth, 2, 2, block, half)
         cut = depth // 2
         one, two = grad[:cut], grad[cut:]
-        one_in = lax.ppermute(take(one, 1 - me_x, 1), "dp", x_pairs)
-        two_in = lax.ppermute(take(two, 1 - h, 2), "seq", y_pairs)
+        one_out, two_out = together(take(one, 1 - me_x, 1), take(two, 1 - h, 2))
+        one_in = lax.ppermute(one_out, "dp", x_pairs)
+        two_in = lax.ppermute(two_out, "seq", y_pairs)
+        one_in, two_in = together(one_in, two_in)
         return add(take(one, me_x, 1), one_in), add(take(two, h, 2), two_in)
 
     def plane_rest(one, two):
-        one_in = lax.ppermute(take(one, 1 - h, 1), "seq", y_pairs)
-        two_in = lax.ppermute(take(two, 1 - me_x, 1), "dp", x_pairs)
+        one_out, two_out = together(take(one, 1 - h, 1), take(two, 1 - me_x, 1))
+        one_in = lax.ppermute(one_out, "seq", y_pairs)
+        two_in = lax.ppermute(two_out, "dp", x_pairs)
+        one_in, two_in = together(one_in, two_in)
         one = add(take(one, h, 1), one_in)
         two = add(take(two, me_x, 1), two_in)
         return jnp.concatenate([one, two], axis=0)
 
     def line_sum(summed):
+        outs = together(
+            *(take(summed, (me_z - step) % depth, 0) for step in range(1, depth))
+        )
         total = take(summed, me_z, 0).astype(F32)
-        for step in range(1, depth):
-            out = take(summed, (me_z - step) % depth, 0)
+        for step, out in enumerate(outs, 1):
             total = total + lax.ppermute(out, "dp", turn(step)).astype(F32)
         return total
 
@@ -197,22 +203,27 @@
         given = lax.ppermute(take(rows_two, 1 - core, 0), "dp", core_pairs)
         return by_core(kept, given, 2).astype(F32)
 
-    grad_second = gradient(stack_second, shifted(cot_halves[0], HALO, rows))
+    grad_second = gradient(stack_second, shifted(cot_mine, HALO, rows))
+    second_pieces = pair[1], x_pair[1], second_turned, *second_across, second_corner
     second_mine = assemble(*(after(piece, grad_second) for piece in second_pieces))
     second_theirs = lax.ppermute(second_mine, "dp", core_pairs)
     half_second = plane_sum(grad_second)
     plane_second = plane_rest(*half_second)
 
     slope = gelu_slope(hidden.astype(F32))
-    blocks = jnp.stack(
-        [take(side.reshape(3, 2, half, half), core, 1) for side in (second_mine, second_theirs)],
-        axis=1,
-    )
-    spread = jnp.dot(
-        after(stack_cot, *half_second),
-        blocks.transpose(0, 1, 3, 2).reshape(3 * channels, half),
+    mine, theirs = (
+        take(side.reshape(3, 2, half, half), core, 1) for side in (second_mine, second_theirs)
+    )
+    product = lax.dot_general(
+        after(cot_two, *half_second),
+        by_core(mine, theirs, 2).reshape(3 * half, channels),
+        (((2,), (1,)), ((), ())),
         preferred_element_type=F32,
     )
+    spread = None
+    for tap in range(3):
+        part = shifted(product[..., tap * half : (tap + 1) * half], HALO - EDGE - (tap - 1) * 8, wide)
+        spread = part if spread is None else spread + part
     grad_mine = jnp.where(valid, cot_base.astype(F32) + spread * slope, 0.0).astype(BF16)
     grad_first = gradient(shifted(stack_first, EDGE, rows), shifted(grad_mine, EDGE, rows))
     plane_first = plane_rest(*plane_sum(after(grad_first, plane_second)))

time: 160 us -> 140 us (0.88)
  starting transfers between devices: 45.7 us -> 36.5 us
  local copies, waits for them, and re-layouts: 13.3 us -> 5.16 us
  waiting for transfers between devices: 53.3 us -> 60.4 us
  other arithmetic: 20.7 us -> 14.9 us
  matrix products: 24.9 us -> 21.1 us
    ppermute x22 -> x20, waiting for transfers between devices: 41.4 us -> 49 us  [the longest x6 17.4 us: along_z(): lax.ppermute(piece, 'dp', turn(step))]
    ppermute x22 -> x20, starting transfers between devices: 30.1 us -> 22.8 us  [the longest x6 7.33 us: along_z(): lax.ppermute(piece, 'dp', turn(step))]
    dot_general x1, matrix products: 6.47 us -> 2.4 us  [shards(): lax.dot_general(after(cot_two, *half_second), by_core(mine, theirs, 2).re...]
    transpose x1 -> x0, local copies, waits for them, and re-layouts: 3.85 us -> none  [shards(): blocks.transpose(0, 1, 3, 2).reshape(3 * channels, half)]
    ppermute x1, waiting for transfers between devices: 4.36 us -> 0.75 us  [shards(): x_pair = lax.ppermute(after(pair, low, high), 'dp', x_pairs)]
    select_n x2, other arithmetic: 2.73 us -> 0.59 us  [by_core(): second = jnp.where(core == 0, theirs, mine)]
    slice x4 -> x0, local copies, waits for them, and re-layouts: 1.9 us -> none  [the longest x2 0.98 us: gather(): by_y = lax.ppermute(from_x[:depth // 2], 'seq', y_pairs)]
    ppermute x6, waiting for transfers between devices: 5.36 us -> 7.23 us  [line_sum(): total = total + lax.ppermute(out, 'dp', turn(step)).astype(F32)]
  transfers between devices with their start and end apart: 38 -> 36, of which waited for: 20 -> 21; matrix products, arithmetic and copies ran while one was open for 33% -> 19% of each run, Pallas kernels for 0% -> 0%
where the time goes in v2:
time: 140 us
  waiting for transfers between devices  60.4 us (43%)
  starting transfers between devices  36.5 us (26%)
  matrix products  21.1 us (15%)
  other arithmetic  14.9 us (11%)
  local copies, waits for them, and re-layouts  5.16 us (4%)
  between operations  1.47 us (1%)
    ppermute x6, waiting for transfers between devices, along_z(): lax.ppermute(piece, 'dp', turn(step))  17.4 us
    ppermute x2, waiting for transfers between devices, plane_sum(): one_in = lax.ppermute(one_out, 'dp', x_pairs)  8.78 us
    dot_general x2, matrix products, gradient(): lax.dot_general(stacked.reshape(2 * rows, 3 * channels), upstream.reshape...  8.54 us
    ppermute x6, starting transfers between devices, line_sum(): total = total + lax.ppermute(out, 'dp', turn(step)).astype(F32)  7.81 us
    ppermute x2, waiting for transfers between devices, plane_rest(): one_in = lax.ppermute(one_out, 'seq', y_pairs)  7.73 us
    ppermute x6, starting transfers between devices, along_z(): lax.ppermute(piece, 'dp', turn(step))  7.33 us
    ppermute x6, waiting for transfers between devices, line_sum(): total = total + lax.ppermute(out, 'dp', turn(step)).astype(F32)  7.23 us
    ppermute x2, waiting for transfers between devices, across(): lax.ppermute(given, 'seq', y_pairs)  7.2 us
  transfers between devices with their start and end apart: 36, of which 21 were waited for; matrix products, arithmetic and copies ran while one was open for 19% of the time, Pallas kernels for 0%

profile of v2, /device:TPU:0, one launch (start us, length us, event | category | flops | bytes accessed | tf_op | source)
XLA Modules:
  0.0 139.6 jit_solution(13170226438784270479)
XLA Ops:
  1.5 3.0 %collective-permute-start = (bf16[16,1536]{1,0:T(8,128)(2,1)S(1)}, bf16[16,1536]{1,0:T(8,128)(2,1)S(1)}, u32[]{:S(2)}, u32[]{:S(2)}) collective-permute-start(bf16[16,1536]{1,0:T(8,128)(2,1)S(1)} %fusion.120), channel_id=1, source_target_pairs={{0,1},{1,0},{2,3},{3,2},{4,5},{5,4},{6,7},{7,6},{8,9},{9,8},{10,11... | collective-permute-start | bytes 147464 | tf_op jit(solution)/shard_map/ppermute | solution.py:73
  4.7 1.9 %collective-permute-done = bf16[16,1536]{1,0:T(8,128)(2,1)S(1)} collective-permute-done((bf16[16,1536]{1,0:T(8,128)(2,1)S(1)}, bf16[16,1536]{1,0:T(8,128)(2,1)S(1)}, u32[]{:S(2)}, u32[]{:S(2)}) %collective-permute-start) | collective-permute-done | bytes 49184 | tf_op jit(solution)/shard_map/ppermute | solution.py:73
  8.9 4.1 %collective-permute-start.2 = (bf16[144,384]{1,0:T(8,128)(2,1)S(1)}, bf16[144,384]{1,0:T(8,128)(2,1)S(1)}, u32[]{:S(2)}, u32[]{:S(2)}) collective-permute-start(bf16[144,384]{1,0:T(8,128)(2,1)S(1)} %get-tuple-element.46), channel_id=1, source_target_pairs={{0,24},{2,26},{4,28},{6,30},{8,0},{10,2},{12,4},{14,6},{16,8},{18,... | collective-permute-start | bytes 331784 | tf_op jit(solution)/shard_map/ppermute | solution.py:85
  14.0 2.5 %collective-permute-done.2 = bf16[144,384]{1,0:T(8,128)(2,1)S(1)} collective-permute-done((bf16[144,384]{1,0:T(8,128)(2,1)S(1)}, bf16[144,384]{1,0:T(8,128)(2,1)S(1)}, u32[]{:S(2)}, u32[]{:S(2)}) %collective-permute-start.2) | collective-permute-done | bytes 110624 | tf_op jit(solution)/shard_map/ppermute | solution.py:85
  16.5 5.8 %collective-permute-done.3 = bf16[144,384]{1,0:T(8,128)(2,1)S(1)} collective-permute-done((bf16[144,384]{1,0:T(8,128)(2,1)S(1)}, bf16[144,384]{1,0:T(8,128)(2,1)S(1)}, u32[]{:S(2)}, u32[]{:S(2)}) %collective-permute-start.3) | collective-permute-done | bytes 110624 | tf_op jit(solution)/shard_map/ppermute | solution.py:85
  23.1 2.4 %collective-permute-start.9 = (bf16[3,144,384]{2,1,0:T(8,128)(2,1)}, bf16[3,144,384]{2,1,0:T(8,128)(2,1)}, u32[]{:S(2)}, u32[]{:S(2)}) collective-permute-start(bf16[3,144,384]{2,1,0:T(8,128)(2,1)} %pad_maximum_fusion.14), channel_id=1, source_target_pairs={{4,1},{5,0},{6,3},{7,2},{0,5},{1,4},{2,7},{3,6},{12,9},{13,8},{14,... | collective-permute-start | bytes 995336 | tf_op jit(solution)/shard_map/ppermute | solution.py:93
  26.1 1.2 collective-permute-start.11
  28.2 3.0 %collective-permute-done.11 = bf16[144,384]{1,0:T(8,128)(2,1)} collective-permute-done((bf16[144,384]{1,0:T(8,128)(2,1)}, bf16[144,384]{1,0:T(8,128)(2,1)}, u32[]{:S(2)}, u32[]{:S(2)}) %collective-permute-start.11) | collective-permute-done | bytes 110624 | tf_op jit(solution)/shard_map/ppermute | solution.py:85
  32.6 6.1 %collective-permute-done.12 = bf16[144,384]{1,0:T(8,128)(2,1)S(1)} collective-permute-done((bf16[144,384]{1,0:T(8,128)(2,1)}, bf16[144,384]{1,0:T(8,128)(2,1)S(1)}, u32[]{:S(2)}, u32[]{:S(2)}) %collective-permute-start.12) | collective-permute-done | bytes 110624 | tf_op jit(solution)/shard_map/ppermute | solution.py:85
  38.7 1.5 %collective-permute-start.7 = (bf16[2,2,144,384]{3,2,1,0:T(8,128)(2,1)S(1)}, bf16[2,2,144,384]{3,2,1,0:T(8,128)(2,1)S(1)}, u32[]{:S(2)}, u32[]{:S(2)}) collective-permute-start(bf16[2,2,144,384]{3,2,1,0:T(8,128)(2,1)S(1)} %pad_maximum_fusion.13), channel_id=1, source_target_pairs={{0,4},{2,6},{4,0},{6,2},{8,12},{10,14},{12,8},{14,10},{16,20},{18,... | collective-permute-start | bytes 1327112 | tf_op jit(solution)/shard_map/ppermute | solution.py:109
  41.1 1.1 select_bitcast_fusion.5
  42.4 7.2 %collective-permute-done.6 = bf16[3,144,384]{2,1,0:T(8,128)(2,1)S(1)} collective-permute-done((bf16[3,144,384]{2,1,0:T(8,128)(2,1)}, bf16[3,144,384]{2,1,0:T(8,128)(2,1)S(1)}, u32[]{:S(2)}, u32[]{:S(2)}) %collective-permute-start.6) | collective-permute-done | bytes 331808 | tf_op jit(solution)/shard_map/ppermute | solution.py:90
  53.1 1.6 %collective-permute-start.15 = (bf16[3,144,384]{2,1,0:T(8,128)(2,1)S(1)}, bf16[3,144,384]{2,1,0:T(8,128)(2,1)S(1)}, u32[]{:S(2)}, u32[]{:S(2)}) collective-permute-start(bf16[3,144,384]{2,1,0:T(8,128)(2,1)S(1)} %pad_maximum_fusion.15), channel_id=1, source_target_pairs={{0,4},{2,6},{4,0},{6,2},{8,12},{10,14},{12,8},{14,10},{16,20},{18,... | collective-permute-start | bytes 995336 | tf_op jit(solution)/shard_map/ppermute | solution.py:90
  56.9 3.4 %fusion.40 = (bf16[2,528,384]{2,1,0:T(8,128)(2,1)S(1)}, bf16[2,528,384]{2,1,0:T(8,128)(2,1)S(1)}) fusion(pred[528]{0:T(1024)(128)(4,1)S(1)} %fusion.121, bf16[2304,384,1]{1,0,2:T(8,128)(2,1)S(1)} %bitcast.213, bf16[2,528,768]{2,1,0:T(8,128)(2,1)S(1)} %get-tuple-element.103, bf16[2,528,768]{2,1,0:T(8,128)(2,1)S(1)} %get-tuple-element.104, ...), kind=kOutput, calls=%fused_computation.69 | convolution fusion | flops 1887215616 | bytes 9069080 | tf_op jit(solution)/shard_map/dot_general | solution.py:141
  63.5 4.2 %fusion.20 = bf16[2304,384]{1,0:T(8,128)(2,1)S(1)} fusion(bf16[2,544,384]{2,1,0:T(8,128)(2,1)S(1)} %fusion.75, bf16[2,528,384]{2,1,0:T(8,128)(2,1)S(1)} %get-tuple-element.108, bf16[2,528,384]{2,1,0:T(8,128)(2,1)S(1)} %get-tuple-element.107, bf16[2,512,768]{2,1,0:T(8,128)(2,1)S(1)} %get-tuple-element.106, bf16[2,512,768]{2,1,0:T(8,128)(2,1)S(1)} %get-tuple-element.105), kind=kOutput, calls=%fused_computation.18 | convolution fusion | flops 1832583168 | bytes 7323648 | tf_op jit(solution)/shard_map/dot_general | solution.py:153
  67.7 3.9 %collective-permute-done.16 = bf16[3,144,384]{2,1,0:T(8,128)(2,1)S(1)} collective-permute-done((bf16[3,144,384]{2,1,0:T(8,128)(2,1)S(1)}, bf16[3,144,384]{2,1,0:T(8,128)(2,1)S(1)}, u32[]{:S(2)}, u32[]{:S(2)}) %collective-permute-start.16) | collective-permute-done | bytes 331808 | tf_op jit(solution)/shard_map/ppermute | solution.py:93
  75.6 2.8 %add_convert_fusion.1 = bf16[2,512,384]{2,1,0:T(8,128)(2,1)S(1)} fusion(bf16[2304,384,1]{1,0,2:T(8,128)(2,1)S(1)} %bitcast.215, bf16[2,528,384]{2,1,0:T(8,128)(2,1)S(1)} %get-tuple-element.148, bf16[2,528,384]{2,1,0:T(8,128)(2,1)S(1)} %get-tuple-element.108, bf16[2,528,384]{2,1,0:T(8,128)(2,1)S(1)} %get-tuple-element.107, ...), kind=kOutput, calls=%fused_computation.92 | convolution fusion | flops 1831993344 | bytes 8110080 | tf_op jit(solution)/shard_map/dot_general | solution.py:233
  78.4 5.3 %collective-permute-done.17 = bf16[2,2,144,384]{3,2,0,1:T(8,128)(2,1)S(1)} collective-permute-done((bf16[2,2,144,384]{3,2,0,1:T(8,128)(2,1)S(1)}, bf16[2,2,144,384]{3,2,0,1:T(8,128)(2,1)S(1)}, u32[]{:S(2)}, u32[]{:S(2)}) %collective-permute-start.17) | collective-permute-done | bytes 442400 | tf_op jit(solution)/shard_map/ppermute | solution.py:170
  84.8 1.1 collective-permute-start.22
  87.0 3.9 %collective-permute-done.22 = bf16[2,144,384]{2,1,0:T(8,128)(2,1)S(1)} collective-permute-done((bf16[2,144,384]{2,1,0:T(8,128)(2,1)S(1)}, bf16[2,144,384]{2,1,0:T(8,128)(2,1)S(1)}, u32[]{:S(2)}, u32[]{:S(2)}) %collective-permute-start.22) | collective-permute-done | bytes 221216 | tf_op jit(solution)/shard_map/ppermute | solution.py:177
  92.1 2.4 %fusion.34 = f32[2,544,1152]{2,1,0:T(8,128)S(1)} fusion(bf16[2,544,768]{2,1,0:T(8,128)(2,1)S(1)} %pad_maximum_fusion.2, bf16[1152,384]{1,0:T(8,128)(2,1)S(1)} %bitcast.234, bf16[1152,384]{1,0:T(8,128)(2,1)S(1)} %bitcast.233), kind=kOutput, calls=%fused_computation.60 | convolution fusion | flops 1928724480 | bytes 8454144 | tf_op jit(solution)/shard_map/dot_general | solution.py:217
  94.5 1.4 fusion.49
  95.9 4.3 %fusion.21 = bf16[2304,384]{1,0:T(8,128)(2,1)S(1)} fusion(bf16[2,528,768]{2,1,0:T(8,128)(2,1)S(1)} %get-tuple-element.103, bf16[2,528,768]{2,1,0:T(8,128)(2,1)S(1)} %get-tuple-element.104, bf16[2,528,768]{2,1,0:T(8,128)(2,1)S(1)} %get-tuple-element.102, bf16[2,528,384]{2,1,0:T(8,128)(2,1)S(1)} %fusion.49), kind=kOutput, calls=%fused_computation.19 | convolution fusion | flops 1827864576 | bytes 7421952 | tf_op jit(solution)/shard_map/dot_general | solution.py:153
  104.1 2.8 %collective-permute-start.31 = (bf16[144,384]{1,0:T(8,128)(2,1)S(1)}, bf16[144,384]{1,0:T(8,128)(2,1)S(1)}, u32[]{:S(2)}, u32[]{:S(2)}) collective-permute-start(bf16[144,384]{1,0:T(8,128)(2,1)S(1)} %get-tuple-element.85), channel_id=1, source_target_pairs={{0,24},{2,26},{4,28},{6,30},{8,0},{10,2},{12,4},{14,6},{16,8},{18,... | collective-permute-start | bytes 331784 | tf_op jit(solution)/shard_map/ppermute | solution.py:190
  106.9 3.4 %collective-permute-done.24 = bf16[2,2,144,384]{3,2,0,1:T(8,128)(2,1)S(1)} collective-permute-done((bf16[2,2,144,384]{3,2,0,1:T(8,128)(2,1)S(1)}, bf16[2,2,144,384]{3,2,0,1:T(8,128)(2,1)S(1)}, u32[]{:S(2)}, u32[]{:S(2)}) %collective-permute-start.24) | collective-permute-done | bytes 442400 | tf_op jit(solution)/shard_map/ppermute | solution.py:170
  110.4 1.4 collective-permute-done.25
  113.0 1.1 collective-permute-start.27
  114.2 3.8 %collective-permute-done.26 = bf16[2,144,384]{2,1,0:T(8,128)(2,1)S(1)} collective-permute-done((bf16[2,144,384]{2,1,0:T(8,128)(2,1)S(1)}, bf16[2,144,384]{2,1,0:T(8,128)(2,1)S(1)}, u32[]{:S(2)}, u32[]{:S(2)}) %collective-permute-start.26) | collective-permute-done | bytes 221216 | tf_op jit(solution)/shard_map/ppermute | solution.py:177
  120.4 2.8 %collective-permute-start.28 = (bf16[144,384]{1,0:T(8,128)(2,1)S(1)}, bf16[144,384]{1,0:T(8,128)(2,1)S(1)}, u32[]{:S(2)}, u32[]{:S(2)}) collective-permute-start(bf16[144,384]{1,0:T(8,128)(2,1)S(1)} %get-tuple-element.82), channel_id=1, source_target_pairs={{0,24},{2,26},{4,28},{6,30},{8,0},{10,2},{12,4},{14,6},{16,8},{18,... | collective-permute-start | bytes 331784 | tf_op jit(solution)/shard_map/ppermute | solution.py:190
  123.4 3.8 %collective-permute-done.30 = bf16[144,384]{1,0:T(8,128)(2,1)S(1)} collective-permute-done((bf16[144,384]{1,0:T(8,128)(2,1)S(1)}, bf16[144,384]{1,0:T(8,128)(2,1)S(1)}, u32[]{:S(2)}, u32[]{:S(2)}) %collective-permute-start.30) | collective-permute-done | bytes 110624 | tf_op jit(solution)/shard_map/ppermute | solution.py:190
  127.1 3.4 %collective-permute-done.29 = bf16[144,384]{1,0:T(8,128)(2,1)S(1)} collective-permute-done((bf16[144,384]{1,0:T(8,128)(2,1)S(1)}, bf16[144,384]{1,0:T(8,128)(2,1)S(1)}, u32[]{:S(2)}, u32[]{:S(2)}) %collective-permute-start.29) | collective-permute-done | bytes 110624 | tf_op jit(solution)/shard_map/ppermute | solution.py:190
  133.8 2.3 %fusion.63 = bf16[1,512,768]{2,1,0:T(8,128)(2,1)} fusion(f32[512,768]{1,0:T(8,128)S(1)} %fusion.68, f32[512,768]{1,0:T(8,128)S(1)} %fusion.65, bf16[2304,384]{1,0:T(8,128)(2,1)S(1)} %get-tuple-element.90, bf16[2304,384]{1,0:T(8,128)(2,1)S(1)} %get-tuple-element.91, bf16[528,384]{1,0:T(8,128)(2,1)S(1)} %get-tuple-element.109, ...), kind=kOutput, calls=%fused_computation.97 | convolution fusion | flops 614989824 | bytes 9879552 | tf_op jit(solution)/shard_map/dot_general | solution.py:244
  (148 shorter events, 39.2 us)
Async XLA Ops:
  8.9 7.6 %collective-permute-start.2 = (bf16[144,384]{1,0:T(8,128)(2,1)S(1)}, bf16[144,384]{1,0:T(8,128)(2,1)S(1)}, u32[]{:S(2)}, u32[]{:S(2)}) collective-permute-start(bf16[144,384]{1,0:T(8,128)(2,1)S(1)} %get-tuple-element.46), channel_id=1, source_target_pairs={{0,24},{2,26},{4,28},{6,30},{8,0},{10,2},{12,4},{14,6},{16,8},{18,... | collective-permute-start | bytes 331784 | tf_op jit(solution)/shard_map/ppermute | solution.py:85
  13.0 9.3 %collective-permute-start.3 = (bf16[144,384]{1,0:T(8,128)(2,1)S(1)}, bf16[144,384]{1,0:T(8,128)(2,1)S(1)}, u32[]{:S(2)}, u32[]{:S(2)}) collective-permute-start(bf16[144,384]{1,0:T(8,128)(2,1)S(1)} %get-tuple-element.46), channel_id=1, source_target_pairs={{0,16},{2,18},{4,20},{6,22},{8,24},{10,26},{12,28},{14,30},{16,0},... | collective-permute-start | bytes 331784 | tf_op jit(solution)/shard_map/ppermute | solution.py:85
  13.0 9.3 %collective-permute-start.4 = (bf16[144,384]{1,0:T(8,128)(2,1)S(1)}, bf16[144,384]{1,0:T(8,128)(2,1)S(1)}, u32[]{:S(2)}, u32[]{:S(2)}) collective-permute-start(bf16[144,384]{1,0:T(8,128)(2,1)S(1)} %get-tuple-element.46), channel_id=1, source_target_pairs={{0,8},{2,10},{4,12},{6,14},{8,16},{10,18},{12,20},{14,22},{16,24},... | collective-permute-start | bytes 331784 | tf_op jit(solution)/shard_map/ppermute | solution.py:85
  23.1 18.1 %collective-permute-start.9 = (bf16[3,144,384]{2,1,0:T(8,128)(2,1)}, bf16[3,144,384]{2,1,0:T(8,128)(2,1)}, u32[]{:S(2)}, u32[]{:S(2)}) collective-permute-start(bf16[3,144,384]{2,1,0:T(8,128)(2,1)} %pad_maximum_fusion.14), channel_id=1, source_target_pairs={{4,1},{5,0},{6,3},{7,2},{0,5},{1,4},{2,7},{3,6},{12,9},{13,8},{14,... | collective-permute-start | bytes 995336 | tf_op jit(solution)/shard_map/ppermute | solution.py:93
  25.4 15.7 %collective-permute-start.8 = (bf16[3,144,384]{2,1,0:T(8,128)(2,1)}, bf16[3,144,384]{2,1,0:T(8,128)(2,1)}, u32[]{:S(2)}, u32[]{:S(2)}) collective-permute-start(bf16[3,144,384]{2,1,0:T(8,128)(2,1)} %pad_maximum_fusion.14), channel_id=1, source_target_pairs={{0,4},{2,6},{4,0},{6,2},{8,12},{10,14},{12,8},{14,10},{16,20},{18,... | collective-permute-start | bytes 995336 | tf_op jit(solution)/shard_map/ppermute | solution.py:90
  26.1 5.1 %collective-permute-start.11 = (bf16[144,384]{1,0:T(8,128)(2,1)}, bf16[144,384]{1,0:T(8,128)(2,1)}, u32[]{:S(2)}, u32[]{:S(2)}) collective-permute-start(bf16[144,384]{1,0:T(8,128)(2,1)} %get-tuple-element.53), channel_id=1, source_target_pairs={{0,24},{2,26},{4,28},{6,30},{8,0},{10,2},{12,4},{14,6},{16,8},{18,... | collective-permute-start | bytes 331784 | tf_op jit(solution)/shard_map/ppermute | solution.py:85
  27.3 28.3 %collective-permute-start.5 = (bf16[544,1536]{1,0:T(8,128)(2,1)S(1)}, bf16[544,1536]{1,0:T(8,128)(2,1)S(1)}, u32[]{:S(2)}, u32[]{:S(2)}) collective-permute-start(bf16[544,1536]{1,0:T(8,128)(2,1)S(1)} %pad_maximum_fusion.1), channel_id=1, source_target_pairs={{0,2},{2,0},{4,6},{6,4},{8,10},{10,8},{12,14},{14,12},{16,18},{18,... | collective-permute-start | bytes 5013512 | tf_op jit(solution)/shard_map/ppermute | solution.py:117
  27.5 11.2 %collective-permute-start.12 = (bf16[144,384]{1,0:T(8,128)(2,1)}, bf16[144,384]{1,0:T(8,128)(2,1)S(1)}, u32[]{:S(2)}, u32[]{:S(2)}) collective-permute-start(bf16[144,384]{1,0:T(8,128)(2,1)} %get-tuple-element.53), channel_id=1, source_target_pairs={{0,16},{2,18},{4,20},{6,22},{8,24},{10,26},{12,28},{14,30},{16,0},... | collective-permute-start | bytes 331784 | tf_op jit(solution)/shard_map/ppermute | solution.py:85
  31.2 9.0 %collective-permute-start.13 = (bf16[144,384]{1,0:T(8,128)(2,1)}, bf16[144,384]{1,0:T(8,128)(2,1)S(1)}, u32[]{:S(2)}, u32[]{:S(2)}) collective-permute-start(bf16[144,384]{1,0:T(8,128)(2,1)} %get-tuple-element.53), channel_id=1, source_target_pairs={{0,8},{2,10},{4,12},{6,14},{8,16},{10,18},{12,20},{14,22},{16,24},... | collective-permute-start | bytes 331784 | tf_op jit(solution)/shard_map/ppermute | solution.py:85
  38.7 11.8 %collective-permute-start.7 = (bf16[2,2,144,384]{3,2,1,0:T(8,128)(2,1)S(1)}, bf16[2,2,144,384]{3,2,1,0:T(8,128)(2,1)S(1)}, u32[]{:S(2)}, u32[]{:S(2)}) collective-permute-start(bf16[2,2,144,384]{3,2,1,0:T(8,128)(2,1)S(1)} %pad_maximum_fusion.13), channel_id=1, source_target_pairs={{0,4},{2,6},{4,0},{6,2},{8,12},{10,14},{12,8},{14,10},{16,20},{18,... | collective-permute-start | bytes 1327112 | tf_op jit(solution)/shard_map/ppermute | solution.py:109
  40.2 9.3 %collective-permute-start.6 = (bf16[3,144,384]{2,1,0:T(8,128)(2,1)}, bf16[3,144,384]{2,1,0:T(8,128)(2,1)S(1)}, u32[]{:S(2)}, u32[]{:S(2)}) collective-permute-start(bf16[3,144,384]{2,1,0:T(8,128)(2,1)} %pad_maximum_fusion.14), channel_id=1, source_target_pairs={{0,1},{1,0},{2,3},{3,2},{4,5},{5,4},{6,7},{7,6},{8,9},{9,8},{10,11... | collective-permute-start | bytes 995336 | tf_op jit(solution)/shard_map/ppermute | solution.py:90
  52.0 9.6 %collective-permute-start.21 = (bf16[2304,384]{1,0:T(8,128)(2,1)S(1)}, bf16[2304,384]{1,0:T(8,128)(2,1)S(1)}, u32[]{:S(2)}, u32[]{:S(2)}) collective-permute-start(bf16[2304,384]{1,0:T(8,128)(2,1)S(1)} %bitcast.212), channel_id=1, source_target_pairs={{0,2},{2,0},{4,6},{6,4},{8,10},{10,8},{12,14},{14,12},{16,18},{18,... | collective-permute-start | bytes 5308424 | tf_op jit(solution)/shard_map/ppermute | solution.py:139
  53.1 14.6 %collective-permute-start.15 = (bf16[3,144,384]{2,1,0:T(8,128)(2,1)S(1)}, bf16[3,144,384]{2,1,0:T(8,128)(2,1)S(1)}, u32[]{:S(2)}, u32[]{:S(2)}) collective-permute-start(bf16[3,144,384]{2,1,0:T(8,128)(2,1)S(1)} %pad_maximum_fusion.15), channel_id=1, source_target_pairs={{0,4},{2,6},{4,0},{6,2},{8,12},{10,14},{12,8},{14,10},{16,20},{18,... | collective-permute-start | bytes 995336 | tf_op jit(solution)/shard_map/ppermute | solution.py:90
  54.6 17.2 %collective-permute-start.14 = (bf16[3,144,384]{2,1,0:T(8,128)(2,1)S(1)}, bf16[3,144,384]{2,1,0:T(8,128)(2,1)S(1)}, u32[]{:S(2)}, u32[]{:S(2)}) collective-permute-start(bf16[3,144,384]{2,1,0:T(8,128)(2,1)S(1)} %pad_maximum_fusion.15), channel_id=1, source_target_pairs={{0,1},{1,0},{2,3},{3,2},{4,5},{5,4},{6,7},{7,6},{8,9},{9,8},{10,11... | collective-permute-start | bytes 995336 | tf_op jit(solution)/shard_map/ppermute | solution.py:90
  60.4 11.2 %collective-permute-start.16 = (bf16[3,144,384]{2,1,0:T(8,128)(2,1)S(1)}, bf16[3,144,384]{2,1,0:T(8,128)(2,1)S(1)}, u32[]{:S(2)}, u32[]{:S(2)}) collective-permute-start(bf16[3,144,384]{2,1,0:T(8,128)(2,1)S(1)} %pad_maximum_fusion.15), channel_id=1, source_target_pairs={{4,1},{5,0},{6,3},{7,2},{0,5},{1,4},{2,7},{3,6},{12,9},{13,8},{14,... | collective-permute-start | bytes 995336 | tf_op jit(solution)/shard_map/ppermute | solution.py:93
  72.0 11.7 %collective-permute-start.17 = (bf16[2,2,144,384]{3,2,0,1:T(8,128)(2,1)S(1)}, bf16[2,2,144,384]{3,2,0,1:T(8,128)(2,1)S(1)}, u32[]{:S(2)}, u32[]{:S(2)}) collective-permute-start(bf16[2,2,144,384]{3,2,0,1:T(8,128)(2,1)S(1)} %bitcast.235), channel_id=1, source_target_pairs={{0,4},{2,6},{4,0},{6,2},{8,12},{10,14},{12,8},{14,10},{16,20},{18,... | collective-permute-start | bytes 1327112 | tf_op jit(solution)/shard_map/ppermute | solution.py:170
  72.8 11.7 %collective-permute-start.18 = (bf16[2,2,144,384]{3,2,1,0:T(8,128)(2,1)S(1)}, bf16[2,2,144,384]{3,2,1,0:T(8,128)(2,1)S(1)}, u32[]{:S(2)}, u32[]{:S(2)}) collective-permute-start(bf16[2,2,144,384]{3,2,1,0:T(8,128)(2,1)S(1)} %dynamic-slice_bitcast_fusion), channel_id=1, source_target_pairs={{0,1},{1,0},{2,3},{3,2},{4,5},{5,4},{6,7},{7,6},{8,9},{9,8},{10,11... | collective-permute-start | bytes 1327112 | tf_op jit(solution)/shard_map/ppermute | solution.py:171
  75.5 16.4 %collective-permute-start.19 = (bf16[2304,384]{1,0:T(8,128)(2,1)S(1)}, bf16[2304,384]{1,0:T(8,128)(2,1)S(1)}, u32[]{:S(2)}, u32[]{:S(2)}) collective-permute-start(bf16[2304,384]{1,0:T(8,128)(2,1)S(1)} %bitcast.214), channel_id=1, source_target_pairs={{0,2},{2,0},{4,6},{6,4},{8,10},{10,8},{12,14},{14,12},{16,18},{18,... | collective-permute-start | bytes 5308424 | tf_op jit(solution)/shard_map/ppermute | solution.py:209
  84.8 6.1 %collective-permute-start.22 = (bf16[2,144,384]{2,1,0:T(8,128)(2,1)S(1)}, bf16[2,144,384]{2,1,0:T(8,128)(2,1)S(1)}, u32[]{:S(2)}, u32[]{:S(2)}) collective-permute-start(bf16[2,144,384]{2,1,0:T(8,128)(2,1)S(1)} %dynamic-slice_bitcast_fusion.4), channel_id=1, source_target_pairs={{0,1},{1,0},{2,3},{3,2},{4,5},{5,4},{6,7},{7,6},{8,9},{9,8},{10,11... | collective-permute-start | bytes 663560 | tf_op jit(solution)/shard_map/ppermute | solution.py:177
  85.9 5.9 %collective-permute-start.23 = (bf16[2,144,384]{2,1,0:T(8,128)(2,1)S(1)}, bf16[2,144,384]{2,1,0:T(8,128)(2,1)S(1)}, u32[]{:S(2)}, u32[]{:S(2)}) collective-permute-start(bf16[2,144,384]{2,1,0:T(8,128)(2,1)S(1)} %dynamic-slice_bitcast_fusion.3), channel_id=1, source_target_pairs={{0,4},{2,6},{4,0},{6,2},{8,12},{10,14},{12,8},{14,10},{16,20},{18,... | collective-permute-start | bytes 663560 | tf_op jit(solution)/shard_map/ppermute | solution.py:178
  100.7 9.6 %collective-permute-start.24 = (bf16[2,2,144,384]{3,2,0,1:T(8,128)(2,1)S(1)}, bf16[2,2,144,384]{3,2,0,1:T(8,128)(2,1)S(1)}, u32[]{:S(2)}, u32[]{:S(2)}) collective-permute-start(bf16[2,2,144,384]{3,2,0,1:T(8,128)(2,1)S(1)} %bitcast.236), channel_id=1, source_target_pairs={{0,4},{2,6},{4,0},{6,2},{8,12},{10,14},{12,8},{14,10},{16,20},{18,... | collective-permute-start | bytes 1327112 | tf_op jit(solution)/shard_map/ppermute | solution.py:170
  101.8 9.9 %collective-permute-start.25 = (bf16[2,2,144,384]{3,2,0,1:T(8,128)(2,1)S(1)}, bf16[2,2,144,384]{3,2,0,1:T(8,128)(2,1)S(1)}, u32[]{:S(2)}, u32[]{:S(2)}) collective-permute-start(bf16[2,2,144,384]{3,2,0,1:T(8,128)(2,1)S(1)} %bitcast.237), channel_id=1, source_target_pairs={{0,1},{1,0},{2,3},{3,2},{4,5},{5,4},{6,7},{7,6},{8,9},{9,8},{10,11... | collective-permute-start | bytes 1327112 | tf_op jit(solution)/shard_map/ppermute | solution.py:171
  103.0 16.3 %collective-permute-start.33 = (bf16[144,384]{1,0:T(8,128)(2,1)S(1)}, bf16[144,384]{1,0:T(8,128)(2,1)S(1)}, u32[]{:S(2)}, u32[]{:S(2)}) collective-permute-start(bf16[144,384]{1,0:T(8,128)(2,1)S(1)} %get-tuple-element.87), channel_id=1, source_target_pairs={{0,8},{2,10},{4,12},{6,14},{8,16},{10,18},{12,20},{14,22},{16,24},... | collective-permute-start | bytes 331784 | tf_op jit(solution)/shard_map/ppermute | solution.py:190
  103.1 17.3 %collective-permute-start.32 = (bf16[144,384]{1,0:T(8,128)(2,1)S(1)}, bf16[144,384]{1,0:T(8,128)(2,1)S(1)}, u32[]{:S(2)}, u32[]{:S(2)}) collective-permute-start(bf16[144,384]{1,0:T(8,128)(2,1)S(1)} %get-tuple-element.86), channel_id=1, source_target_pairs={{0,16},{2,18},{4,20},{6,22},{8,24},{10,26},{12,28},{14,30},{16,0},... | collective-permute-start | bytes 331784 | tf_op jit(solution)/shard_map/ppermute | solution.py:190
  104.1 19.1 %collective-permute-start.31 = (bf16[144,384]{1,0:T(8,128)(2,1)S(1)}, bf16[144,384]{1,0:T(8,128)(2,1)S(1)}, u32[]{:S(2)}, u32[]{:S(2)}) collective-permute-start(bf16[144,384]{1,0:T(8,128)(2,1)S(1)} %get-tuple-element.85), channel_id=1, source_target_pairs={{0,24},{2,26},{4,28},{6,30},{8,0},{10,2},{12,4},{14,6},{16,8},{18,... | collective-permute-start | bytes 331784 | tf_op jit(solution)/shard_map/ppermute | solution.py:190
  112.0 6.0 %collective-permute-start.26 = (bf16[2,144,384]{2,1,0:T(8,128)(2,1)S(1)}, bf16[2,144,384]{2,1,0:T(8,128)(2,1)S(1)}, u32[]{:S(2)}, u32[]{:S(2)}) collective-permute-start(bf16[2,144,384]{2,1,0:T(8,128)(2,1)S(1)} %dynamic-slice_bitcast_fusion.2), channel_id=1, source_target_pairs={{0,1},{1,0},{2,3},{3,2},{4,5},{5,4},{6,7},{7,6},{8,9},{9,8},{10,11... | collective-permute-start | bytes 663560 | tf_op jit(solution)/shard_map/ppermute | solution.py:177
  113.0 5.9 %collective-permute-start.27 = (bf16[2,144,384]{2,1,0:T(8,128)(2,1)S(1)}, bf16[2,144,384]{2,1,0:T(8,128)(2,1)S(1)}, u32[]{:S(2)}, u32[]{:S(2)}) collective-permute-start(bf16[2,144,384]{2,1,0:T(8,128)(2,1)S(1)} %dynamic-slice_bitcast_fusion.1), channel_id=1, source_target_pairs={{0,4},{2,6},{4,0},{6,2},{8,12},{10,14},{12,8},{14,10},{16,20},{18,... | collective-permute-start | bytes 663560 | tf_op jit(solution)/shard_map/ppermute | solution.py:178
  118.0 13.7 %collective-permute-start.20 = (bf16[1040,384]{1,0:T(8,128)(2,1)S(1)}, bf16[1040,384]{1,0:T(8,128)(2,1)S(1)}, u32[]{:S(2)}, u32[]{:S(2)}) collective-permute-start(bf16[1040,384]{1,0:T(8,128)(2,1)S(1)} %pad_maximum_fusion.9), channel_id=1, source_target_pairs={{0,2},{2,0},{4,6},{6,4},{8,10},{10,8},{12,14},{14,12},{16,18},{18,... | collective-permute-start | bytes 2396168 | tf_op jit(solution)/shard_map/ppermute | solution.py:236
  119.3 7.9 %collective-permute-start.30 = (bf16[144,384]{1,0:T(8,128)(2,1)S(1)}, bf16[144,384]{1,0:T(8,128)(2,1)S(1)}, u32[]{:S(2)}, u32[]{:S(2)}) collective-permute-start(bf16[144,384]{1,0:T(8,128)(2,1)S(1)} %get-tuple-element.84), channel_id=1, source_target_pairs={{0,8},{2,10},{4,12},{6,14},{8,16},{10,18},{12,20},{14,22},{16,24},... | collective-permute-start | bytes 331784 | tf_op jit(solution)/shard_map/ppermute | solution.py:190
  119.4 11.2 %collective-permute-start.29 = (bf16[144,384]{1,0:T(8,128)(2,1)S(1)}, bf16[144,384]{1,0:T(8,128)(2,1)S(1)}, u32[]{:S(2)}, u32[]{:S(2)}) collective-permute-start(bf16[144,384]{1,0:T(8,128)(2,1)S(1)} %get-tuple-element.83), channel_id=1, source_target_pairs={{0,16},{2,18},{4,20},{6,22},{8,24},{10,26},{12,28},{14,30},{16,0},... | collective-permute-start | bytes 331784 | tf_op jit(solution)/shard_map/ppermute | solution.py:190
  120.4 10.2 %collective-permute-start.28 = (bf16[144,384]{1,0:T(8,128)(2,1)S(1)}, bf16[144,384]{1,0:T(8,128)(2,1)S(1)}, u32[]{:S(2)}, u32[]{:S(2)}) collective-permute-start(bf16[144,384]{1,0:T(8,128)(2,1)S(1)} %get-tuple-element.82), channel_id=1, source_target_pairs={{0,24},{2,26},{4,28},{6,30},{8,0},{10,2},{12,4},{14,6},{16,8},{18,... | collective-permute-start | bytes 331784 | tf_op jit(solution)/shard_map/ppermute | solution.py:190
  130.7 6.0 %collective-permute-start.34 = (bf16[2,144,384]{2,1,0:T(8,128)(2,1)S(1)}, bf16[2,144,384]{2,1,0:T(8,128)(2,1)S(1)}, u32[]{:S(2)}, u32[]{:S(2)}) collective-permute-start(bf16[2,144,384]{2,1,0:T(8,128)(2,1)S(1)} %pad_maximum_fusion.16), channel_id=1, source_target_pairs={{0,1},{1,0},{2,3},{3,2},{4,5},{5,4},{6,7},{7,6},{8,9},{9,8},{10,11... | collective-permute-start | bytes 663560 | tf_op jit(solution)/shard_map/ppermute | solution.py:198
  (19 other events, 127.1 us)

commit v3 on v2

--- a/solution.py
+++ b/solution.py
@@ -107,17 +107,19 @@
         return lines.reshape(parts * block, half)
 
     x_pair = lax.ppermute(after(pair, low, high), "dp", x_pairs)
-    first_turned = along_z(0, low, high)
+    first_turned, x_pair = together(along_z(0, low, high), x_pair)
     first_across = across(first_turned)
     first_corner = corner(first_turned)
-    second_turned = along_z(1, first_turned)
-    second_across = across(second_turned, first_corner)
 
     extended = after(jnp.concatenate([low, joined, high], axis=0), first_turned)
     partner = lax.ppermute(extended, "dp", core_pairs)
     pairs = jnp.stack([extended, partner])
     features_two, cot_two = pairs[..., :channels], pairs[..., channels:]
     act_first = gelu_value(features_two.astype(F32)).astype(BF16)
+    second_turned = along_z(1)
+    second_across = across(second_turned, first_corner, *first_across)
+    second_corner = corner(second_turned, first_corner, *first_across)
+    second_pieces = pair[1], x_pair[1], second_turned, *second_across, second_corner
     wide = rows + 2 * EDGE
 
     def shifted(array, offset, count):
@@ -135,13 +137,15 @@
     slope_first = gelu_slope(features[0].astype(F32))
 
     first_base = shifted(half_of(features_two, core, 2), HALO - EDGE, wide)
-    first_mine = assemble(pair[0], x_pair[0], first_turned, *first_across, first_corner)
+    first_pieces = pair[0], x_pair[0], first_turned, *first_across, first_corner
+    first_mine = assemble(*together(*first_pieces, second_turned)[:-1])
     first_theirs = lax.ppermute(first_mine, "dp", core_pairs)
     hidden = (
         first_base.astype(F32) + jnp.dot(stack_first, first_mine, preferred_element_type=F32)
     ).astype(BF16)
     act_mine = jnp.where(valid, gelu_value(hidden.astype(F32)), 0.0).astype(BF16)
-    second_corner = corner(second_turned, act_mine)
+    second_mine = assemble(*second_pieces)
+    second_theirs = lax.ppermute(second_mine, "dp", core_pairs)
     act_theirs = lax.ppermute(act_mine, "dp", core_pairs)[::-1]
     act_second = by_core(act_mine, act_theirs, 2)
     stack_second = jnp.concatenate(
@@ -162,60 +166,61 @@
     def add(left, right):
         return (left.astype(F32) + right.astype(F32)).astype(BF16)
 
-    def plane_sum(grad):
+    cut = depth // 2
+
+    def first_out(grad):
         grad = grad.reshape(depth, 2, 2, block, half)
-        cut = depth // 2
-        one, two = grad[:cut], grad[cut:]
-        one_out, two_out = together(take(one, 1 - me_x, 1), take(two, 1 - h, 2))
-        one_in = lax.ppermute(one_out, "dp", x_pairs)
-        two_in = lax.ppermute(two_out, "seq", y_pairs)
-        one_in, two_in = together(one_in, two_in)
-        return add(take(one, me_x, 1), one_in), add(take(two, h, 2), two_in)
-
-    def plane_rest(one, two):
-        one_out, two_out = together(take(one, 1 - h, 1), take(two, 1 - me_x, 1))
-        one_in = lax.ppermute(one_out, "seq", y_pairs)
-        two_in = lax.ppermute(two_out, "dp", x_pairs)
-        one_in, two_in = together(one_in, two_in)
-        one = add(take(one, h, 1), one_in)
-        two = add(take(two, me_x, 1), two_in)
+        return take(grad[:cut], 1 - me_x, 1), take(grad[cut:], 1 - h, 2)
+
+    def first_sum(grad, one_in, two_in):
+        grad = grad.reshape(depth, 2, 2, block, half)
+        return add(take(grad[:cut], me_x, 1), one_in), add(take(grad[cut:], h, 2), two_in)
+
+    def second_out(one, two):
+        return take(one, 1 - h, 1), take(two, 1 - me_x, 1)
+
+    def second_sum(one, two, one_in, two_in):
+        one, two = add(take(one, h, 1), one_in), add(take(two, me_x, 1), two_in)
         return jnp.concatenate([one, two], axis=0)
 
-    def line_sum(summed):
-        outs = together(
-            *(take(summed, (me_z - step) % depth, 0) for step in range(1, depth))
-        )
+    def line_out(summed):
+        return tuple(take(summed, (me_z - step) % depth, 0) for step in range(1, depth))
+
+    def line_sum(summed, came):
         total = take(summed, me_z, 0).astype(F32)
-        for step, out in enumerate(outs, 1):
-            total = total + lax.ppermute(out, "dp", turn(step)).astype(F32)
+        for part in came:
+            total = total + part.astype(F32)
         return total
 
-    def finish(totals):
+    def by_x(array):
+        return lax.ppermute(array, "dp", x_pairs)
+
+    def by_y(array):
+        return lax.ppermute(array, "seq", y_pairs)
+
+    def by_z(outs):
+        return tuple(lax.ppermute(out, "dp", turn(step)) for step, out in enumerate(outs, 1))
+
+    def across_y(total):
         if seqs > 2:
             groups = [[i for i in range(seqs) if i % 2 == k] for k in range(2)]
-            totals = lax.psum(totals, "seq", axis_index_groups=groups)
-        mine = totals.astype(BF16)
-        theirs = lax.ppermute(mine, "seq", y_pairs)
-        rows_two = jnp.stack(
-            [jnp.where(h == 0, mine, theirs), jnp.where(h == 0, theirs, mine)], axis=0
-        )
-        kept = take(rows_two, core, 0)
-        given = lax.ppermute(take(rows_two, 1 - core, 0), "dp", core_pairs)
+            total = lax.psum(total, "seq", axis_index_groups=groups)
+        mine = total.astype(BF16)
+        return mine, by_y(mine)
+
+    def finish(*pieces):
+        mine, theirs = jnp.stack(pieces[::2]), jnp.stack(pieces[1::2])
+        same = h == core
+        kept = jnp.where(same, mine, theirs)
+        given = lax.ppermute(jnp.where(same, theirs, mine), "dp", core_pairs)
         return by_core(kept, given, 2).astype(F32)
-
-    grad_second = gradient(stack_second, shifted(cot_mine, HALO, rows))
-    second_pieces = pair[1], x_pair[1], second_turned, *second_across, second_corner
-    second_mine = assemble(*(after(piece, grad_second) for piece in second_pieces))
-    second_theirs = lax.ppermute(second_mine, "dp", core_pairs)
-    half_second = plane_sum(grad_second)
-    plane_second = plane_rest(*half_second)
 
     slope = gelu_slope(hidden.astype(F32))
     mine, theirs = (
         take(side.reshape(3, 2, half, half), core, 1) for side in (second_mine, second_theirs)
     )
     product = lax.dot_general(
-        after(cot_two, *half_second),
+        cot_two,
         by_core(mine, theirs, 2).reshape(3 * half, channels),
         (((2,), (1,)), ((), ())),
         preferred_element_type=F32,
@@ -225,15 +230,32 @@
         part = shifted(product[..., tap * half : (tap + 1) * half], HALO - EDGE - (tap - 1) * 8, wide)
         spread = part if spread is None else spread + part
     grad_mine = jnp.where(valid, cot_base.astype(F32) + spread * slope, 0.0).astype(BF16)
-    grad_first = gradient(shifted(stack_first, EDGE, rows), shifted(grad_mine, EDGE, rows))
-    plane_first = plane_rest(*plane_sum(after(grad_first, plane_second)))
+    grad_first = gradient(
+        shifted(stack_first, EDGE, rows), shifted(grad_mine, EDGE, rows)
+    )
+    x_out, y_out = together(*first_out(grad_first))
+    first_came = by_x(x_out), by_y(y_out)
+    grad_second = gradient(stack_second, shifted(cot_mine, HALO, rows))
 
     tower_mine = (
         shifted(hidden, EDGE, rows).astype(F32)
         + jnp.dot(stack_second, second_mine, preferred_element_type=F32)
     ).astype(BF16)
     sent = jnp.concatenate([tower_mine[1], grad_mine[1]], axis=0)
+    sent, grad_second = together(sent, grad_second)
     came = lax.ppermute(sent, "dp", core_pairs)
+    came, *first_came = together(came, *first_came)
+    half_first = first_sum(grad_first, *first_came)
+    y_out, x_out, x_next, y_next = together(*second_out(*half_first), *first_out(grad_second))
+    y_in, x_in, x_come, y_come = together(by_y(y_out), by_x(x_out), by_x(x_next), by_y(y_next))
+    plane_first = second_sum(*half_first, y_in, x_in)
+    half_second = first_sum(grad_second, x_come, y_come)
+    y_out, x_out, *outs = together(*second_out(*half_second), *line_out(plane_first))
+    y_in, x_in, *line_first = together(by_y(y_out), by_x(x_out), *by_z(outs))
+    plane_second = second_sum(*half_second, y_in, x_in)
+    total_first = line_sum(plane_first, line_first)
+    total_first, *outs = together(total_first, *line_out(plane_second))
+    line_second = by_z(outs)
     tower = by_core(tower_mine[0], came[:rows], 1)
     grad_hidden = by_core(grad_mine[0], came[rows:], 1)
 
@@ -249,7 +271,10 @@
         grad_hidden[EDGE : EDGE + rows].astype(F32) + spread * slope_first
     ).astype(BF16)
 
-    done = finish(jnp.stack([line_sum(plane_first), line_sum(plane_second)]))
+    total_first, grad_input = together(total_first, grad_input)
+    across_first = across_y(total_first)
+    across_second = across_y(line_sum(plane_second, line_second))
+    done = finish(*together(*across_first, *across_second))
     return (tower[None], grad_input[None], done[0], done[1])
 
 

time: 140 us -> 140 us (level)
  starting transfers between devices: 36.5 us -> 43.6 us
  other arithmetic: 14.9 us -> 10.8 us
  local copies, waits for them, and re-layouts: 5.16 us -> 3.55 us
  waiting for transfers between devices: 60.4 us -> 58.9 us
    ppermute x2, waiting for transfers between devices: 0.01 us -> 8.03 us  [across(): lax.ppermute(given, 'dp', x_pairs)]
    ppermute x6, waiting for transfers between devices: 17.4 us -> 12.6 us  [along_z(): lax.ppermute(piece, 'dp', turn(step))]
    ppermute x6, starting transfers between devices: 7.33 us -> 10.6 us  [along_z(): lax.ppermute(piece, 'dp', turn(step))]
    ppermute x16 -> x17, starting transfers between devices: 17 us -> 19.9 us  [the longest x6 10.4 us: by_z(): lax.ppermute(out, 'dp', turn(step))]
    ppermute x16 -> x17, waiting for transfers between devices: 28.8 us -> 26.2 us  [the longest x6 17.4 us: by_y(): return lax.ppermute(array, 'seq', y_pairs)]
    ppermute x2, waiting for transfers between devices: 7.2 us -> 5.18 us  [across(): lax.ppermute(given, 'seq', y_pairs)]
    unnamed x30 -> x8, local copies, waits for them, and re-layouts: 1.72 us -> 0.02 us
    another operation x2, other arithmetic: 1.74 us -> 0.1 us  [along_z(): jnp.stack(together(*(lax.ppermute(piece, 'dp', turn(step)) for step in ra...]
  transfers between devices with their start and end apart: 36 -> 37, of which waited for: 21 -> 17; matrix products, arithmetic and copies ran while one was open for 19% -> 24% of each run, Pallas kernels for 0% -> 0%
where the time goes in v3:
time: 140 us
  waiting for transfers between devices  58.9 us (42%)
  starting transfers between devices  43.6 us (31%)
  matrix products  21.8 us (16%)
  other arithmetic  10.8 us (8%)
  local copies, waits for them, and re-layouts  3.55 us (3%)
    ppermute x6, waiting for transfers between devices, by_y(): return lax.ppermute(array, 'seq', y_pairs)  17.4 us
    ppermute x6, waiting for transfers between devices, along_z(): lax.ppermute(piece, 'dp', turn(step))  12.6 us
    ppermute x6, starting transfers between devices, along_z(): lax.ppermute(piece, 'dp', turn(step))  10.6 us
    ppermute x6, starting transfers between devices, by_z(): lax.ppermute(out, 'dp', turn(step))  10.4 us
    dot_general x2, matrix products, gradient(): lax.dot_general(stacked.reshape(2 * rows, 3 * channels), upstream.reshape...  8.27 us
    ppermute x2, waiting for transfers between devices, across(): lax.ppermute(given, 'dp', x_pairs)  8.03 us
    ppermute x6, waiting for transfers between devices, by_z(): lax.ppermute(out, 'dp', turn(step))  6.57 us
    ppermute x6, starting transfers between devices, by_y(): return lax.ppermute(array, 'seq', y_pairs)  6.12 us
  transfers between devices with their start and end apart: 37, of which 17 were waited for; matrix products, arithmetic and copies ran while one was open for 24% of the time, Pallas kernels for 0%

profile of v3, /device:TPU:0, one launch (start us, length us, event | category | flops | bytes accessed | tf_op | source)
XLA Modules:
  0.0 139.9 jit_solution(9056259738392734298)
XLA Ops:
  1.5 3.0 %collective-permute-start = (bf16[16,1536]{1,0:T(8,128)(2,1)S(1)}, bf16[16,1536]{1,0:T(8,128)(2,1)S(1)}, u32[]{:S(2)}, u32[]{:S(2)}) collective-permute-start(bf16[16,1536]{1,0:T(8,128)(2,1)S(1)} %fusion.115), channel_id=1, source_target_pairs={{0,1},{1,0},{2,3},{3,2},{4,5},{5,4},{6,7},{7,6},{8,9},{9,8},{10,11... | collective-permute-start | bytes 147464 | tf_op jit(solution)/shard_map/ppermute | solution.py:73
  4.7 1.9 %collective-permute-done = bf16[16,1536]{1,0:T(8,128)(2,1)S(1)} collective-permute-done((bf16[16,1536]{1,0:T(8,128)(2,1)S(1)}, bf16[16,1536]{1,0:T(8,128)(2,1)S(1)}, u32[]{:S(2)}, u32[]{:S(2)}) %collective-permute-start) | collective-permute-done | bytes 49184 | tf_op jit(solution)/shard_map/ppermute | solution.py:73
  6.9 2.1 %collective-permute-start.5 = (bf16[2,2,144,384]{3,2,1,0:T(8,128)(2,1)S(1)}, bf16[2,2,144,384]{3,2,1,0:T(8,128)(2,1)S(1)}, u32[]{:S(2)}, u32[]{:S(2)}) collective-permute-start(bf16[2,2,144,384]{3,2,1,0:T(8,128)(2,1)S(1)} %pad_maximum_fusion.11), channel_id=1, source_target_pairs={{0,4},{2,6},{4,0},{6,2},{8,12},{10,14},{12,8},{14,10},{16,20},{18,... | collective-permute-start | bytes 1327112 | tf_op jit(solution)/shard_map/ppermute | solution.py:109
  9.0 3.7 %collective-permute-start.2 = (bf16[144,384]{1,0:T(8,128)(2,1)S(1)}, bf16[144,384]{1,0:T(8,128)(2,1)S(1)}, u32[]{:S(2)}, u32[]{:S(2)}) collective-permute-start(bf16[144,384]{1,0:T(8,128)(2,1)S(1)} %dynamic-slice_bitcast_fusion.5), channel_id=1, source_target_pairs={{0,24},{2,26},{4,28},{6,30},{8,0},{10,2},{12,4},{14,6},{16,8},{18,... | collective-permute-start | bytes 331784 | tf_op jit(solution)/shard_map/ppermute | solution.py:85
  14.3 2.8 %collective-permute-start.10 = (bf16[144,384]{1,0:T(8,128)(2,1)}, bf16[144,384]{1,0:T(8,128)(2,1)S(1)}, u32[]{:S(2)}, u32[]{:S(2)}) collective-permute-start(bf16[144,384]{1,0:T(8,128)(2,1)} %dynamic-slice_bitcast_fusion.4), channel_id=1, source_target_pairs={{0,24},{2,26},{4,28},{6,30},{8,0},{10,2},{12,4},{14,6},{16,8},{18,... | collective-permute-start | bytes 331784 | tf_op jit(solution)/shard_map/ppermute | solution.py:85
  17.1 5.8 %collective-permute-done.3 = bf16[144,384]{1,0:T(8,128)(2,1)S(1)} collective-permute-done((bf16[144,384]{1,0:T(8,128)(2,1)S(1)}, bf16[144,384]{1,0:T(8,128)(2,1)S(1)}, u32[]{:S(2)}, u32[]{:S(2)}) %collective-permute-start.3) | collective-permute-done | bytes 110624 | tf_op jit(solution)/shard_map/ppermute | solution.py:85
  24.3 1.5 %collective-permute-start.7 = (bf16[3,144,384]{2,1,0:T(8,128)(2,1)S(1)}, bf16[3,144,384]{2,1,0:T(8,128)(2,1)}, u32[]{:S(2)}, u32[]{:S(2)}) collective-permute-start(bf16[3,144,384]{2,1,0:T(8,128)(2,1)S(1)} %pad_maximum_fusion.12), channel_id=1, source_target_pairs={{0,4},{2,6},{4,0},{6,2},{8,12},{10,14},{12,8},{14,10},{16,20},{18,... | collective-permute-start | bytes 995336 | tf_op jit(solution)/shard_map/ppermute | solution.py:90
  26.6 3.2 %collective-permute-start.11 = (bf16[144,384]{1,0:T(8,128)(2,1)}, bf16[144,384]{1,0:T(8,128)(2,1)S(1)}, u32[]{:S(2)}, u32[]{:S(2)}) collective-permute-start(bf16[144,384]{1,0:T(8,128)(2,1)} %dynamic-slice_bitcast_fusion.4), channel_id=1, source_target_pairs={{0,16},{2,18},{4,20},{6,22},{8,24},{10,26},{12,28},{14,30},{16,0},... | collective-permute-start | bytes 331784 | tf_op jit(solution)/shard_map/ppermute | solution.py:85
  29.7 5.4 %collective-permute-done.11 = bf16[144,384]{1,0:T(8,128)(2,1)S(1)} collective-permute-done((bf16[144,384]{1,0:T(8,128)(2,1)}, bf16[144,384]{1,0:T(8,128)(2,1)S(1)}, u32[]{:S(2)}, u32[]{:S(2)}) %collective-permute-start.11) | collective-permute-done | bytes 110624 | tf_op jit(solution)/shard_map/ppermute | solution.py:85
  35.1 1.4 collective-permute-done.12
  39.5 1.5 %collective-permute-start.16 = (bf16[3,144,384]{2,1,0:T(8,128)(2,1)S(1)}, bf16[3,144,384]{2,1,0:T(8,128)(2,1)S(1)}, u32[]{:S(2)}, u32[]{:S(2)}) collective-permute-start(bf16[3,144,384]{2,1,0:T(8,128)(2,1)S(1)} %pad_maximum_fusion.13), channel_id=1, source_target_pairs={{4,1},{5,0},{6,3},{7,2},{0,5},{1,4},{2,7},{3,6},{12,9},{13,8},{14,... | collective-permute-start | bytes 995336 | tf_op jit(solution)/shard_map/ppermute | solution.py:93
  41.3 1.5 %collective-permute-start.14 = (bf16[3,144,384]{2,1,0:T(8,128)(2,1)S(1)}, bf16[3,144,384]{2,1,0:T(8,128)(2,1)S(1)}, u32[]{:S(2)}, u32[]{:S(2)}) collective-permute-start(bf16[3,144,384]{2,1,0:T(8,128)(2,1)S(1)} %pad_maximum_fusion.13), channel_id=1, source_target_pairs={{0,1},{1,0},{2,3},{3,2},{4,5},{5,4},{6,7},{7,6},{8,9},{9,8},{10,11... | collective-permute-start | bytes 995336 | tf_op jit(solution)/shard_map/ppermute | solution.py:90
  42.8 6.9 %collective-permute-done.15 = bf16[3,144,384]{2,1,0:T(8,128)(2,1)S(1)} collective-permute-done((bf16[3,144,384]{2,1,0:T(8,128)(2,1)S(1)}, bf16[3,144,384]{2,1,0:T(8,128)(2,1)S(1)}, u32[]{:S(2)}, u32[]{:S(2)}) %collective-permute-start.15) | collective-permute-done | bytes 331808 | tf_op jit(solution)/shard_map/ppermute | solution.py:90
  49.7 4.9 %collective-permute-done.16 = bf16[3,144,384]{2,1,0:T(8,128)(2,1)S(1)} collective-permute-done((bf16[3,144,384]{2,1,0:T(8,128)(2,1)S(1)}, bf16[3,144,384]{2,1,0:T(8,128)(2,1)S(1)}, u32[]{:S(2)}, u32[]{:S(2)}) %collective-permute-start.16) | collective-permute-done | bytes 331808 | tf_op jit(solution)/shard_map/ppermute | solution.py:93
  54.7 3.9 %collective-permute-done.14 = bf16[3,144,384]{2,1,0:T(8,128)(2,1)S(1)} collective-permute-done((bf16[3,144,384]{2,1,0:T(8,128)(2,1)S(1)}, bf16[3,144,384]{2,1,0:T(8,128)(2,1)S(1)}, u32[]{:S(2)}, u32[]{:S(2)}) %collective-permute-start.14) | collective-permute-done | bytes 331808 | tf_op jit(solution)/shard_map/ppermute | solution.py:90
  65.4 2.4 %fusion.34 = f32[2,544,1152]{2,1,0:T(8,128)S(1)} fusion(bf16[1152,384]{1,0:T(8,128)(2,1)S(1)} %bitcast.226, bf16[1152,384]{1,0:T(8,128)(2,1)S(1)} %bitcast.225, bf16[1,544,1536]{2,1,0:T(8,128)(2,1)S(1)} %bitcast.202, bf16[1,544,1536]{2,1,0:T(8,128)(2,1)S(1)} %bitcast.197), kind=kOutput, calls=%fused_computation.60 | convolution fusion | flops 1932066816 | bytes 10125312 | tf_op jit(solution)/shard_map/dot_general | solution.py:222
  67.8 4.2 %fusion.50 = (bf16[2,528,384]{2,1,0:T(8,128)(2,1)S(1)}, bf16[2,528,384]{2,1,0:T(8,128)(2,1)S(1)}, bf16[2,528,384]{2,1,0:T(8,128)(2,1)S(1)}) fusion(f32[2,544,1152]{2,1,0:T(8,128)S(1)} %fusion.34, bf16[2,544,384]{2,1,0:T(8,128)(2,1)S(1)} %fusion.77, pred[528]{0:T(1024)(128)(4,1)S(1)} %fusion.116, bf16[2304,384,1]{1,0,2:T(8,128)(2,1)S(1)} %bitcast.199, ...), kind=kOutput, calls=%fused_computation.79 | convolution fusion | flops 1892487168 | bytes 15557144 | tf_op jit(solution)/shard_map/dot_general | solution.py:144
  72.1 4.1 %fusion.21 = bf16[2304,384]{1,0:T(8,128)(2,1)S(1)} fusion(bf16[2,528,768]{2,1,0:T(8,128)(2,1)S(1)} %get-tuple-element.125, bf16[2,528,768]{2,1,0:T(8,128)(2,1)S(1)} %get-tuple-element.126, bf16[2,528,768]{2,1,0:T(8,128)(2,1)S(1)} %get-tuple-element.124, bf16[2,528,384]{2,1,0:T(8,128)(2,1)S(1)} %get-tuple-element.145), kind=kOutput, calls=%fused_computation.19 | convolution fusion | flops 1827864576 | bytes 7421952 | tf_op jit(solution)/shard_map/dot_general | solution.py:157
  77.3 1.4 %collective-permute-start.20 = (bf16[2,2,144,384]{3,2,0,1:T(8,128)(2,1)S(1)}, bf16[2,2,144,384]{3,2,0,1:T(8,128)(2,1)S(1)}, u32[]{:S(2)}, u32[]{:S(2)}) collective-permute-start(bf16[2,2,144,384]{3,2,0,1:T(8,128)(2,1)S(1)} %bitcast.230), channel_id=1, source_target_pairs={{0,1},{1,0},{2,3},{3,2},{4,5},{5,4},{6,7},{7,6},{8,9},{9,8},{10,11... | collective-permute-start | bytes 1327112 | tf_op jit(solution)/shard_map/ppermute | solution.py:199
  79.6 4.2 %fusion.20 = bf16[2304,384]{1,0:T(8,128)(2,1)S(1)} fusion(bf16[2,544,384]{2,1,0:T(8,128)(2,1)S(1)} %fusion.77, bf16[2,528,384]{2,1,0:T(8,128)(2,1)S(1)} %get-tuple-element.130, bf16[2,528,384]{2,1,0:T(8,128)(2,1)S(1)} %get-tuple-element.129, bf16[2,512,768]{2,1,0:T(8,128)(2,1)S(1)} %get-tuple-element.128, bf16[2,512,768]{2,1,0:T(8,128)(2,1)S(1)} %get-tuple-element.127), kind=kOutput, calls=%fused_computation.18 | convolution fusion | flops 1832583168 | bytes 7323648 | tf_op jit(solution)/shard_map/dot_general | solution.py:157
  83.8 3.1 %add_convert_fusion.1 = bf16[2,512,384]{2,1,0:T(8,128)(2,1)S(1)} fusion(bf16[2304,384,1]{1,0,2:T(8,128)(2,1)S(1)} %bitcast.205, bf16[2,528,384]{2,1,0:T(8,128)(2,1)S(1)} %get-tuple-element.171, bf16[2,528,384]{2,1,0:T(8,128)(2,1)S(1)} %get-tuple-element.130, bf16[2,528,384]{2,1,0:T(8,128)(2,1)S(1)} %get-tuple-element.129, ...), kind=kOutput, calls=%fused_computation.93 | convolution fusion | flops 1831993344 | bytes 8110080 | tf_op jit(solution)/shard_map/dot_general | solution.py:242
  87.6 1.8 %collective-permute-done.19 = bf16[2,2,144,384]{3,2,0,1:T(8,128)(2,1)S(1)} collective-permute-done((bf16[2,2,144,384]{3,2,0,1:T(8,128)(2,1)S(1)}, bf16[2,2,144,384]{3,2,0,1:T(8,128)(2,1)S(1)}, u32[]{:S(2)}, u32[]{:S(2)}) %collective-permute-start.19) | collective-permute-done | bytes 442400 | tf_op jit(solution)/shard_map/ppermute | solution.py:196
  89.9 1.6 %collective-permute-start.23 = (bf16[2,2,144,384]{3,2,0,1:T(8,128)(2,1)S(1)}, bf16[2,2,144,384]{3,2,0,1:T(8,128)(2,1)S(1)}, u32[]{:S(2)}, u32[]{:S(2)}) collective-permute-start(bf16[2,2,144,384]{3,2,0,1:T(8,128)(2,1)S(1)} %bitcast.227), channel_id=1, source_target_pairs={{0,4},{2,6},{4,0},{6,2},{8,12},{10,14},{12,8},{14,10},{16,20},{18,... | collective-permute-start | bytes 1327112 | tf_op jit(solution)/shard_map/ppermute | solution.py:196
  91.5 1.4 %collective-permute-start.24 = (bf16[2,2,144,384]{3,2,0,1:T(8,128)(2,1)S(1)}, bf16[2,2,144,384]{3,2,0,1:T(8,128)(2,1)S(1)}, u32[]{:S(2)}, u32[]{:S(2)}) collective-permute-start(bf16[2,2,144,384]{3,2,0,1:T(8,128)(2,1)S(1)} %bitcast.229), channel_id=1, source_target_pairs={{0,1},{1,0},{2,3},{3,2},{4,5},{5,4},{6,7},{7,6},{8,9},{9,8},{10,11... | collective-permute-start | bytes 1327112 | tf_op jit(solution)/shard_map/ppermute | solution.py:199
  94.7 13.2 %collective-permute-done.21 = bf16[2,144,384]{2,1,0:T(8,128)(2,1)S(1)} collective-permute-done((bf16[2,144,384]{2,1,0:T(8,128)(2,1)S(1)}, bf16[2,144,384]{2,1,0:T(8,128)(2,1)S(1)}, u32[]{:S(2)}, u32[]{:S(2)}) %collective-permute-start.21) | collective-permute-done | bytes 221216 | tf_op jit(solution)/shard_map/ppermute | solution.py:199
  111.0 4.5 %collective-permute-start.28 = (bf16[144,384]{1,0:T(8,128)(2,1)S(1)}, bf16[144,384]{1,0:T(8,128)(2,1)S(1)}, u32[]{:S(2)}, u32[]{:S(2)}) collective-permute-start(bf16[144,384]{1,0:T(8,128)(2,1)S(1)} %get-tuple-element.93), channel_id=1, source_target_pairs={{0,16},{2,18},{4,20},{6,22},{8,24},{10,26},{12,28},{14,30},{16,0},... | collective-permute-start | bytes 331784 | tf_op jit(solution)/shard_map/ppermute | solution.py:202
  115.5 1.9 %collective-permute-start.29 = (bf16[144,384]{1,0:T(8,128)(2,1)S(1)}, bf16[144,384]{1,0:T(8,128)(2,1)S(1)}, u32[]{:S(2)}, u32[]{:S(2)}) collective-permute-start(bf16[144,384]{1,0:T(8,128)(2,1)S(1)} %get-tuple-element.94), channel_id=1, source_target_pairs={{0,8},{2,10},{4,12},{6,14},{8,16},{10,18},{12,20},{14,22},{16,24},... | collective-permute-start | bytes 331784 | tf_op jit(solution)/shard_map/ppermute | solution.py:202
  118.3 5.4 %collective-permute-done.28 = bf16[144,384]{1,0:T(8,128)(2,1)S(1)} collective-permute-done((bf16[144,384]{1,0:T(8,128)(2,1)S(1)}, bf16[144,384]{1,0:T(8,128)(2,1)S(1)}, u32[]{:S(2)}, u32[]{:S(2)}) %collective-permute-start.28) | collective-permute-done | bytes 110624 | tf_op jit(solution)/shard_map/ppermute | solution.py:202
  124.8 3.2 %collective-permute-start.32 = (bf16[144,384]{1,0:T(8,128)(2,1)S(1)}, bf16[144,384]{1,0:T(8,128)(2,1)S(1)}, u32[]{:S(2)}, u32[]{:S(2)}) collective-permute-start(bf16[144,384]{1,0:T(8,128)(2,1)S(1)} %get-tuple-element.103), channel_id=1, source_target_pairs={{0,24},{2,26},{4,28},{6,30},{8,0},{10,2},{12,4},{14,6},{16,8},{18,... | collective-permute-start | bytes 331784 | tf_op jit(solution)/shard_map/ppermute | solution.py:202
  128.0 2.3 %fusion.61 = bf16[512,768]{1,0:T(8,128)(2,1)} fusion(f32[512,768]{1,0:T(8,128)S(1)} %fusion.70, f32[512,768]{1,0:T(8,128)S(1)} %fusion.67, bf16[2304,384]{1,0:T(8,128)(2,1)S(1)} %get-tuple-element.112, bf16[2304,384]{1,0:T(8,128)(2,1)S(1)} %get-tuple-element.113, bf16[528,384]{1,0:T(8,128)(2,1)S(1)} %get-tuple-element.131, ...), kind=kOutput, calls=%fused_computation.94 | convolution fusion | flops 614989824 | bytes 9879552 | tf_op jit(solution)/shard_map/dot_general | solution.py:266
  133.3 1.8 %collective-permute-done.31 = bf16[144,384]{1,0:T(8,128)(2,1)S(1)} collective-permute-done((bf16[144,384]{1,0:T(8,128)(2,1)S(1)}, bf16[144,384]{1,0:T(8,128)(2,1)S(1)}, u32[]{:S(2)}, u32[]{:S(2)}) %collective-permute-start.31) | collective-permute-done | bytes 110624 | tf_op jit(solution)/shard_map/ppermute | solution.py:199
  135.0 2.2 %collective-permute-done.35 = bf16[144,384]{1,0:T(8,128)(2,1)S(1)} collective-permute-done((bf16[144,384]{1,0:T(8,128)(2,1)S(1)}, bf16[144,384]{1,0:T(8,128)(2,1)S(1)}, u32[]{:S(2)}, u32[]{:S(2)}) %collective-permute-start.35) | collective-permute-done | bytes 110624 | tf_op jit(solution)/shard_map/ppermute | solution.py:199
  (125 shorter events, 30.7 us)
Async XLA Ops:
  1.5 5.1 %collective-permute-start = (bf16[16,1536]{1,0:T(8,128)(2,1)S(1)}, bf16[16,1536]{1,0:T(8,128)(2,1)S(1)}, u32[]{:S(2)}, u32[]{:S(2)}) collective-permute-start(bf16[16,1536]{1,0:T(8,128)(2,1)S(1)} %fusion.115), channel_id=1, source_target_pairs={{0,1},{1,0},{2,3},{3,2},{4,5},{5,4},{6,7},{7,6},{8,9},{9,8},{10,11... | collective-permute-start | bytes 147464 | tf_op jit(solution)/shard_map/ppermute | solution.py:73
  6.9 16.1 %collective-permute-start.5 = (bf16[2,2,144,384]{3,2,1,0:T(8,128)(2,1)S(1)}, bf16[2,2,144,384]{3,2,1,0:T(8,128)(2,1)S(1)}, u32[]{:S(2)}, u32[]{:S(2)}) collective-permute-start(bf16[2,2,144,384]{3,2,1,0:T(8,128)(2,1)S(1)} %pad_maximum_fusion.11), channel_id=1, source_target_pairs={{0,4},{2,6},{4,0},{6,2},{8,12},{10,14},{12,8},{14,10},{16,20},{18,... | collective-permute-start | bytes 1327112 | tf_op jit(solution)/shard_map/ppermute | solution.py:109
  9.0 8.1 %collective-permute-start.2 = (bf16[144,384]{1,0:T(8,128)(2,1)S(1)}, bf16[144,384]{1,0:T(8,128)(2,1)S(1)}, u32[]{:S(2)}, u32[]{:S(2)}) collective-permute-start(bf16[144,384]{1,0:T(8,128)(2,1)S(1)} %dynamic-slice_bitcast_fusion.5), channel_id=1, source_target_pairs={{0,24},{2,26},{4,28},{6,30},{8,0},{10,2},{12,4},{14,6},{16,8},{18,... | collective-permute-start | bytes 331784 | tf_op jit(solution)/shard_map/ppermute | solution.py:85
  12.7 10.3 %collective-permute-start.3 = (bf16[144,384]{1,0:T(8,128)(2,1)S(1)}, bf16[144,384]{1,0:T(8,128)(2,1)S(1)}, u32[]{:S(2)}, u32[]{:S(2)}) collective-permute-start(bf16[144,384]{1,0:T(8,128)(2,1)S(1)} %dynamic-slice_bitcast_fusion.5), channel_id=1, source_target_pairs={{0,16},{2,18},{4,20},{6,22},{8,24},{10,26},{12,28},{14,30},{16,0},... | collective-permute-start | bytes 331784 | tf_op jit(solution)/shard_map/ppermute | solution.py:85
  12.7 10.3 %collective-permute-start.4 = (bf16[144,384]{1,0:T(8,128)(2,1)S(1)}, bf16[144,384]{1,0:T(8,128)(2,1)S(1)}, u32[]{:S(2)}, u32[]{:S(2)}) collective-permute-start(bf16[144,384]{1,0:T(8,128)(2,1)S(1)} %dynamic-slice_bitcast_fusion.5), channel_id=1, source_target_pairs={{0,8},{2,10},{4,12},{6,14},{8,16},{10,18},{12,20},{14,22},{16,24},... | collective-permute-start | bytes 331784 | tf_op jit(solution)/shard_map/ppermute | solution.py:85
  14.3 15.4 %collective-permute-start.10 = (bf16[144,384]{1,0:T(8,128)(2,1)}, bf16[144,384]{1,0:T(8,128)(2,1)S(1)}, u32[]{:S(2)}, u32[]{:S(2)}) collective-permute-start(bf16[144,384]{1,0:T(8,128)(2,1)} %dynamic-slice_bitcast_fusion.4), channel_id=1, source_target_pairs={{0,24},{2,26},{4,28},{6,30},{8,0},{10,2},{12,4},{14,6},{16,8},{18,... | collective-permute-start | bytes 331784 | tf_op jit(solution)/shard_map/ppermute | solution.py:85
  23.0 13.5 %collective-permute-start.9 = (bf16[3,144,384]{2,1,0:T(8,128)(2,1)S(1)}, bf16[3,144,384]{2,1,0:T(8,128)(2,1)S(1)}, u32[]{:S(2)}, u32[]{:S(2)}) collective-permute-start(bf16[3,144,384]{2,1,0:T(8,128)(2,1)S(1)} %pad_maximum_fusion.12), channel_id=1, source_target_pairs={{4,1},{5,0},{6,3},{7,2},{0,5},{1,4},{2,7},{3,6},{12,9},{13,8},{14,... | collective-permute-start | bytes 995336 | tf_op jit(solution)/shard_map/ppermute | solution.py:93
  24.3 13.4 %collective-permute-start.7 = (bf16[3,144,384]{2,1,0:T(8,128)(2,1)S(1)}, bf16[3,144,384]{2,1,0:T(8,128)(2,1)}, u32[]{:S(2)}, u32[]{:S(2)}) collective-permute-start(bf16[3,144,384]{2,1,0:T(8,128)(2,1)S(1)} %pad_maximum_fusion.12), channel_id=1, source_target_pairs={{0,4},{2,6},{4,0},{6,2},{8,12},{10,14},{12,8},{14,10},{16,20},{18,... | collective-permute-start | bytes 995336 | tf_op jit(solution)/shard_map/ppermute | solution.py:90
  25.8 13.2 %collective-permute-start.8 = (bf16[3,144,384]{2,1,0:T(8,128)(2,1)S(1)}, bf16[3,144,384]{2,1,0:T(8,128)(2,1)}, u32[]{:S(2)}, u32[]{:S(2)}) collective-permute-start(bf16[3,144,384]{2,1,0:T(8,128)(2,1)S(1)} %pad_maximum_fusion.12), channel_id=1, source_target_pairs={{0,1},{1,0},{2,3},{3,2},{4,5},{5,4},{6,7},{7,6},{8,9},{9,8},{10,11... | collective-permute-start | bytes 995336 | tf_op jit(solution)/shard_map/ppermute | solution.py:90
  26.6 8.5 %collective-permute-start.11 = (bf16[144,384]{1,0:T(8,128)(2,1)}, bf16[144,384]{1,0:T(8,128)(2,1)S(1)}, u32[]{:S(2)}, u32[]{:S(2)}) collective-permute-start(bf16[144,384]{1,0:T(8,128)(2,1)} %dynamic-slice_bitcast_fusion.4), channel_id=1, source_target_pairs={{0,16},{2,18},{4,20},{6,22},{8,24},{10,26},{12,28},{14,30},{16,0},... | collective-permute-start | bytes 331784 | tf_op jit(solution)/shard_map/ppermute | solution.py:85
  29.7 6.8 %collective-permute-start.12 = (bf16[144,384]{1,0:T(8,128)(2,1)}, bf16[144,384]{1,0:T(8,128)(2,1)S(1)}, u32[]{:S(2)}, u32[]{:S(2)}) collective-permute-start(bf16[144,384]{1,0:T(8,128)(2,1)} %dynamic-slice_bitcast_fusion.4), channel_id=1, source_target_pairs={{0,8},{2,10},{4,12},{6,14},{8,16},{10,18},{12,20},{14,22},{16,24},... | collective-permute-start | bytes 331784 | tf_op jit(solution)/shard_map/ppermute | solution.py:85
  39.0 10.7 %collective-permute-start.15 = (bf16[3,144,384]{2,1,0:T(8,128)(2,1)S(1)}, bf16[3,144,384]{2,1,0:T(8,128)(2,1)S(1)}, u32[]{:S(2)}, u32[]{:S(2)}) collective-permute-start(bf16[3,144,384]{2,1,0:T(8,128)(2,1)S(1)} %pad_maximum_fusion.13), channel_id=1, source_target_pairs={{0,4},{2,6},{4,0},{6,2},{8,12},{10,14},{12,8},{14,10},{16,20},{18,... | collective-permute-start | bytes 995336 | tf_op jit(solution)/shard_map/ppermute | solution.py:90
  39.5 15.1 %collective-permute-start.16 = (bf16[3,144,384]{2,1,0:T(8,128)(2,1)S(1)}, bf16[3,144,384]{2,1,0:T(8,128)(2,1)S(1)}, u32[]{:S(2)}, u32[]{:S(2)}) collective-permute-start(bf16[3,144,384]{2,1,0:T(8,128)(2,1)S(1)} %pad_maximum_fusion.13), channel_id=1, source_target_pairs={{4,1},{5,0},{6,3},{7,2},{0,5},{1,4},{2,7},{3,6},{12,9},{13,8},{14,... | collective-permute-start | bytes 995336 | tf_op jit(solution)/shard_map/ppermute | solution.py:93
  41.2 22.5 %collective-permute-start.6 = (bf16[544,1536]{1,0:T(8,128)(2,1)S(1)}, bf16[544,1536]{1,0:T(8,128)(2,1)S(1)}, u32[]{:S(2)}, u32[]{:S(2)}) collective-permute-start(bf16[544,1536]{1,0:T(8,128)(2,1)S(1)} %pad_maximum_fusion.1), channel_id=1, source_target_pairs={{0,2},{2,0},{4,6},{6,4},{8,10},{10,8},{12,14},{14,12},{16,18},{18,... | collective-permute-start | bytes 5013512 | tf_op jit(solution)/shard_map/ppermute | solution.py:115
  41.3 17.4 %collective-permute-start.14 = (bf16[3,144,384]{2,1,0:T(8,128)(2,1)S(1)}, bf16[3,144,384]{2,1,0:T(8,128)(2,1)S(1)}, u32[]{:S(2)}, u32[]{:S(2)}) collective-permute-start(bf16[3,144,384]{2,1,0:T(8,128)(2,1)S(1)} %pad_maximum_fusion.13), channel_id=1, source_target_pairs={{0,1},{1,0},{2,3},{3,2},{4,5},{5,4},{6,7},{7,6},{8,9},{9,8},{10,11... | collective-permute-start | bytes 995336 | tf_op jit(solution)/shard_map/ppermute | solution.py:90
  60.2 5.1 %collective-permute-start.17 = (bf16[2304,384]{1,0:T(8,128)(2,1)S(1)}, bf16[2304,384]{1,0:T(8,128)(2,1)S(1)}, u32[]{:S(2)}, u32[]{:S(2)}) collective-permute-start(bf16[2304,384]{1,0:T(8,128)(2,1)S(1)} %bitcast.203), channel_id=1, source_target_pairs={{0,2},{2,0},{4,6},{6,4},{8,10},{10,8},{12,14},{14,12},{16,18},{18,... | collective-permute-start | bytes 5308424 | tf_op jit(solution)/shard_map/ppermute | solution.py:148
  63.1 29.8 %collective-permute-start.30 = (bf16[2304,384]{1,0:T(8,128)(2,1)S(1)}, bf16[2304,384]{1,0:T(8,128)(2,1)S(1)}, u32[]{:S(2)}, u32[]{:S(2)}) collective-permute-start(bf16[2304,384]{1,0:T(8,128)(2,1)S(1)} %bitcast.198), channel_id=1, source_target_pairs={{0,2},{2,0},{4,6},{6,4},{8,10},{10,8},{12,14},{14,12},{16,18},{18,... | collective-permute-start | bytes 5308424 | tf_op jit(solution)/shard_map/ppermute | solution.py:142
  72.0 6.8 %collective-permute-start.13 = (bf16[2,528,384]{2,1,0:T(8,128)(2,1)S(1)}, bf16[2,528,384]{2,1,0:T(8,128)(2,1)S(1)}, u32[]{:S(2)}, u32[]{:S(2)}) collective-permute-start(bf16[2,528,384]{2,1,0:T(8,128)(2,1)S(1)} %get-tuple-element.146), channel_id=1, source_target_pairs={{0,2},{2,0},{4,6},{6,4},{8,10},{10,8},{12,14},{14,12},{16,18},{18,... | collective-permute-start | bytes 2433032 | tf_op jit(solution)/shard_map/ppermute | solution.py:149
  76.7 12.6 %collective-permute-start.19 = (bf16[2,2,144,384]{3,2,0,1:T(8,128)(2,1)S(1)}, bf16[2,2,144,384]{3,2,0,1:T(8,128)(2,1)S(1)}, u32[]{:S(2)}, u32[]{:S(2)}) collective-permute-start(bf16[2,2,144,384]{3,2,0,1:T(8,128)(2,1)S(1)} %bitcast.228), channel_id=1, source_target_pairs={{0,4},{2,6},{4,0},{6,2},{8,12},{10,14},{12,8},{14,10},{16,20},{18,... | collective-permute-start | bytes 1327112 | tf_op jit(solution)/shard_map/ppermute | solution.py:196
  77.3 12.3 %collective-permute-start.20 = (bf16[2,2,144,384]{3,2,0,1:T(8,128)(2,1)S(1)}, bf16[2,2,144,384]{3,2,0,1:T(8,128)(2,1)S(1)}, u32[]{:S(2)}, u32[]{:S(2)}) collective-permute-start(bf16[2,2,144,384]{3,2,0,1:T(8,128)(2,1)S(1)} %bitcast.230), channel_id=1, source_target_pairs={{0,1},{1,0},{2,3},{3,2},{4,5},{5,4},{6,7},{7,6},{8,9},{9,8},{10,11... | collective-permute-start | bytes 1327112 | tf_op jit(solution)/shard_map/ppermute | solution.py:199
  89.9 18.0 %collective-permute-start.23 = (bf16[2,2,144,384]{3,2,0,1:T(8,128)(2,1)S(1)}, bf16[2,2,144,384]{3,2,0,1:T(8,128)(2,1)S(1)}, u32[]{:S(2)}, u32[]{:S(2)}) collective-permute-start(bf16[2,2,144,384]{3,2,0,1:T(8,128)(2,1)S(1)} %bitcast.227), channel_id=1, source_target_pairs={{0,4},{2,6},{4,0},{6,2},{8,12},{10,14},{12,8},{14,10},{16,20},{18,... | collective-permute-start | bytes 1327112 | tf_op jit(solution)/shard_map/ppermute | solution.py:196
  91.5 16.4 %collective-permute-start.24 = (bf16[2,2,144,384]{3,2,0,1:T(8,128)(2,1)S(1)}, bf16[2,2,144,384]{3,2,0,1:T(8,128)(2,1)S(1)}, u32[]{:S(2)}, u32[]{:S(2)}) collective-permute-start(bf16[2,2,144,384]{3,2,0,1:T(8,128)(2,1)S(1)} %bitcast.229), channel_id=1, source_target_pairs={{0,1},{1,0},{2,3},{3,2},{4,5},{5,4},{6,7},{7,6},{8,9},{9,8},{10,11... | collective-permute-start | bytes 1327112 | tf_op jit(solution)/shard_map/ppermute | solution.py:199
  93.4 14.5 %collective-permute-start.21 = (bf16[2,144,384]{2,1,0:T(8,128)(2,1)S(1)}, bf16[2,144,384]{2,1,0:T(8,128)(2,1)S(1)}, u32[]{:S(2)}, u32[]{:S(2)}) collective-permute-start(bf16[2,144,384]{2,1,0:T(8,128)(2,1)S(1)} %dynamic-slice_bitcast_fusion.3), channel_id=1, source_target_pairs={{0,1},{1,0},{2,3},{3,2},{4,5},{5,4},{6,7},{7,6},{8,9},{9,8},{10,11... | collective-permute-start | bytes 663560 | tf_op jit(solution)/shard_map/ppermute | solution.py:199
  94.1 13.8 %collective-permute-start.22 = (bf16[2,144,384]{2,1,0:T(8,128)(2,1)S(1)}, bf16[2,144,384]{2,1,0:T(8,128)(2,1)S(1)}, u32[]{:S(2)}, u32[]{:S(2)}) collective-permute-start(bf16[2,144,384]{2,1,0:T(8,128)(2,1)S(1)} %dynamic-slice_bitcast_fusion.2), channel_id=1, source_target_pairs={{0,4},{2,6},{4,0},{6,2},{8,12},{10,14},{12,8},{14,10},{16,20},{18,... | collective-permute-start | bytes 663560 | tf_op jit(solution)/shard_map/ppermute | solution.py:196
  108.6 15.1 %collective-permute-start.25 = (bf16[2,144,384]{2,1,0:T(8,128)(2,1)S(1)}, bf16[2,144,384]{2,1,0:T(8,128)(2,1)S(1)}, u32[]{:S(2)}, u32[]{:S(2)}) collective-permute-start(bf16[2,144,384]{2,1,0:T(8,128)(2,1)S(1)} %dynamic-slice_bitcast_fusion.1), channel_id=1, source_target_pairs={{0,1},{1,0},{2,3},{3,2},{4,5},{5,4},{6,7},{7,6},{8,9},{9,8},{10,11... | collective-permute-start | bytes 663560 | tf_op jit(solution)/shard_map/ppermute | solution.py:199
  109.5 14.2 %collective-permute-start.26 = (bf16[2,144,384]{2,1,0:T(8,128)(2,1)S(1)}, bf16[2,144,384]{2,1,0:T(8,128)(2,1)S(1)}, u32[]{:S(2)}, u32[]{:S(2)}) collective-permute-start(bf16[2,144,384]{2,1,0:T(8,128)(2,1)S(1)} %dynamic-slice_bitcast_fusion), channel_id=1, source_target_pairs={{0,4},{2,6},{4,0},{6,2},{8,12},{10,14},{12,8},{14,10},{16,20},{18,... | collective-permute-start | bytes 663560 | tf_op jit(solution)/shard_map/ppermute | solution.py:196
  110.9 7.4 %collective-permute-start.27 = (bf16[144,384]{1,0:T(8,128)(2,1)S(1)}, bf16[144,384]{1,0:T(8,128)(2,1)S(1)}, u32[]{:S(2)}, u32[]{:S(2)}) collective-permute-start(bf16[144,384]{1,0:T(8,128)(2,1)S(1)} %get-tuple-element.92), channel_id=1, source_target_pairs={{0,24},{2,26},{4,28},{6,30},{8,0},{10,2},{12,4},{14,6},{16,8},{18,... | collective-permute-start | bytes 331784 | tf_op jit(solution)/shard_map/ppermute | solution.py:202
  111.0 12.7 %collective-permute-start.28 = (bf16[144,384]{1,0:T(8,128)(2,1)S(1)}, bf16[144,384]{1,0:T(8,128)(2,1)S(1)}, u32[]{:S(2)}, u32[]{:S(2)}) collective-permute-start(bf16[144,384]{1,0:T(8,128)(2,1)S(1)} %get-tuple-element.93), channel_id=1, source_target_pairs={{0,16},{2,18},{4,20},{6,22},{8,24},{10,26},{12,28},{14,30},{16,0},... | collective-permute-start | bytes 331784 | tf_op jit(solution)/shard_map/ppermute | solution.py:202
  115.5 8.2 %collective-permute-start.29 = (bf16[144,384]{1,0:T(8,128)(2,1)S(1)}, bf16[144,384]{1,0:T(8,128)(2,1)S(1)}, u32[]{:S(2)}, u32[]{:S(2)}) collective-permute-start(bf16[144,384]{1,0:T(8,128)(2,1)S(1)} %get-tuple-element.94), channel_id=1, source_target_pairs={{0,8},{2,10},{4,12},{6,14},{8,16},{10,18},{12,20},{14,22},{16,24},... | collective-permute-start | bytes 331784 | tf_op jit(solution)/shard_map/ppermute | solution.py:202
  124.1 7.0 %collective-permute-start.34 = (bf16[144,384]{1,0:T(8,128)(2,1)S(1)}, bf16[144,384]{1,0:T(8,128)(2,1)S(1)}, u32[]{:S(2)}, u32[]{:S(2)}) collective-permute-start(bf16[144,384]{1,0:T(8,128)(2,1)S(1)} %get-tuple-element.105), channel_id=1, source_target_pairs={{0,8},{2,10},{4,12},{6,14},{8,16},{10,18},{12,20},{14,22},{16,24},... | collective-permute-start | bytes 331784 | tf_op jit(solution)/shard_map/ppermute | solution.py:202
  124.2 8.1 %collective-permute-start.33 = (bf16[144,384]{1,0:T(8,128)(2,1)S(1)}, bf16[144,384]{1,0:T(8,128)(2,1)S(1)}, u32[]{:S(2)}, u32[]{:S(2)}) collective-permute-start(bf16[144,384]{1,0:T(8,128)(2,1)S(1)} %get-tuple-element.104), channel_id=1, source_target_pairs={{0,16},{2,18},{4,20},{6,22},{8,24},{10,26},{12,28},{14,30},{16,0},... | collective-permute-start | bytes 331784 | tf_op jit(solution)/shard_map/ppermute | solution.py:202
  124.8 7.5 %collective-permute-start.32 = (bf16[144,384]{1,0:T(8,128)(2,1)S(1)}, bf16[144,384]{1,0:T(8,128)(2,1)S(1)}, u32[]{:S(2)}, u32[]{:S(2)}) collective-permute-start(bf16[144,384]{1,0:T(8,128)(2,1)S(1)} %get-tuple-element.103), channel_id=1, source_target_pairs={{0,24},{2,26},{4,28},{6,30},{8,0},{10,2},{12,4},{14,6},{16,8},{18,... | collective-permute-start | bytes 331784 | tf_op jit(solution)/shard_map/ppermute | solution.py:202
  (9 other events, 92.1 us)

commit v4 on v3

--- a/solution.py
+++ b/solution.py
@@ -44,7 +44,6 @@
     core_pairs = [(i, i ^ 1) for i in range(parts)]
     x_pairs = [(i, i ^ 2) for i in range(parts)]
     y_pairs = [(i, i ^ 1) for i in range(seqs)]
-    xy_pairs = [((i ^ 2) * seqs + k, i * seqs + (k ^ 1)) for i in range(parts) for k in range(seqs)]
 
     def turn(step):
         return [(i, (i - 4 * step) % parts) for i in range(parts)]
@@ -68,6 +67,7 @@
     )
 
     joined = jnp.concatenate([features[0], cotangent[0]], axis=1)
+    joined, pair = together(joined, pair)
     if seqs == 2:
         rim = jnp.where(h == 0, joined[rows - HALO :], joined[:HALO])
         rim = lax.ppermute(rim, "seq", y_pairs)
@@ -79,18 +79,17 @@
         low = lax.ppermute(joined[rows - HALO :], "seq", onward)
         high = lax.ppermute(joined[:HALO], "seq", back)
 
-    def along_z(which, *others):
-        piece = after(lax.dynamic_index_in_dim(pair[which], h, 0, keepdims=False), *others)
-        return jnp.stack(
-            together(*(lax.ppermute(piece, "dp", turn(step)) for step in range(1, depth)))
-        )
-
-    def across(turned, *others):
-        given = after(turned, *others)
-        return lax.ppermute(given, "dp", x_pairs), lax.ppermute(given, "seq", y_pairs)
-
-    def corner(turned, *others):
-        return lax.ppermute(after(turned, *others), ("dp", "seq"), xy_pairs)
+    def by_x(array):
+        return lax.ppermute(array, "dp", x_pairs)
+
+    def by_y(array):
+        return lax.ppermute(array, "seq", y_pairs)
+
+    def by_z(outs):
+        return tuple(lax.ppermute(out, "dp", turn(step)) for step, out in enumerate(outs, 1))
+
+    def along_z(piece):
+        return jnp.stack(together(*by_z([piece] * (depth - 1))))
 
     def assemble(own, across, turned, from_x, from_y, from_xy):
         def on(flag, here, there, axis):
@@ -106,20 +105,21 @@
         lines = lax.dynamic_slice_in_dim(lines, (depth - me_z) % depth, depth, axis=0)
         return lines.reshape(parts * block, half)
 
-    x_pair = lax.ppermute(after(pair, low, high), "dp", x_pairs)
-    first_turned, x_pair = together(along_z(0, low, high), x_pair)
-    first_across = across(first_turned)
-    first_corner = corner(first_turned)
-
-    extended = after(jnp.concatenate([low, joined, high], axis=0), first_turned)
+    first_piece, second_piece = (take(pair[which], h, 0) for which in range(2))
+    first_turned, x_pair = together(along_z(first_piece), by_x(pair))
+    low, high, second_piece = together(low, high, second_piece)
+    second_turned = along_z(second_piece)
+    first_x, first_y = by_x(first_turned), by_y(first_turned)
+    first_x, first_y, second_turned = together(first_x, first_y, second_turned)
+    second_x, second_y = by_x(second_turned), by_y(second_turned)
+    first_pieces = pair[0], x_pair[0], first_turned, first_x, first_y, by_y(first_x)
+    second_pieces = pair[1], x_pair[1], second_turned, second_x, second_y, by_x(second_y)
+
+    extended = jnp.concatenate([low, joined, high], axis=0)
     partner = lax.ppermute(extended, "dp", core_pairs)
     pairs = jnp.stack([extended, partner])
     features_two, cot_two = pairs[..., :channels], pairs[..., channels:]
     act_first = gelu_value(features_two.astype(F32)).astype(BF16)
-    second_turned = along_z(1)
-    second_across = across(second_turned, first_corner, *first_across)
-    second_corner = corner(second_turned, first_corner, *first_across)
-    second_pieces = pair[1], x_pair[1], second_turned, *second_across, second_corner
     wide = rows + 2 * EDGE
 
     def shifted(array, offset, count):
@@ -137,8 +137,7 @@
     slope_first = gelu_slope(features[0].astype(F32))
 
     first_base = shifted(half_of(features_two, core, 2), HALO - EDGE, wide)
-    first_pieces = pair[0], x_pair[0], first_turned, *first_across, first_corner
-    first_mine = assemble(*together(*first_pieces, second_turned)[:-1])
+    first_mine = assemble(*first_pieces)
     first_theirs = lax.ppermute(first_mine, "dp", core_pairs)
     hidden = (
         first_base.astype(F32) + jnp.dot(stack_first, first_mine, preferred_element_type=F32)
@@ -191,15 +190,6 @@
         for part in came:
             total = total + part.astype(F32)
         return total
-
-    def by_x(array):
-        return lax.ppermute(array, "dp", x_pairs)
-
-    def by_y(array):
-        return lax.ppermute(array, "seq", y_pairs)
-
-    def by_z(outs):
-        return tuple(lax.ppermute(out, "dp", turn(step)) for step, out in enumerate(outs, 1))
 
     def across_y(total):
         if seqs > 2:

time: 140 us -> 133 us (0.950)
  waiting for transfers between devices: 58.9 us -> 54.5 us
  starting transfers between devices: 43.6 us -> 41.1 us
    ppermute x13 -> x0, waiting for transfers between devices: 30.7 us -> none  [the longest x6 12.6 us: along_z(): lax.ppermute(piece, 'dp', turn(step))]
    ppermute x13 -> x0, starting transfers between devices: 19.8 us -> none  [the longest x6 10.6 us: along_z(): lax.ppermute(piece, 'dp', turn(step))]
    ppermute x6 -> x12, starting transfers between devices: 10.4 us -> 21.6 us  [by_z(): lax.ppermute(out, 'dp', turn(step))]
    ppermute x4 -> x8, waiting for transfers between devices: 1.78 us -> 13 us  [by_x(): return lax.ppermute(array, 'dp', x_pairs)]
    ppermute x6 -> x12, waiting for transfers between devices: 6.57 us -> 14.1 us  [by_z(): lax.ppermute(out, 'dp', turn(step))]
    ppermute x6 -> x9, waiting for transfers between devices: 17.4 us -> 24.4 us  [by_y(): return lax.ppermute(array, 'seq', y_pairs)]
    ppermute x4 -> x8, starting transfers between devices: 3.29 us -> 7.44 us  [by_x(): return lax.ppermute(array, 'dp', x_pairs)]
    ppermute x6 -> x9, starting transfers between devices: 6.12 us -> 8.94 us  [by_y(): return lax.ppermute(array, 'seq', y_pairs)]
  transfers between devices with their start and end apart: 37 -> 37, of which waited for: 17 -> 18; matrix products, arithmetic and copies ran while one was open for 24% -> 25% of each run, Pallas kernels for 0% -> 0%
where the time goes in v4:
time: 133 us
  waiting for transfers between devices  54.5 us (41%)
  starting transfers between devices  41.1 us (31%)
  matrix products  21.8 us (16%)
  other arithmetic  11.2 us (8%)
  local copies, waits for them, and re-layouts  3.09 us (2%)
    ppermute x9, waiting for transfers between devices, by_y(): return lax.ppermute(array, 'seq', y_pairs)  24.4 us
    ppermute x12, starting transfers between devices, by_z(): lax.ppermute(out, 'dp', turn(step))  21.6 us
    ppermute x12, waiting for transfers between devices, by_z(): lax.ppermute(out, 'dp', turn(step))  14.1 us
    ppermute x8, waiting for transfers between devices, by_x(): return lax.ppermute(array, 'dp', x_pairs)  13 us
    ppermute x9, starting transfers between devices, by_y(): return lax.ppermute(array, 'seq', y_pairs)  8.94 us
    dot_general x2, matrix products, gradient(): lax.dot_general(stacked.reshape(2 * rows, 3 * channels), upstream.reshape...  8.26 us
    ppermute x8, starting transfers between devices, by_x(): return lax.ppermute(array, 'dp', x_pairs)  7.44 us
    dot_general x1, matrix products, shards(): jnp.dot(stack_first, first_mine, preferred_element_type=F32)  4.18 us
  transfers between devices with their start and end apart: 37, of which 18 were waited for; matrix products, arithmetic and copies ran while one was open for 25% of the time, Pallas kernels for 0%

profile of v4, /device:TPU:0, one launch (start us, length us, event | category | flops | bytes accessed | tf_op | source)
XLA Modules:
  0.0 132.9 jit_solution(16798982189779188407)
XLA Ops:
  2.2 1.6 %pad_maximum_fusion.1 = bf16[512,1536]{1,0:T(8,128)(2,1)S(1)} fusion(bf16[512,768]{1,0:T(8,128)(2,1)} %bitcast.220, bf16[512,768]{1,0:T(8,128)(2,1)} %bitcast.221), kind=kLoop, calls=%fused_computation.92 | loop fusion | flops 3145728 | bytes 3145728 | tf_op jit(solution)/shard_map/concatenate | solution.py:69
  4.1 4.8 %collective-permute-start.3 = (bf16[144,384]{1,0:T(8,128)(2,1)S(1)}, bf16[144,384]{1,0:T(8,128)(2,1)S(1)}, u32[]{:S(2)}, u32[]{:S(2)}) collective-permute-start(bf16[144,384]{1,0:T(8,128)(2,1)S(1)} %dynamic-slice_bitcast_fusion.4), channel_id=1, source_target_pairs={{0,24},{2,26},{4,28},{6,30},{8,0},{10,2},{12,4},{14,6},{16,8},{18,... | collective-permute-start | bytes 331784 | tf_op jit(solution)/shard_map/ppermute | solution.py:89
  9.9 1.5 %collective-permute-start.6 = (bf16[2,2,144,384]{3,2,1,0:T(8,128)(2,1)S(1)}, bf16[2,2,144,384]{3,2,1,0:T(8,128)(2,1)S(1)}, u32[]{:S(2)}, u32[]{:S(2)}) collective-permute-start(bf16[2,2,144,384]{3,2,1,0:T(8,128)(2,1)S(1)} %pad_maximum_fusion.11), channel_id=1, source_target_pairs={{0,4},{2,6},{4,0},{6,2},{8,12},{10,14},{12,8},{14,10},{16,20},{18,... | collective-permute-start | bytes 1327112 | tf_op jit(solution)/shard_map/ppermute | solution.py:83
  11.4 1.6 %collective-permute-start.1 = (bf16[16,1536]{1,0:T(8,128)(2,1)S(1)}, bf16[16,1536]{1,0:T(8,128)(2,1)S(1)}, u32[]{:S(2)}, u32[]{:S(2)}) collective-permute-start(bf16[16,1536]{1,0:T(8,128)(2,1)S(1)} %slice_select_fusion), channel_id=1, source_target_pairs={{0,1},{1,0},{2,3},{3,2},{4,5},{5,4},{6,7},{7,6},{8,9},{9,8},{10,11... | collective-permute-start | bytes 147464 | tf_op jit(solution)/shard_map/ppermute | solution.py:73
  13.0 2.6 %collective-permute-done.1 = bf16[16,1536]{1,0:T(8,128)(2,1)S(1)} collective-permute-done((bf16[16,1536]{1,0:T(8,128)(2,1)S(1)}, bf16[16,1536]{1,0:T(8,128)(2,1)S(1)}, u32[]{:S(2)}, u32[]{:S(2)}) %collective-permute-start.1) | collective-permute-done | bytes 49184 | tf_op jit(solution)/shard_map/ppermute | solution.py:73
  15.6 2.9 %collective-permute-start.9 = (bf16[144,384]{1,0:T(8,128)(2,1)S(1)}, bf16[144,384]{1,0:T(8,128)(2,1)S(1)}, u32[]{:S(2)}, u32[]{:S(2)}) collective-permute-start(bf16[144,384]{1,0:T(8,128)(2,1)S(1)} %dynamic-slice_bitcast_fusion.5), channel_id=1, source_target_pairs={{0,24},{2,26},{4,28},{6,30},{8,0},{10,2},{12,4},{14,6},{16,8},{18,... | collective-permute-start | bytes 331784 | tf_op jit(solution)/shard_map/ppermute | solution.py:89
  23.0 1.5 %collective-permute-start.8 = (bf16[3,144,384]{2,1,0:T(8,128)(2,1)S(1)}, bf16[3,144,384]{2,1,0:T(8,128)(2,1)S(1)}, u32[]{:S(2)}, u32[]{:S(2)}) collective-permute-start(bf16[3,144,384]{2,1,0:T(8,128)(2,1)S(1)} %pad_maximum_fusion.12), channel_id=1, source_target_pairs={{0,1},{1,0},{2,3},{3,2},{4,5},{5,4},{6,7},{7,6},{8,9},{9,8},{10,11... | collective-permute-start | bytes 995336 | tf_op jit(solution)/shard_map/ppermute | solution.py:86
  24.5 4.4 %collective-permute-done.10 = bf16[144,384]{1,0:T(8,128)(2,1)S(1)} collective-permute-done((bf16[144,384]{1,0:T(8,128)(2,1)S(1)}, bf16[144,384]{1,0:T(8,128)(2,1)S(1)}, u32[]{:S(2)}, u32[]{:S(2)}) %collective-permute-start.10) | collective-permute-done | bytes 110624 | tf_op jit(solution)/shard_map/ppermute | solution.py:89
  31.3 1.5 %collective-permute-start.14 = (bf16[3,144,384]{2,1,0:T(8,128)(2,1)S(1)}, bf16[3,144,384]{2,1,0:T(8,128)(2,1)S(1)}, u32[]{:S(2)}, u32[]{:S(2)}) collective-permute-start(bf16[3,144,384]{2,1,0:T(8,128)(2,1)S(1)} %pad_maximum_fusion.13), channel_id=1, source_target_pairs={{0,1},{1,0},{2,3},{3,2},{4,5},{5,4},{6,7},{7,6},{8,9},{9,8},{10,11... | collective-permute-start | bytes 995336 | tf_op jit(solution)/shard_map/ppermute | solution.py:86
  33.5 5.3 %collective-permute-done.14 = bf16[3,144,384]{2,1,0:T(8,128)(2,1)S(1)} collective-permute-done((bf16[3,144,384]{2,1,0:T(8,128)(2,1)S(1)}, bf16[3,144,384]{2,1,0:T(8,128)(2,1)S(1)}, u32[]{:S(2)}, u32[]{:S(2)}) %collective-permute-start.14) | collective-permute-done | bytes 331808 | tf_op jit(solution)/shard_map/ppermute | solution.py:86
  40.0 1.6 %collective-permute-start.12 = (bf16[3,144,384]{2,1,0:T(8,128)(2,1)S(1)}, bf16[3,144,384]{2,1,0:T(8,128)(2,1)S(1)}, u32[]{:S(2)}, u32[]{:S(2)}) collective-permute-start(bf16[3,144,384]{2,1,0:T(8,128)(2,1)S(1)} %collective-permute-done.7), channel_id=1, source_target_pairs={{0,1},{1,0},{2,3},{3,2},{4,5},{5,4},{6,7},{7,6},{8,9},{9,8},{10,11... | collective-permute-start | bytes 995336 | tf_op jit(solution)/shard_map/ppermute | solution.py:86
  41.6 2.1 %collective-permute-done.15 = bf16[3,144,384]{2,1,0:T(8,128)(2,1)S(1)} collective-permute-done((bf16[3,144,384]{2,1,0:T(8,128)(2,1)S(1)}, bf16[3,144,384]{2,1,0:T(8,128)(2,1)S(1)}, u32[]{:S(2)}, u32[]{:S(2)}) %collective-permute-start.15) | collective-permute-done | bytes 331808 | tf_op jit(solution)/shard_map/ppermute | solution.py:83
  43.7 6.7 %collective-permute-done.16 = bf16[3,144,384]{2,1,0:T(8,128)(2,1)S(1)} collective-permute-done((bf16[3,144,384]{2,1,0:T(8,128)(2,1)S(1)}, bf16[3,144,384]{2,1,0:T(8,128)(2,1)S(1)}, u32[]{:S(2)}, u32[]{:S(2)}) %collective-permute-start.16) | collective-permute-done | bytes 331808 | tf_op jit(solution)/shard_map/ppermute | solution.py:83
  56.1 2.4 %fusion.34 = f32[2,544,1152]{2,1,0:T(8,128)S(1)} fusion(bf16[1152,384]{1,0:T(8,128)(2,1)S(1)} %bitcast.219, bf16[1152,384]{1,0:T(8,128)(2,1)S(1)} %bitcast.218, bf16[1,544,1536]{2,1,0:T(8,128)(2,1)S(1)} %bitcast.202, bf16[1,544,1536]{2,1,0:T(8,128)(2,1)S(1)} %bitcast.199), kind=kOutput, calls=%fused_computation.60 | convolution fusion | flops 1932066816 | bytes 10125312 | tf_op jit(solution)/shard_map/dot_general | solution.py:212
  58.5 4.2 %fusion.50 = (bf16[2,528,384]{2,1,0:T(8,128)(2,1)S(1)}, bf16[2,528,384]{2,1,0:T(8,128)(2,1)S(1)}, bf16[2,528,384]{2,1,0:T(8,128)(2,1)S(1)}) fusion(f32[2,544,1152]{2,1,0:T(8,128)S(1)} %fusion.34, bf16[2,544,384]{2,1,0:T(8,128)(2,1)S(1)} %fusion.77, pred[528]{0:T(1024)(128)(4,1)S(1)} %fusion.113, bf16[2304,384,1]{1,0,2:T(8,128)(2,1)S(1)} %bitcast.196, ...), kind=kOutput, calls=%fused_computation.78 | convolution fusion | flops 1892487168 | bytes 15557144 | tf_op jit(solution)/shard_map/dot_general | solution.py:143
  62.8 4.1 %fusion.21 = bf16[2304,384]{1,0:T(8,128)(2,1)S(1)} fusion(bf16[2,528,768]{2,1,0:T(8,128)(2,1)S(1)} %get-tuple-element.121, bf16[2,528,768]{2,1,0:T(8,128)(2,1)S(1)} %get-tuple-element.122, bf16[2,528,768]{2,1,0:T(8,128)(2,1)S(1)} %get-tuple-element.120, bf16[2,528,384]{2,1,0:T(8,128)(2,1)S(1)} %get-tuple-element.141), kind=kOutput, calls=%fused_computation.19 | convolution fusion | flops 1827864576 | bytes 7421952 | tf_op jit(solution)/shard_map/dot_general | solution.py:156
  69.2 4.2 %fusion.20 = bf16[2304,384]{1,0:T(8,128)(2,1)S(1)} fusion(bf16[2,544,384]{2,1,0:T(8,128)(2,1)S(1)} %fusion.77, bf16[2,528,384]{2,1,0:T(8,128)(2,1)S(1)} %get-tuple-element.126, bf16[2,528,384]{2,1,0:T(8,128)(2,1)S(1)} %get-tuple-element.125, bf16[2,512,768]{2,1,0:T(8,128)(2,1)S(1)} %get-tuple-element.124, bf16[2,512,768]{2,1,0:T(8,128)(2,1)S(1)} %get-tuple-element.123), kind=kOutput, calls=%fused_computation.18 | convolution fusion | flops 1832583168 | bytes 7323648 | tf_op jit(solution)/shard_map/dot_general | solution.py:156
  73.4 3.1 %add_convert_fusion.1 = bf16[2,512,384]{2,1,0:T(8,128)(2,1)S(1)} fusion(bf16[2304,384,1]{1,0,2:T(8,128)(2,1)S(1)} %bitcast.205, bf16[2,528,384]{2,1,0:T(8,128)(2,1)S(1)} %get-tuple-element.169, bf16[2,528,384]{2,1,0:T(8,128)(2,1)S(1)} %get-tuple-element.126, bf16[2,528,384]{2,1,0:T(8,128)(2,1)S(1)} %get-tuple-element.125, ...), kind=kOutput, calls=%fused_computation.93 | convolution fusion | flops 1831993344 | bytes 8110080 | tf_op jit(solution)/shard_map/dot_general | solution.py:232
  77.2 2.8 %collective-permute-done.19 = bf16[2,2,144,384]{3,2,0,1:T(8,128)(2,1)S(1)} collective-permute-done((bf16[2,2,144,384]{3,2,0,1:T(8,128)(2,1)S(1)}, bf16[2,2,144,384]{3,2,0,1:T(8,128)(2,1)S(1)}, u32[]{:S(2)}, u32[]{:S(2)}) %collective-permute-start.19) | collective-permute-done | bytes 442400 | tf_op jit(solution)/shard_map/ppermute | solution.py:83
  80.4 1.7 %collective-permute-start.23 = (bf16[2,2,144,384]{3,2,0,1:T(8,128)(2,1)S(1)}, bf16[2,2,144,384]{3,2,0,1:T(8,128)(2,1)S(1)}, u32[]{:S(2)}, u32[]{:S(2)}) collective-permute-start(bf16[2,2,144,384]{3,2,0,1:T(8,128)(2,1)S(1)} %bitcast.222), channel_id=1, source_target_pairs={{0,4},{2,6},{4,0},{6,2},{8,12},{10,14},{12,8},{14,10},{16,20},{18,... | collective-permute-start | bytes 1327112 | tf_op jit(solution)/shard_map/ppermute | solution.py:83
  83.2 1.6 %collective-permute-start.21 = (bf16[2,144,384]{2,1,0:T(8,128)(2,1)S(1)}, bf16[2,144,384]{2,1,0:T(8,128)(2,1)S(1)}, u32[]{:S(2)}, u32[]{:S(2)}) collective-permute-start(bf16[2,144,384]{2,1,0:T(8,128)(2,1)S(1)} %dynamic-slice_bitcast_fusion.3), channel_id=1, source_target_pairs={{0,1},{1,0},{2,3},{3,2},{4,5},{5,4},{6,7},{7,6},{8,9},{9,8},{10,11... | collective-permute-start | bytes 663560 | tf_op jit(solution)/shard_map/ppermute | solution.py:86
  85.2 12.8 %collective-permute-done.21 = bf16[2,144,384]{2,1,0:T(8,128)(2,1)S(1)} collective-permute-done((bf16[2,144,384]{2,1,0:T(8,128)(2,1)S(1)}, bf16[2,144,384]{2,1,0:T(8,128)(2,1)S(1)}, u32[]{:S(2)}, u32[]{:S(2)}) %collective-permute-start.21) | collective-permute-done | bytes 221216 | tf_op jit(solution)/shard_map/ppermute | solution.py:86
  101.1 3.6 %collective-permute-start.27 = (bf16[144,384]{1,0:T(8,128)(2,1)S(1)}, bf16[144,384]{1,0:T(8,128)(2,1)S(1)}, u32[]{:S(2)}, u32[]{:S(2)}) collective-permute-start(bf16[144,384]{1,0:T(8,128)(2,1)S(1)} %get-tuple-element.88), channel_id=1, source_target_pairs={{0,24},{2,26},{4,28},{6,30},{8,0},{10,2},{12,4},{14,6},{16,8},{18,... | collective-permute-start | bytes 331784 | tf_op jit(solution)/shard_map/ppermute | solution.py:89
  104.7 1.8 %collective-permute-start.28 = (bf16[144,384]{1,0:T(8,128)(2,1)S(1)}, bf16[144,384]{1,0:T(8,128)(2,1)S(1)}, u32[]{:S(2)}, u32[]{:S(2)}) collective-permute-start(bf16[144,384]{1,0:T(8,128)(2,1)S(1)} %get-tuple-element.89), channel_id=1, source_target_pairs={{0,16},{2,18},{4,20},{6,22},{8,24},{10,26},{12,28},{14,30},{16,0},... | collective-permute-start | bytes 331784 | tf_op jit(solution)/shard_map/ppermute | solution.py:89
  106.6 1.9 %collective-permute-start.29 = (bf16[144,384]{1,0:T(8,128)(2,1)S(1)}, bf16[144,384]{1,0:T(8,128)(2,1)S(1)}, u32[]{:S(2)}, u32[]{:S(2)}) collective-permute-start(bf16[144,384]{1,0:T(8,128)(2,1)S(1)} %get-tuple-element.90), channel_id=1, source_target_pairs={{0,8},{2,10},{4,12},{6,14},{8,16},{10,18},{12,20},{14,22},{16,24},... | collective-permute-start | bytes 331784 | tf_op jit(solution)/shard_map/ppermute | solution.py:89
  109.4 6.0 %collective-permute-done.28 = bf16[144,384]{1,0:T(8,128)(2,1)S(1)} collective-permute-done((bf16[144,384]{1,0:T(8,128)(2,1)S(1)}, bf16[144,384]{1,0:T(8,128)(2,1)S(1)}, u32[]{:S(2)}, u32[]{:S(2)}) %collective-permute-start.28) | collective-permute-done | bytes 110624 | tf_op jit(solution)/shard_map/ppermute | solution.py:89
  115.9 1.5 %collective-permute-start.33 = (bf16[144,384]{1,0:T(8,128)(2,1)S(1)}, bf16[144,384]{1,0:T(8,128)(2,1)S(1)}, u32[]{:S(2)}, u32[]{:S(2)}) collective-permute-start(bf16[144,384]{1,0:T(8,128)(2,1)S(1)} %get-tuple-element.100), channel_id=1, source_target_pairs={{0,16},{2,18},{4,20},{6,22},{8,24},{10,26},{12,28},{14,30},{16,0},... | collective-permute-start | bytes 331784 | tf_op jit(solution)/shard_map/ppermute | solution.py:89
  117.5 2.8 %collective-permute-start.32 = (bf16[144,384]{1,0:T(8,128)(2,1)S(1)}, bf16[144,384]{1,0:T(8,128)(2,1)S(1)}, u32[]{:S(2)}, u32[]{:S(2)}) collective-permute-start(bf16[144,384]{1,0:T(8,128)(2,1)S(1)} %get-tuple-element.99), channel_id=1, source_target_pairs={{0,24},{2,26},{4,28},{6,30},{8,0},{10,2},{12,4},{14,6},{16,8},{18,... | collective-permute-start | bytes 331784 | tf_op jit(solution)/shard_map/ppermute | solution.py:89
  120.3 2.3 %fusion.61 = bf16[512,768]{1,0:T(8,128)(2,1)} fusion(f32[512,768]{1,0:T(8,128)S(1)} %fusion.70, f32[512,768]{1,0:T(8,128)S(1)} %fusion.67, bf16[2304,384]{1,0:T(8,128)(2,1)S(1)} %get-tuple-element.108, bf16[2304,384]{1,0:T(8,128)(2,1)S(1)} %get-tuple-element.109, bf16[528,384]{1,0:T(8,128)(2,1)S(1)} %get-tuple-element.127, ...), kind=kOutput, calls=%fused_computation.94 | convolution fusion | flops 614989824 | bytes 9879552 | tf_op jit(solution)/shard_map/dot_general | solution.py:256
  123.7 1.6 %collective-permute-done.33 = bf16[144,384]{1,0:T(8,128)(2,1)S(1)} collective-permute-done((bf16[144,384]{1,0:T(8,128)(2,1)S(1)}, bf16[144,384]{1,0:T(8,128)(2,1)S(1)}, u32[]{:S(2)}, u32[]{:S(2)}) %collective-permute-start.33) | collective-permute-done | bytes 110624 | tf_op jit(solution)/shard_map/ppermute | solution.py:89
  125.5 1.9 %collective-permute-done.31 = bf16[144,384]{1,0:T(8,128)(2,1)S(1)} collective-permute-done((bf16[144,384]{1,0:T(8,128)(2,1)S(1)}, bf16[144,384]{1,0:T(8,128)(2,1)S(1)}, u32[]{:S(2)}, u32[]{:S(2)}) %collective-permute-start.31) | collective-permute-done | bytes 110624 | tf_op jit(solution)/shard_map/ppermute | solution.py:86
  127.4 2.8 %collective-permute-done.35 = bf16[144,384]{1,0:T(8,128)(2,1)S(1)} collective-permute-done((bf16[144,384]{1,0:T(8,128)(2,1)S(1)}, bf16[144,384]{1,0:T(8,128)(2,1)S(1)}, u32[]{:S(2)}, u32[]{:S(2)}) %collective-permute-start.35) | collective-permute-done | bytes 110624 | tf_op jit(solution)/shard_map/ppermute | solution.py:86
  (126 shorter events, 30.5 us)
Async XLA Ops:
  4.1 14.4 %collective-permute-start.3 = (bf16[144,384]{1,0:T(8,128)(2,1)S(1)}, bf16[144,384]{1,0:T(8,128)(2,1)S(1)}, u32[]{:S(2)}, u32[]{:S(2)}) collective-permute-start(bf16[144,384]{1,0:T(8,128)(2,1)S(1)} %dynamic-slice_bitcast_fusion.4), channel_id=1, source_target_pairs={{0,24},{2,26},{4,28},{6,30},{8,0},{10,2},{12,4},{14,6},{16,8},{18,... | collective-permute-start | bytes 331784 | tf_op jit(solution)/shard_map/ppermute | solution.py:89
  8.9 12.1 %collective-permute-start.4 = (bf16[144,384]{1,0:T(8,128)(2,1)S(1)}, bf16[144,384]{1,0:T(8,128)(2,1)S(1)}, u32[]{:S(2)}, u32[]{:S(2)}) collective-permute-start(bf16[144,384]{1,0:T(8,128)(2,1)S(1)} %dynamic-slice_bitcast_fusion.4), channel_id=1, source_target_pairs={{0,16},{2,18},{4,20},{6,22},{8,24},{10,26},{12,28},{14,30},{16,0},... | collective-permute-start | bytes 331784 | tf_op jit(solution)/shard_map/ppermute | solution.py:89
  8.9 12.1 %collective-permute-start.5 = (bf16[144,384]{1,0:T(8,128)(2,1)S(1)}, bf16[144,384]{1,0:T(8,128)(2,1)S(1)}, u32[]{:S(2)}, u32[]{:S(2)}) collective-permute-start(bf16[144,384]{1,0:T(8,128)(2,1)S(1)} %dynamic-slice_bitcast_fusion.4), channel_id=1, source_target_pairs={{0,8},{2,10},{4,12},{6,14},{8,16},{10,18},{12,20},{14,22},{16,24},... | collective-permute-start | bytes 331784 | tf_op jit(solution)/shard_map/ppermute | solution.py:89
  9.9 11.6 %collective-permute-start.6 = (bf16[2,2,144,384]{3,2,1,0:T(8,128)(2,1)S(1)}, bf16[2,2,144,384]{3,2,1,0:T(8,128)(2,1)S(1)}, u32[]{:S(2)}, u32[]{:S(2)}) collective-permute-start(bf16[2,2,144,384]{3,2,1,0:T(8,128)(2,1)S(1)} %pad_maximum_fusion.11), channel_id=1, source_target_pairs={{0,4},{2,6},{4,0},{6,2},{8,12},{10,14},{12,8},{14,10},{16,20},{18,... | collective-permute-start | bytes 1327112 | tf_op jit(solution)/shard_map/ppermute | solution.py:83
  15.6 8.9 %collective-permute-start.9 = (bf16[144,384]{1,0:T(8,128)(2,1)S(1)}, bf16[144,384]{1,0:T(8,128)(2,1)S(1)}, u32[]{:S(2)}, u32[]{:S(2)}) collective-permute-start(bf16[144,384]{1,0:T(8,128)(2,1)S(1)} %dynamic-slice_bitcast_fusion.5), channel_id=1, source_target_pairs={{0,24},{2,26},{4,28},{6,30},{8,0},{10,2},{12,4},{14,6},{16,8},{18,... | collective-permute-start | bytes 331784 | tf_op jit(solution)/shard_map/ppermute | solution.py:89
  18.5 10.4 %collective-permute-start.10 = (bf16[144,384]{1,0:T(8,128)(2,1)S(1)}, bf16[144,384]{1,0:T(8,128)(2,1)S(1)}, u32[]{:S(2)}, u32[]{:S(2)}) collective-permute-start(bf16[144,384]{1,0:T(8,128)(2,1)S(1)} %dynamic-slice_bitcast_fusion.5), channel_id=1, source_target_pairs={{0,16},{2,18},{4,20},{6,22},{8,24},{10,26},{12,28},{14,30},{16,0},... | collective-permute-start | bytes 331784 | tf_op jit(solution)/shard_map/ppermute | solution.py:89
  21.0 7.9 %collective-permute-start.11 = (bf16[144,384]{1,0:T(8,128)(2,1)S(1)}, bf16[144,384]{1,0:T(8,128)(2,1)S(1)}, u32[]{:S(2)}, u32[]{:S(2)}) collective-permute-start(bf16[144,384]{1,0:T(8,128)(2,1)S(1)} %dynamic-slice_bitcast_fusion.5), channel_id=1, source_target_pairs={{0,8},{2,10},{4,12},{6,14},{8,16},{10,18},{12,20},{14,22},{16,24},... | collective-permute-start | bytes 331784 | tf_op jit(solution)/shard_map/ppermute | solution.py:89
  21.5 8.4 %collective-permute-start.7 = (bf16[3,144,384]{2,1,0:T(8,128)(2,1)S(1)}, bf16[3,144,384]{2,1,0:T(8,128)(2,1)S(1)}, u32[]{:S(2)}, u32[]{:S(2)}) collective-permute-start(bf16[3,144,384]{2,1,0:T(8,128)(2,1)S(1)} %pad_maximum_fusion.12), channel_id=1, source_target_pairs={{0,4},{2,6},{4,0},{6,2},{8,12},{10,14},{12,8},{14,10},{16,20},{18,... | collective-permute-start | bytes 995336 | tf_op jit(solution)/shard_map/ppermute | solution.py:83
  23.0 8.3 %collective-permute-start.8 = (bf16[3,144,384]{2,1,0:T(8,128)(2,1)S(1)}, bf16[3,144,384]{2,1,0:T(8,128)(2,1)S(1)}, u32[]{:S(2)}, u32[]{:S(2)}) collective-permute-start(bf16[3,144,384]{2,1,0:T(8,128)(2,1)S(1)} %pad_maximum_fusion.12), channel_id=1, source_target_pairs={{0,1},{1,0},{2,3},{3,2},{4,5},{5,4},{6,7},{7,6},{8,9},{9,8},{10,11... | collective-permute-start | bytes 995336 | tf_op jit(solution)/shard_map/ppermute | solution.py:86
  31.3 7.4 %collective-permute-start.14 = (bf16[3,144,384]{2,1,0:T(8,128)(2,1)S(1)}, bf16[3,144,384]{2,1,0:T(8,128)(2,1)S(1)}, u32[]{:S(2)}, u32[]{:S(2)}) collective-permute-start(bf16[3,144,384]{2,1,0:T(8,128)(2,1)S(1)} %pad_maximum_fusion.13), channel_id=1, source_target_pairs={{0,1},{1,0},{2,3},{3,2},{4,5},{5,4},{6,7},{7,6},{8,9},{9,8},{10,11... | collective-permute-start | bytes 995336 | tf_op jit(solution)/shard_map/ppermute | solution.py:86
  33.0 21.4 %collective-permute-start.2 = (bf16[544,1536]{1,0:T(8,128)(2,1)S(1)}, bf16[544,1536]{1,0:T(8,128)(2,1)S(1)}, u32[]{:S(2)}, u32[]{:S(2)}) collective-permute-start(bf16[544,1536]{1,0:T(8,128)(2,1)S(1)} %constant_dynamic-update-slice_fusion), channel_id=1, source_target_pairs={{0,2},{2,0},{4,6},{6,4},{8,10},{10,8},{12,14},{14,12},{16,18},{18,... | collective-permute-start | bytes 5013512 | tf_op jit(solution)/shard_map/ppermute | solution.py:119
  33.1 10.7 %collective-permute-start.15 = (bf16[3,144,384]{2,1,0:T(8,128)(2,1)S(1)}, bf16[3,144,384]{2,1,0:T(8,128)(2,1)S(1)}, u32[]{:S(2)}, u32[]{:S(2)}) collective-permute-start(bf16[3,144,384]{2,1,0:T(8,128)(2,1)S(1)} %pad_maximum_fusion.13), channel_id=1, source_target_pairs={{0,4},{2,6},{4,0},{6,2},{8,12},{10,14},{12,8},{14,10},{16,20},{18,... | collective-permute-start | bytes 995336 | tf_op jit(solution)/shard_map/ppermute | solution.py:83
  38.7 11.6 %collective-permute-start.16 = (bf16[3,144,384]{2,1,0:T(8,128)(2,1)S(1)}, bf16[3,144,384]{2,1,0:T(8,128)(2,1)S(1)}, u32[]{:S(2)}, u32[]{:S(2)}) collective-permute-start(bf16[3,144,384]{2,1,0:T(8,128)(2,1)S(1)} %collective-permute-done.14), channel_id=1, source_target_pairs={{0,4},{2,6},{4,0},{6,2},{8,12},{10,14},{12,8},{14,10},{16,20},{18,... | collective-permute-start | bytes 995336 | tf_op jit(solution)/shard_map/ppermute | solution.py:83
  40.0 12.1 %collective-permute-start.12 = (bf16[3,144,384]{2,1,0:T(8,128)(2,1)S(1)}, bf16[3,144,384]{2,1,0:T(8,128)(2,1)S(1)}, u32[]{:S(2)}, u32[]{:S(2)}) collective-permute-start(bf16[3,144,384]{2,1,0:T(8,128)(2,1)S(1)} %collective-permute-done.7), channel_id=1, source_target_pairs={{0,1},{1,0},{2,3},{3,2},{4,5},{5,4},{6,7},{7,6},{8,9},{9,8},{10,11... | collective-permute-start | bytes 995336 | tf_op jit(solution)/shard_map/ppermute | solution.py:86
  53.8 28.9 %collective-permute-start.30 = (bf16[2304,384]{1,0:T(8,128)(2,1)S(1)}, bf16[2304,384]{1,0:T(8,128)(2,1)S(1)}, u32[]{:S(2)}, u32[]{:S(2)}) collective-permute-start(bf16[2304,384]{1,0:T(8,128)(2,1)S(1)} %bitcast.195), channel_id=1, source_target_pairs={{0,2},{2,0},{4,6},{6,4},{8,10},{10,8},{12,14},{14,12},{16,18},{18,... | collective-permute-start | bytes 5308424 | tf_op jit(solution)/shard_map/ppermute | solution.py:141
  62.7 5.7 %collective-permute-start.13 = (bf16[2,528,384]{2,1,0:T(8,128)(2,1)S(1)}, bf16[2,528,384]{2,1,0:T(8,128)(2,1)S(1)}, u32[]{:S(2)}, u32[]{:S(2)}) collective-permute-start(bf16[2,528,384]{2,1,0:T(8,128)(2,1)S(1)} %get-tuple-element.142), channel_id=1, source_target_pairs={{0,2},{2,0},{4,6},{6,4},{8,10},{10,8},{12,14},{14,12},{16,18},{18,... | collective-permute-start | bytes 2433032 | tf_op jit(solution)/shard_map/ppermute | solution.py:148
  67.4 12.6 %collective-permute-start.19 = (bf16[2,2,144,384]{3,2,0,1:T(8,128)(2,1)S(1)}, bf16[2,2,144,384]{3,2,0,1:T(8,128)(2,1)S(1)}, u32[]{:S(2)}, u32[]{:S(2)}) collective-permute-start(bf16[2,2,144,384]{3,2,0,1:T(8,128)(2,1)S(1)} %bitcast.223), channel_id=1, source_target_pairs={{0,4},{2,6},{4,0},{6,2},{8,12},{10,14},{12,8},{14,10},{16,20},{18,... | collective-permute-start | bytes 1327112 | tf_op jit(solution)/shard_map/ppermute | solution.py:83
  67.8 12.3 %collective-permute-start.20 = (bf16[2,2,144,384]{3,2,0,1:T(8,128)(2,1)S(1)}, bf16[2,2,144,384]{3,2,0,1:T(8,128)(2,1)S(1)}, u32[]{:S(2)}, u32[]{:S(2)}) collective-permute-start(bf16[2,2,144,384]{3,2,0,1:T(8,128)(2,1)S(1)} %bitcast.225), channel_id=1, source_target_pairs={{0,1},{1,0},{2,3},{3,2},{4,5},{5,4},{6,7},{7,6},{8,9},{9,8},{10,11... | collective-permute-start | bytes 1327112 | tf_op jit(solution)/shard_map/ppermute | solution.py:86
  80.4 17.6 %collective-permute-start.23 = (bf16[2,2,144,384]{3,2,0,1:T(8,128)(2,1)S(1)}, bf16[2,2,144,384]{3,2,0,1:T(8,128)(2,1)S(1)}, u32[]{:S(2)}, u32[]{:S(2)}) collective-permute-start(bf16[2,2,144,384]{3,2,0,1:T(8,128)(2,1)S(1)} %bitcast.222), channel_id=1, source_target_pairs={{0,4},{2,6},{4,0},{6,2},{8,12},{10,14},{12,8},{14,10},{16,20},{18,... | collective-permute-start | bytes 1327112 | tf_op jit(solution)/shard_map/ppermute | solution.py:83
  82.2 15.9 %collective-permute-start.24 = (bf16[2,2,144,384]{3,2,0,1:T(8,128)(2,1)S(1)}, bf16[2,2,144,384]{3,2,0,1:T(8,128)(2,1)S(1)}, u32[]{:S(2)}, u32[]{:S(2)}) collective-permute-start(bf16[2,2,144,384]{3,2,0,1:T(8,128)(2,1)S(1)} %bitcast.224), channel_id=1, source_target_pairs={{0,1},{1,0},{2,3},{3,2},{4,5},{5,4},{6,7},{7,6},{8,9},{9,8},{10,11... | collective-permute-start | bytes 1327112 | tf_op jit(solution)/shard_map/ppermute | solution.py:86
  83.2 14.9 %collective-permute-start.21 = (bf16[2,144,384]{2,1,0:T(8,128)(2,1)S(1)}, bf16[2,144,384]{2,1,0:T(8,128)(2,1)S(1)}, u32[]{:S(2)}, u32[]{:S(2)}) collective-permute-start(bf16[2,144,384]{2,1,0:T(8,128)(2,1)S(1)} %dynamic-slice_bitcast_fusion.3), channel_id=1, source_target_pairs={{0,1},{1,0},{2,3},{3,2},{4,5},{5,4},{6,7},{7,6},{8,9},{9,8},{10,11... | collective-permute-start | bytes 663560 | tf_op jit(solution)/shard_map/ppermute | solution.py:86
  84.8 13.3 %collective-permute-start.22 = (bf16[2,144,384]{2,1,0:T(8,128)(2,1)S(1)}, bf16[2,144,384]{2,1,0:T(8,128)(2,1)S(1)}, u32[]{:S(2)}, u32[]{:S(2)}) collective-permute-start(bf16[2,144,384]{2,1,0:T(8,128)(2,1)S(1)} %dynamic-slice_bitcast_fusion.2), channel_id=1, source_target_pairs={{0,4},{2,6},{4,0},{6,2},{8,12},{10,14},{12,8},{14,10},{16,20},{18,... | collective-permute-start | bytes 663560 | tf_op jit(solution)/shard_map/ppermute | solution.py:83
  98.7 16.7 %collective-permute-start.25 = (bf16[2,144,384]{2,1,0:T(8,128)(2,1)S(1)}, bf16[2,144,384]{2,1,0:T(8,128)(2,1)S(1)}, u32[]{:S(2)}, u32[]{:S(2)}) collective-permute-start(bf16[2,144,384]{2,1,0:T(8,128)(2,1)S(1)} %dynamic-slice_bitcast_fusion.1), channel_id=1, source_target_pairs={{0,1},{1,0},{2,3},{3,2},{4,5},{5,4},{6,7},{7,6},{8,9},{9,8},{10,11... | collective-permute-start | bytes 663560 | tf_op jit(solution)/shard_map/ppermute | solution.py:86
  99.9 15.5 %collective-permute-start.26 = (bf16[2,144,384]{2,1,0:T(8,128)(2,1)S(1)}, bf16[2,144,384]{2,1,0:T(8,128)(2,1)S(1)}, u32[]{:S(2)}, u32[]{:S(2)}) collective-permute-start(bf16[2,144,384]{2,1,0:T(8,128)(2,1)S(1)} %dynamic-slice_bitcast_fusion), channel_id=1, source_target_pairs={{0,4},{2,6},{4,0},{6,2},{8,12},{10,14},{12,8},{14,10},{16,20},{18,... | collective-permute-start | bytes 663560 | tf_op jit(solution)/shard_map/ppermute | solution.py:83
  101.1 8.2 %collective-permute-start.27 = (bf16[144,384]{1,0:T(8,128)(2,1)S(1)}, bf16[144,384]{1,0:T(8,128)(2,1)S(1)}, u32[]{:S(2)}, u32[]{:S(2)}) collective-permute-start(bf16[144,384]{1,0:T(8,128)(2,1)S(1)} %get-tuple-element.88), channel_id=1, source_target_pairs={{0,24},{2,26},{4,28},{6,30},{8,0},{10,2},{12,4},{14,6},{16,8},{18,... | collective-permute-start | bytes 331784 | tf_op jit(solution)/shard_map/ppermute | solution.py:89
  104.7 10.7 %collective-permute-start.28 = (bf16[144,384]{1,0:T(8,128)(2,1)S(1)}, bf16[144,384]{1,0:T(8,128)(2,1)S(1)}, u32[]{:S(2)}, u32[]{:S(2)}) collective-permute-start(bf16[144,384]{1,0:T(8,128)(2,1)S(1)} %get-tuple-element.89), channel_id=1, source_target_pairs={{0,16},{2,18},{4,20},{6,22},{8,24},{10,26},{12,28},{14,30},{16,0},... | collective-permute-start | bytes 331784 | tf_op jit(solution)/shard_map/ppermute | solution.py:89
  106.6 8.8 %collective-permute-start.29 = (bf16[144,384]{1,0:T(8,128)(2,1)S(1)}, bf16[144,384]{1,0:T(8,128)(2,1)S(1)}, u32[]{:S(2)}, u32[]{:S(2)}) collective-permute-start(bf16[144,384]{1,0:T(8,128)(2,1)S(1)} %get-tuple-element.90), channel_id=1, source_target_pairs={{0,8},{2,10},{4,12},{6,14},{8,16},{10,18},{12,20},{14,22},{16,24},... | collective-permute-start | bytes 331784 | tf_op jit(solution)/shard_map/ppermute | solution.py:89
  115.8 7.9 %collective-permute-start.34 = (bf16[144,384]{1,0:T(8,128)(2,1)S(1)}, bf16[144,384]{1,0:T(8,128)(2,1)S(1)}, u32[]{:S(2)}, u32[]{:S(2)}) collective-permute-start(bf16[144,384]{1,0:T(8,128)(2,1)S(1)} %get-tuple-element.101), channel_id=1, source_target_pairs={{0,8},{2,10},{4,12},{6,14},{8,16},{10,18},{12,20},{14,22},{16,24},... | collective-permute-start | bytes 331784 | tf_op jit(solution)/shard_map/ppermute | solution.py:89
  115.9 9.3 %collective-permute-start.33 = (bf16[144,384]{1,0:T(8,128)(2,1)S(1)}, bf16[144,384]{1,0:T(8,128)(2,1)S(1)}, u32[]{:S(2)}, u32[]{:S(2)}) collective-permute-start(bf16[144,384]{1,0:T(8,128)(2,1)S(1)} %get-tuple-element.100), channel_id=1, source_target_pairs={{0,16},{2,18},{4,20},{6,22},{8,24},{10,26},{12,28},{14,30},{16,0},... | collective-permute-start | bytes 331784 | tf_op jit(solution)/shard_map/ppermute | solution.py:89
  117.5 7.8 %collective-permute-start.32 = (bf16[144,384]{1,0:T(8,128)(2,1)S(1)}, bf16[144,384]{1,0:T(8,128)(2,1)S(1)}, u32[]{:S(2)}, u32[]{:S(2)}) collective-permute-start(bf16[144,384]{1,0:T(8,128)(2,1)S(1)} %get-tuple-element.99), channel_id=1, source_target_pairs={{0,24},{2,26},{4,28},{6,30},{8,0},{10,2},{12,4},{14,6},{16,8},{18,... | collective-permute-start | bytes 331784 | tf_op jit(solution)/shard_map/ppermute | solution.py:89
  122.6 4.8 %collective-permute-start.31 = (bf16[144,384]{1,0:T(8,128)(2,1)S(1)}, bf16[144,384]{1,0:T(8,128)(2,1)S(1)}, u32[]{:S(2)}, u32[]{:S(2)}) collective-permute-start(bf16[144,384]{1,0:T(8,128)(2,1)S(1)} %fusion.96), channel_id=1, source_target_pairs={{0,1},{1,0},{2,3},{3,2},{4,5},{5,4},{6,7},{7,6},{8,9},{9,8},{10,11... | collective-permute-start | bytes 331784 | tf_op jit(solution)/shard_map/ppermute | solution.py:86
  125.4 4.8 %collective-permute-start.35 = (bf16[144,384]{1,0:T(8,128)(2,1)S(1)}, bf16[144,384]{1,0:T(8,128)(2,1)S(1)}, u32[]{:S(2)}, u32[]{:S(2)}) collective-permute-start(bf16[144,384]{1,0:T(8,128)(2,1)S(1)} %fusion.94), channel_id=1, source_target_pairs={{0,1},{1,0},{2,3},{3,2},{4,5},{5,4},{6,7},{7,6},{8,9},{9,8},{10,11... | collective-permute-start | bytes 331784 | tf_op jit(solution)/shard_map/ppermute | solution.py:86
  (8 other events, 29.6 us)

commit v5 on v4

--- a/solution.py
+++ b/solution.py
@@ -199,11 +199,17 @@
         return mine, by_y(mine)
 
     def finish(*pieces):
-        mine, theirs = jnp.stack(pieces[::2]), jnp.stack(pieces[1::2])
+        mine, theirs = pieces[::2], pieces[1::2]
         same = h == core
-        kept = jnp.where(same, mine, theirs)
-        given = lax.ppermute(jnp.where(same, theirs, mine), "dp", core_pairs)
-        return by_core(kept, given, 2).astype(F32)
+        given = jnp.stack([jnp.where(same, *pair) for pair in zip(theirs, mine)])
+        given = lax.ppermute(given, "dp", core_pairs).astype(F32)
+        kept = [jnp.where(same, *pair).astype(F32) for pair in zip(mine, theirs)]
+        return [
+            lax.dynamic_update_slice_in_dim(
+                jnp.concatenate([own, own], axis=1), came, (1 - core) * half, axis=1
+            )
+            for own, came in zip(kept, given)
+        ]
 
     slope = gelu_slope(hidden.astype(F32))
     mine, theirs = (
@@ -236,14 +242,15 @@
     came = lax.ppermute(sent, "dp", core_pairs)
     came, *first_came = together(came, *first_came)
     half_first = first_sum(grad_first, *first_came)
-    y_out, x_out, x_next, y_next = together(*second_out(*half_first), *first_out(grad_second))
+    x_next, y_next = together(*first_out(grad_second))
+    y_out, x_out = together(*second_out(*half_first))
     y_in, x_in, x_come, y_come = together(by_y(y_out), by_x(x_out), by_x(x_next), by_y(y_next))
     plane_first = second_sum(*half_first, y_in, x_in)
     half_second = first_sum(grad_second, x_come, y_come)
     y_out, x_out, *outs = together(*second_out(*half_second), *line_out(plane_first))
-    y_in, x_in, *line_first = together(by_y(y_out), by_x(x_out), *by_z(outs))
+    total_first = line_sum(plane_first, together(*by_z(outs)))
+    y_in, x_in, total_first = together(by_y(y_out), by_x(x_out), total_first)
     plane_second = second_sum(*half_second, y_in, x_in)
-    total_first = line_sum(plane_first, line_first)
     total_first, *outs = together(total_first, *line_out(plane_second))
     line_second = by_z(outs)
     tower = by_core(tower_mine[0], came[:rows], 1)

time: 133 us -> 130 us (0.977)
  waiting for transfers between devices: 54.5 us -> 50.7 us
    ppermute x8, waiting for transfers between devices: 13 us -> 9.63 us  [by_x(): return lax.ppermute(array, 'dp', x_pairs)]
    ppermute x9, waiting for transfers between devices: 24.4 us -> 21.5 us  [by_y(): return lax.ppermute(array, 'seq', y_pairs)]
    ppermute x9, starting transfers between devices: 8.94 us -> 10.5 us  [by_y(): return lax.ppermute(array, 'seq', y_pairs)]
    ppermute x1, waiting for transfers between devices: 0.01 us -> 1.51 us  [shards(): second_theirs = lax.ppermute(second_mine, 'dp', core_pairs)]
  transfers between devices with their start and end apart: 37 -> 37, of which waited for: 18 -> 20; matrix products, arithmetic and copies ran while one was open for 25% -> 20% of each run, Pallas kernels for 0% -> 0%
where the time goes in v5:
time: 130 us
  waiting for transfers between devices  50.7 us (39%)
  starting transfers between devices  41.8 us (32%)
  matrix products  21.8 us (17%)
  other arithmetic  11.1 us (9%)
  local copies, waits for them, and re-layouts  3.06 us (2%)
    ppermute x9, waiting for transfers between devices, by_y(): return lax.ppermute(array, 'seq', y_pairs)  21.5 us
    ppermute x12, starting transfers between devices, by_z(): lax.ppermute(out, 'dp', turn(step))  21.2 us
    ppermute x12, waiting for transfers between devices, by_z(): lax.ppermute(out, 'dp', turn(step))  14.1 us
    ppermute x9, starting transfers between devices, by_y(): return lax.ppermute(array, 'seq', y_pairs)  10.5 us
    ppermute x8, waiting for transfers between devices, by_x(): return lax.ppermute(array, 'dp', x_pairs)  9.63 us
    dot_general x2, matrix products, gradient(): lax.dot_general(stacked.reshape(2 * rows, 3 * channels), upstream.reshape...  8.28 us
    ppermute x8, starting transfers between devices, by_x(): return lax.ppermute(array, 'dp', x_pairs)  7.49 us
    dot_general x1, matrix products, shards(): jnp.dot(stack_first, first_mine, preferred_element_type=F32)  4.18 us
  transfers between devices with their start and end apart: 37, of which 20 were waited for; matrix products, arithmetic and copies ran while one was open for 20% of the time, Pallas kernels for 0%

profile of v5, /device:TPU:0, one launch (start us, length us, event | category | flops | bytes accessed | tf_op | source)
XLA Modules:
  0.0 129.8 jit_solution(6830802699596616315)
XLA Ops:
  2.2 1.5 %pad_maximum_fusion.1 = bf16[512,1536]{1,0:T(8,128)(2,1)S(1)} fusion(bf16[512,768]{1,0:T(8,128)(2,1)} %bitcast.220, bf16[512,768]{1,0:T(8,128)(2,1)} %bitcast.221), kind=kLoop, calls=%fused_computation.92 | loop fusion | flops 3145728 | bytes 3145728 | tf_op jit(solution)/shard_map/concatenate | solution.py:69
  4.0 4.9 %collective-permute-start.3 = (bf16[144,384]{1,0:T(8,128)(2,1)S(1)}, bf16[144,384]{1,0:T(8,128)(2,1)S(1)}, u32[]{:S(2)}, u32[]{:S(2)}) collective-permute-start(bf16[144,384]{1,0:T(8,128)(2,1)S(1)} %dynamic-slice_bitcast_fusion.4), channel_id=1, source_target_pairs={{0,24},{2,26},{4,28},{6,30},{8,0},{10,2},{12,4},{14,6},{16,8},{18,... | collective-permute-start | bytes 331784 | tf_op jit(solution)/shard_map/ppermute | solution.py:89
  9.9 1.5 %collective-permute-start.6 = (bf16[2,2,144,384]{3,2,1,0:T(8,128)(2,1)S(1)}, bf16[2,2,144,384]{3,2,1,0:T(8,128)(2,1)S(1)}, u32[]{:S(2)}, u32[]{:S(2)}) collective-permute-start(bf16[2,2,144,384]{3,2,1,0:T(8,128)(2,1)S(1)} %pad_maximum_fusion.11), channel_id=1, source_target_pairs={{0,4},{2,6},{4,0},{6,2},{8,12},{10,14},{12,8},{14,10},{16,20},{18,... | collective-permute-start | bytes 1327112 | tf_op jit(solution)/shard_map/ppermute | solution.py:83
  11.4 1.6 %collective-permute-start.1 = (bf16[16,1536]{1,0:T(8,128)(2,1)S(1)}, bf16[16,1536]{1,0:T(8,128)(2,1)S(1)}, u32[]{:S(2)}, u32[]{:S(2)}) collective-permute-start(bf16[16,1536]{1,0:T(8,128)(2,1)S(1)} %slice_select_fusion), channel_id=1, source_target_pairs={{0,1},{1,0},{2,3},{3,2},{4,5},{5,4},{6,7},{7,6},{8,9},{9,8},{10,11... | collective-permute-start | bytes 147464 | tf_op jit(solution)/shard_map/ppermute | solution.py:73
  13.0 2.6 %collective-permute-done.1 = bf16[16,1536]{1,0:T(8,128)(2,1)S(1)} collective-permute-done((bf16[16,1536]{1,0:T(8,128)(2,1)S(1)}, bf16[16,1536]{1,0:T(8,128)(2,1)S(1)}, u32[]{:S(2)}, u32[]{:S(2)}) %collective-permute-start.1) | collective-permute-done | bytes 49184 | tf_op jit(solution)/shard_map/ppermute | solution.py:73
  15.6 2.9 %collective-permute-start.9 = (bf16[144,384]{1,0:T(8,128)(2,1)S(1)}, bf16[144,384]{1,0:T(8,128)(2,1)S(1)}, u32[]{:S(2)}, u32[]{:S(2)}) collective-permute-start(bf16[144,384]{1,0:T(8,128)(2,1)S(1)} %dynamic-slice_bitcast_fusion.5), channel_id=1, source_target_pairs={{0,24},{2,26},{4,28},{6,30},{8,0},{10,2},{12,4},{14,6},{16,8},{18,... | collective-permute-start | bytes 331784 | tf_op jit(solution)/shard_map/ppermute | solution.py:89
  22.9 1.5 %collective-permute-start.8 = (bf16[3,144,384]{2,1,0:T(8,128)(2,1)S(1)}, bf16[3,144,384]{2,1,0:T(8,128)(2,1)S(1)}, u32[]{:S(2)}, u32[]{:S(2)}) collective-permute-start(bf16[3,144,384]{2,1,0:T(8,128)(2,1)S(1)} %pad_maximum_fusion.12), channel_id=1, source_target_pairs={{0,1},{1,0},{2,3},{3,2},{4,5},{5,4},{6,7},{7,6},{8,9},{9,8},{10,11... | collective-permute-start | bytes 995336 | tf_op jit(solution)/shard_map/ppermute | solution.py:86
  24.5 4.2 %collective-permute-done.10 = bf16[144,384]{1,0:T(8,128)(2,1)S(1)} collective-permute-done((bf16[144,384]{1,0:T(8,128)(2,1)S(1)}, bf16[144,384]{1,0:T(8,128)(2,1)S(1)}, u32[]{:S(2)}, u32[]{:S(2)}) %collective-permute-start.10) | collective-permute-done | bytes 110624 | tf_op jit(solution)/shard_map/ppermute | solution.py:89
  31.1 1.5 %collective-permute-start.14 = (bf16[3,144,384]{2,1,0:T(8,128)(2,1)S(1)}, bf16[3,144,384]{2,1,0:T(8,128)(2,1)S(1)}, u32[]{:S(2)}, u32[]{:S(2)}) collective-permute-start(bf16[3,144,384]{2,1,0:T(8,128)(2,1)S(1)} %pad_maximum_fusion.13), channel_id=1, source_target_pairs={{0,1},{1,0},{2,3},{3,2},{4,5},{5,4},{6,7},{7,6},{8,9},{9,8},{10,11... | collective-permute-start | bytes 995336 | tf_op jit(solution)/shard_map/ppermute | solution.py:86
  33.7 8.2 %collective-permute-done.14 = bf16[3,144,384]{2,1,0:T(8,128)(2,1)S(1)} collective-permute-done((bf16[3,144,384]{2,1,0:T(8,128)(2,1)S(1)}, bf16[3,144,384]{2,1,0:T(8,128)(2,1)S(1)}, u32[]{:S(2)}, u32[]{:S(2)}) %collective-permute-start.14) | collective-permute-done | bytes 331808 | tf_op jit(solution)/shard_map/ppermute | solution.py:86
  42.2 3.3 %collective-permute-done.12 = bf16[3,144,384]{2,1,0:T(8,128)(2,1)S(1)} collective-permute-done((bf16[3,144,384]{2,1,0:T(8,128)(2,1)S(1)}, bf16[3,144,384]{2,1,0:T(8,128)(2,1)S(1)}, u32[]{:S(2)}, u32[]{:S(2)}) %collective-permute-start.12) | collective-permute-done | bytes 331808 | tf_op jit(solution)/shard_map/ppermute | solution.py:86
  47.4 1.6 %collective-permute-done.16 = bf16[3,144,384]{2,1,0:T(8,128)(2,1)S(1)} collective-permute-done((bf16[3,144,384]{2,1,0:T(8,128)(2,1)S(1)}, bf16[3,144,384]{2,1,0:T(8,128)(2,1)S(1)}, u32[]{:S(2)}, u32[]{:S(2)}) %collective-permute-start.16) | collective-permute-done | bytes 331808 | tf_op jit(solution)/shard_map/ppermute | solution.py:83
  52.8 1.5 %collective-permute-done.17 = bf16[2304,384]{1,0:T(8,128)(2,1)S(1)} collective-permute-done((bf16[2304,384]{1,0:T(8,128)(2,1)S(1)}, bf16[2304,384]{1,0:T(8,128)(2,1)S(1)}, u32[]{:S(2)}, u32[]{:S(2)}) %collective-permute-start.17) | collective-permute-done | bytes 1769504 | tf_op jit(solution)/shard_map/ppermute | solution.py:147
  54.4 2.4 %fusion.34 = f32[2,544,1152]{2,1,0:T(8,128)S(1)} fusion(bf16[1152,384]{1,0:T(8,128)(2,1)S(1)} %bitcast.219, bf16[1152,384]{1,0:T(8,128)(2,1)S(1)} %bitcast.218, bf16[1,544,1536]{2,1,0:T(8,128)(2,1)S(1)} %bitcast.206, bf16[1,544,1536]{2,1,0:T(8,128)(2,1)S(1)} %bitcast.203), kind=kOutput, calls=%fused_computation.60 | convolution fusion | flops 1932066816 | bytes 10125312 | tf_op jit(solution)/shard_map/dot_general | solution.py:218
  56.8 4.2 %fusion.50 = (bf16[2,528,384]{2,1,0:T(8,128)(2,1)S(1)}, bf16[2,528,384]{2,1,0:T(8,128)(2,1)S(1)}, bf16[2,528,384]{2,1,0:T(8,128)(2,1)S(1)}) fusion(f32[2,544,1152]{2,1,0:T(8,128)S(1)} %fusion.34, bf16[2,544,384]{2,1,0:T(8,128)(2,1)S(1)} %fusion.77, pred[528]{0:T(1024)(128)(4,1)S(1)} %fusion.115, bf16[2304,384,1]{1,0,2:T(8,128)(2,1)S(1)} %bitcast.200, ...), kind=kOutput, calls=%fused_computation.78 | convolution fusion | flops 1892487168 | bytes 15557144 | tf_op jit(solution)/shard_map/dot_general | solution.py:143
  61.2 4.1 %fusion.21 = bf16[2304,384]{1,0:T(8,128)(2,1)S(1)} fusion(bf16[2,528,768]{2,1,0:T(8,128)(2,1)S(1)} %get-tuple-element.123, bf16[2,528,768]{2,1,0:T(8,128)(2,1)S(1)} %get-tuple-element.124, bf16[2,528,768]{2,1,0:T(8,128)(2,1)S(1)} %get-tuple-element.122, bf16[2,528,384]{2,1,0:T(8,128)(2,1)S(1)} %get-tuple-element.141), kind=kOutput, calls=%fused_computation.19 | convolution fusion | flops 1827864576 | bytes 7421952 | tf_op jit(solution)/shard_map/dot_general | solution.py:156
  66.5 1.5 %collective-permute-start.20 = (bf16[2,2,144,384]{3,2,0,1:T(8,128)(2,1)S(1)}, bf16[2,2,144,384]{3,2,0,1:T(8,128)(2,1)S(1)}, u32[]{:S(2)}, u32[]{:S(2)}) collective-permute-start(bf16[2,2,144,384]{3,2,0,1:T(8,128)(2,1)S(1)} %bitcast.223), channel_id=1, source_target_pairs={{0,1},{1,0},{2,3},{3,2},{4,5},{5,4},{6,7},{7,6},{8,9},{9,8},{10,11... | collective-permute-start | bytes 1327112 | tf_op jit(solution)/shard_map/ppermute | solution.py:86
  68.9 4.2 %fusion.20 = bf16[2304,384]{1,0:T(8,128)(2,1)S(1)} fusion(bf16[2,544,384]{2,1,0:T(8,128)(2,1)S(1)} %fusion.77, bf16[2,528,384]{2,1,0:T(8,128)(2,1)S(1)} %get-tuple-element.128, bf16[2,528,384]{2,1,0:T(8,128)(2,1)S(1)} %get-tuple-element.127, bf16[2,512,768]{2,1,0:T(8,128)(2,1)S(1)} %get-tuple-element.126, bf16[2,512,768]{2,1,0:T(8,128)(2,1)S(1)} %get-tuple-element.125), kind=kOutput, calls=%fused_computation.18 | convolution fusion | flops 1832583168 | bytes 7323648 | tf_op jit(solution)/shard_map/dot_general | solution.py:156
  73.1 3.1 %add_convert_fusion.1 = bf16[2,512,384]{2,1,0:T(8,128)(2,1)S(1)} fusion(bf16[2304,384,1]{1,0,2:T(8,128)(2,1)S(1)} %bitcast.209, bf16[2,528,384]{2,1,0:T(8,128)(2,1)S(1)} %get-tuple-element.173, bf16[2,528,384]{2,1,0:T(8,128)(2,1)S(1)} %get-tuple-element.128, bf16[2,528,384]{2,1,0:T(8,128)(2,1)S(1)} %get-tuple-element.127, ...), kind=kOutput, calls=%fused_computation.93 | convolution fusion | flops 1831993344 | bytes 8110080 | tf_op jit(solution)/shard_map/dot_general | solution.py:238
  79.2 1.6 %collective-permute-start.21 = (bf16[2,144,384]{2,1,0:T(8,128)(2,1)S(1)}, bf16[2,144,384]{2,1,0:T(8,128)(2,1)S(1)}, u32[]{:S(2)}, u32[]{:S(2)}) collective-permute-start(bf16[2,144,384]{2,1,0:T(8,128)(2,1)S(1)} %dynamic-slice_bitcast_fusion.3), channel_id=1, source_target_pairs={{0,1},{1,0},{2,3},{3,2},{4,5},{5,4},{6,7},{7,6},{8,9},{9,8},{10,11... | collective-permute-start | bytes 663560 | tf_op jit(solution)/shard_map/ppermute | solution.py:86
  83.7 6.2 %collective-permute-done.23 = bf16[2,2,144,384]{3,2,0,1:T(8,128)(2,1)S(1)} collective-permute-done((bf16[2,2,144,384]{3,2,0,1:T(8,128)(2,1)S(1)}, bf16[2,2,144,384]{3,2,0,1:T(8,128)(2,1)S(1)}, u32[]{:S(2)}, u32[]{:S(2)}) %collective-permute-start.23) | collective-permute-done | bytes 442400 | tf_op jit(solution)/shard_map/ppermute | solution.py:83
  91.4 4.0 %collective-permute-done.21 = bf16[2,144,384]{2,1,0:T(8,128)(2,1)S(1)} collective-permute-done((bf16[2,144,384]{2,1,0:T(8,128)(2,1)S(1)}, bf16[2,144,384]{2,1,0:T(8,128)(2,1)S(1)}, u32[]{:S(2)}, u32[]{:S(2)}) %collective-permute-start.21) | collective-permute-done | bytes 221216 | tf_op jit(solution)/shard_map/ppermute | solution.py:86
  96.0 3.6 %collective-permute-start.27 = (bf16[144,384]{1,0:T(8,128)(2,1)S(1)}, bf16[144,384]{1,0:T(8,128)(2,1)S(1)}, u32[]{:S(2)}, u32[]{:S(2)}) collective-permute-start(bf16[144,384]{1,0:T(8,128)(2,1)S(1)} %get-tuple-element.89), channel_id=1, source_target_pairs={{0,24},{2,26},{4,28},{6,30},{8,0},{10,2},{12,4},{14,6},{16,8},{18,... | collective-permute-start | bytes 331784 | tf_op jit(solution)/shard_map/ppermute | solution.py:89
  99.6 1.9 %collective-permute-start.28 = (bf16[144,384]{1,0:T(8,128)(2,1)S(1)}, bf16[144,384]{1,0:T(8,128)(2,1)S(1)}, u32[]{:S(2)}, u32[]{:S(2)}) collective-permute-start(bf16[144,384]{1,0:T(8,128)(2,1)S(1)} %get-tuple-element.90), channel_id=1, source_target_pairs={{0,16},{2,18},{4,20},{6,22},{8,24},{10,26},{12,28},{14,30},{16,0},... | collective-permute-start | bytes 331784 | tf_op jit(solution)/shard_map/ppermute | solution.py:89
  101.5 1.9 %collective-permute-start.29 = (bf16[144,384]{1,0:T(8,128)(2,1)S(1)}, bf16[144,384]{1,0:T(8,128)(2,1)S(1)}, u32[]{:S(2)}, u32[]{:S(2)}) collective-permute-start(bf16[144,384]{1,0:T(8,128)(2,1)S(1)} %get-tuple-element.91), channel_id=1, source_target_pairs={{0,8},{2,10},{4,12},{6,14},{8,16},{10,18},{12,20},{14,22},{16,24},... | collective-permute-start | bytes 331784 | tf_op jit(solution)/shard_map/ppermute | solution.py:89
  103.4 2.3 %fusion.61 = bf16[512,768]{1,0:T(8,128)(2,1)} fusion(f32[512,768]{1,0:T(8,128)S(1)} %fusion.70, f32[512,768]{1,0:T(8,128)S(1)} %fusion.67, bf16[2304,384]{1,0:T(8,128)(2,1)S(1)} %get-tuple-element.110, bf16[2304,384]{1,0:T(8,128)(2,1)S(1)} %get-tuple-element.111, bf16[528,384]{1,0:T(8,128)(2,1)S(1)} %get-tuple-element.129, ...), kind=kOutput, calls=%fused_computation.94 | convolution fusion | flops 614989824 | bytes 9879552 | tf_op jit(solution)/shard_map/dot_general | solution.py:263
  106.6 4.5 %collective-permute-done.28 = bf16[144,384]{1,0:T(8,128)(2,1)S(1)} collective-permute-done((bf16[144,384]{1,0:T(8,128)(2,1)S(1)}, bf16[144,384]{1,0:T(8,128)(2,1)S(1)}, u32[]{:S(2)}, u32[]{:S(2)}) %collective-permute-start.28) | collective-permute-done | bytes 110624 | tf_op jit(solution)/shard_map/ppermute | solution.py:89
  112.5 2.4 %collective-permute-start.33 = (bf16[144,384]{1,0:T(8,128)(2,1)S(1)}, bf16[144,384]{1,0:T(8,128)(2,1)S(1)}, u32[]{:S(2)}, u32[]{:S(2)}) collective-permute-start(bf16[144,384]{1,0:T(8,128)(2,1)S(1)} %get-tuple-element.102), channel_id=1, source_target_pairs={{0,16},{2,18},{4,20},{6,22},{8,24},{10,26},{12,28},{14,30},{16,0},... | collective-permute-start | bytes 331784 | tf_op jit(solution)/shard_map/ppermute | solution.py:89
  116.4 1.6 %collective-permute-start.31 = (bf16[144,384]{1,0:T(8,128)(2,1)S(1)}, bf16[144,384]{1,0:T(8,128)(2,1)S(1)}, u32[]{:S(2)}, u32[]{:S(2)}) collective-permute-start(bf16[144,384]{1,0:T(8,128)(2,1)S(1)} %fusion.98), channel_id=1, source_target_pairs={{0,1},{1,0},{2,3},{3,2},{4,5},{5,4},{6,7},{7,6},{8,9},{9,8},{10,11... | collective-permute-start | bytes 331784 | tf_op jit(solution)/shard_map/ppermute | solution.py:86
  118.0 1.9 %collective-permute-done.34 = bf16[144,384]{1,0:T(8,128)(2,1)S(1)} collective-permute-done((bf16[144,384]{1,0:T(8,128)(2,1)S(1)}, bf16[144,384]{1,0:T(8,128)(2,1)S(1)}, u32[]{:S(2)}, u32[]{:S(2)}) %collective-permute-start.34) | collective-permute-done | bytes 110624 | tf_op jit(solution)/shard_map/ppermute | solution.py:89
  119.9 2.3 %collective-permute-done.33 = bf16[144,384]{1,0:T(8,128)(2,1)S(1)} collective-permute-done((bf16[144,384]{1,0:T(8,128)(2,1)S(1)}, bf16[144,384]{1,0:T(8,128)(2,1)S(1)}, u32[]{:S(2)}, u32[]{:S(2)}) %collective-permute-start.33) | collective-permute-done | bytes 110624 | tf_op jit(solution)/shard_map/ppermute | solution.py:89
  124.5 2.7 %collective-permute-done.35 = bf16[144,384]{1,0:T(8,128)(2,1)S(1)} collective-permute-done((bf16[144,384]{1,0:T(8,128)(2,1)S(1)}, bf16[144,384]{1,0:T(8,128)(2,1)S(1)}, u32[]{:S(2)}, u32[]{:S(2)}) %collective-permute-start.35) | collective-permute-done | bytes 110624 | tf_op jit(solution)/shard_map/ppermute | solution.py:86
  (133 shorter events, 35.5 us)
Async XLA Ops:
  4.0 14.5 %collective-permute-start.3 = (bf16[144,384]{1,0:T(8,128)(2,1)S(1)}, bf16[144,384]{1,0:T(8,128)(2,1)S(1)}, u32[]{:S(2)}, u32[]{:S(2)}) collective-permute-start(bf16[144,384]{1,0:T(8,128)(2,1)S(1)} %dynamic-slice_bitcast_fusion.4), channel_id=1, source_target_pairs={{0,24},{2,26},{4,28},{6,30},{8,0},{10,2},{12,4},{14,6},{16,8},{18,... | collective-permute-start | bytes 331784 | tf_op jit(solution)/shard_map/ppermute | solution.py:89
  8.9 12.0 %collective-permute-start.4 = (bf16[144,384]{1,0:T(8,128)(2,1)S(1)}, bf16[144,384]{1,0:T(8,128)(2,1)S(1)}, u32[]{:S(2)}, u32[]{:S(2)}) collective-permute-start(bf16[144,384]{1,0:T(8,128)(2,1)S(1)} %dynamic-slice_bitcast_fusion.4), channel_id=1, source_target_pairs={{0,16},{2,18},{4,20},{6,22},{8,24},{10,26},{12,28},{14,30},{16,0},... | collective-permute-start | bytes 331784 | tf_op jit(solution)/shard_map/ppermute | solution.py:89
  8.9 12.0 %collective-permute-start.5 = (bf16[144,384]{1,0:T(8,128)(2,1)S(1)}, bf16[144,384]{1,0:T(8,128)(2,1)S(1)}, u32[]{:S(2)}, u32[]{:S(2)}) collective-permute-start(bf16[144,384]{1,0:T(8,128)(2,1)S(1)} %dynamic-slice_bitcast_fusion.4), channel_id=1, source_target_pairs={{0,8},{2,10},{4,12},{6,14},{8,16},{10,18},{12,20},{14,22},{16,24},... | collective-permute-start | bytes 331784 | tf_op jit(solution)/shard_map/ppermute | solution.py:89
  9.9 11.5 %collective-permute-start.6 = (bf16[2,2,144,384]{3,2,1,0:T(8,128)(2,1)S(1)}, bf16[2,2,144,384]{3,2,1,0:T(8,128)(2,1)S(1)}, u32[]{:S(2)}, u32[]{:S(2)}) collective-permute-start(bf16[2,2,144,384]{3,2,1,0:T(8,128)(2,1)S(1)} %pad_maximum_fusion.11), channel_id=1, source_target_pairs={{0,4},{2,6},{4,0},{6,2},{8,12},{10,14},{12,8},{14,10},{16,20},{18,... | collective-permute-start | bytes 1327112 | tf_op jit(solution)/shard_map/ppermute | solution.py:83
  15.6 8.9 %collective-permute-start.9 = (bf16[144,384]{1,0:T(8,128)(2,1)S(1)}, bf16[144,384]{1,0:T(8,128)(2,1)S(1)}, u32[]{:S(2)}, u32[]{:S(2)}) collective-permute-start(bf16[144,384]{1,0:T(8,128)(2,1)S(1)} %dynamic-slice_bitcast_fusion.5), channel_id=1, source_target_pairs={{0,24},{2,26},{4,28},{6,30},{8,0},{10,2},{12,4},{14,6},{16,8},{18,... | collective-permute-start | bytes 331784 | tf_op jit(solution)/shard_map/ppermute | solution.py:89
  18.6 10.2 %collective-permute-start.10 = (bf16[144,384]{1,0:T(8,128)(2,1)S(1)}, bf16[144,384]{1,0:T(8,128)(2,1)S(1)}, u32[]{:S(2)}, u32[]{:S(2)}) collective-permute-start(bf16[144,384]{1,0:T(8,128)(2,1)S(1)} %dynamic-slice_bitcast_fusion.5), channel_id=1, source_target_pairs={{0,16},{2,18},{4,20},{6,22},{8,24},{10,26},{12,28},{14,30},{16,0},... | collective-permute-start | bytes 331784 | tf_op jit(solution)/shard_map/ppermute | solution.py:89
  20.9 7.9 %collective-permute-start.11 = (bf16[144,384]{1,0:T(8,128)(2,1)S(1)}, bf16[144,384]{1,0:T(8,128)(2,1)S(1)}, u32[]{:S(2)}, u32[]{:S(2)}) collective-permute-start(bf16[144,384]{1,0:T(8,128)(2,1)S(1)} %dynamic-slice_bitcast_fusion.5), channel_id=1, source_target_pairs={{0,8},{2,10},{4,12},{6,14},{8,16},{10,18},{12,20},{14,22},{16,24},... | collective-permute-start | bytes 331784 | tf_op jit(solution)/shard_map/ppermute | solution.py:89
  21.4 8.2 %collective-permute-start.7 = (bf16[3,144,384]{2,1,0:T(8,128)(2,1)S(1)}, bf16[3,144,384]{2,1,0:T(8,128)(2,1)S(1)}, u32[]{:S(2)}, u32[]{:S(2)}) collective-permute-start(bf16[3,144,384]{2,1,0:T(8,128)(2,1)S(1)} %pad_maximum_fusion.12), channel_id=1, source_target_pairs={{0,4},{2,6},{4,0},{6,2},{8,12},{10,14},{12,8},{14,10},{16,20},{18,... | collective-permute-start | bytes 995336 | tf_op jit(solution)/shard_map/ppermute | solution.py:83
  22.9 8.2 %collective-permute-start.8 = (bf16[3,144,384]{2,1,0:T(8,128)(2,1)S(1)}, bf16[3,144,384]{2,1,0:T(8,128)(2,1)S(1)}, u32[]{:S(2)}, u32[]{:S(2)}) collective-permute-start(bf16[3,144,384]{2,1,0:T(8,128)(2,1)S(1)} %pad_maximum_fusion.12), channel_id=1, source_target_pairs={{0,1},{1,0},{2,3},{3,2},{4,5},{5,4},{6,7},{7,6},{8,9},{9,8},{10,11... | collective-permute-start | bytes 995336 | tf_op jit(solution)/shard_map/ppermute | solution.py:86
  24.5 26.2 %collective-permute-start.2 = (bf16[544,1536]{1,0:T(8,128)(2,1)S(1)}, bf16[544,1536]{1,0:T(8,128)(2,1)S(1)}, u32[]{:S(2)}, u32[]{:S(2)}) collective-permute-start(bf16[544,1536]{1,0:T(8,128)(2,1)S(1)} %constant_dynamic-update-slice_fusion), channel_id=1, source_target_pairs={{0,2},{2,0},{4,6},{6,4},{8,10},{10,8},{12,14},{14,12},{16,18},{18,... | collective-permute-start | bytes 5013512 | tf_op jit(solution)/shard_map/ppermute | solution.py:119
  31.1 10.7 %collective-permute-start.14 = (bf16[3,144,384]{2,1,0:T(8,128)(2,1)S(1)}, bf16[3,144,384]{2,1,0:T(8,128)(2,1)S(1)}, u32[]{:S(2)}, u32[]{:S(2)}) collective-permute-start(bf16[3,144,384]{2,1,0:T(8,128)(2,1)S(1)} %pad_maximum_fusion.13), channel_id=1, source_target_pairs={{0,1},{1,0},{2,3},{3,2},{4,5},{5,4},{6,7},{7,6},{8,9},{9,8},{10,11... | collective-permute-start | bytes 995336 | tf_op jit(solution)/shard_map/ppermute | solution.py:86
  32.7 12.9 %collective-permute-start.12 = (bf16[3,144,384]{2,1,0:T(8,128)(2,1)S(1)}, bf16[3,144,384]{2,1,0:T(8,128)(2,1)S(1)}, u32[]{:S(2)}, u32[]{:S(2)}) collective-permute-start(bf16[3,144,384]{2,1,0:T(8,128)(2,1)S(1)} %collective-permute-done.7), channel_id=1, source_target_pairs={{0,1},{1,0},{2,3},{3,2},{4,5},{5,4},{6,7},{7,6},{8,9},{9,8},{10,11... | collective-permute-start | bytes 995336 | tf_op jit(solution)/shard_map/ppermute | solution.py:86
  33.2 14.2 %collective-permute-start.15 = (bf16[3,144,384]{2,1,0:T(8,128)(2,1)S(1)}, bf16[3,144,384]{2,1,0:T(8,128)(2,1)S(1)}, u32[]{:S(2)}, u32[]{:S(2)}) collective-permute-start(bf16[3,144,384]{2,1,0:T(8,128)(2,1)S(1)} %pad_maximum_fusion.13), channel_id=1, source_target_pairs={{0,4},{2,6},{4,0},{6,2},{8,12},{10,14},{12,8},{14,10},{16,20},{18,... | collective-permute-start | bytes 995336 | tf_op jit(solution)/shard_map/ppermute | solution.py:83
  41.9 7.1 %collective-permute-start.16 = (bf16[3,144,384]{2,1,0:T(8,128)(2,1)S(1)}, bf16[3,144,384]{2,1,0:T(8,128)(2,1)S(1)}, u32[]{:S(2)}, u32[]{:S(2)}) collective-permute-start(bf16[3,144,384]{2,1,0:T(8,128)(2,1)S(1)} %collective-permute-done.14), channel_id=1, source_target_pairs={{0,4},{2,6},{4,0},{6,2},{8,12},{10,14},{12,8},{14,10},{16,20},{18,... | collective-permute-start | bytes 995336 | tf_op jit(solution)/shard_map/ppermute | solution.py:83
  47.2 5.0 %collective-permute-start.30 = (bf16[2304,384]{1,0:T(8,128)(2,1)S(1)}, bf16[2304,384]{1,0:T(8,128)(2,1)S(1)}, u32[]{:S(2)}, u32[]{:S(2)}) collective-permute-start(bf16[2304,384]{1,0:T(8,128)(2,1)S(1)} %bitcast.199), channel_id=1, source_target_pairs={{0,2},{2,0},{4,6},{6,4},{8,10},{10,8},{12,14},{14,12},{16,18},{18,... | collective-permute-start | bytes 5308424 | tf_op jit(solution)/shard_map/ppermute | solution.py:141
  61.0 7.0 %collective-permute-start.13 = (bf16[2,528,384]{2,1,0:T(8,128)(2,1)S(1)}, bf16[2,528,384]{2,1,0:T(8,128)(2,1)S(1)}, u32[]{:S(2)}, u32[]{:S(2)}) collective-permute-start(bf16[2,528,384]{2,1,0:T(8,128)(2,1)S(1)} %get-tuple-element.142), channel_id=1, source_target_pairs={{0,2},{2,0},{4,6},{6,4},{8,10},{10,8},{12,14},{14,12},{16,18},{18,... | collective-permute-start | bytes 2433032 | tf_op jit(solution)/shard_map/ppermute | solution.py:148
  65.8 13.0 %collective-permute-start.19 = (bf16[2,2,144,384]{3,2,0,1:T(8,128)(2,1)S(1)}, bf16[2,2,144,384]{3,2,0,1:T(8,128)(2,1)S(1)}, u32[]{:S(2)}, u32[]{:S(2)}) collective-permute-start(bf16[2,2,144,384]{3,2,0,1:T(8,128)(2,1)S(1)} %bitcast.222), channel_id=1, source_target_pairs={{0,4},{2,6},{4,0},{6,2},{8,12},{10,14},{12,8},{14,10},{16,20},{18,... | collective-permute-start | bytes 1327112 | tf_op jit(solution)/shard_map/ppermute | solution.py:83
  66.5 12.4 %collective-permute-start.20 = (bf16[2,2,144,384]{3,2,0,1:T(8,128)(2,1)S(1)}, bf16[2,2,144,384]{3,2,0,1:T(8,128)(2,1)S(1)}, u32[]{:S(2)}, u32[]{:S(2)}) collective-permute-start(bf16[2,2,144,384]{3,2,0,1:T(8,128)(2,1)S(1)} %bitcast.223), channel_id=1, source_target_pairs={{0,1},{1,0},{2,3},{3,2},{4,5},{5,4},{6,7},{7,6},{8,9},{9,8},{10,11... | collective-permute-start | bytes 1327112 | tf_op jit(solution)/shard_map/ppermute | solution.py:86
  76.9 13.0 %collective-permute-start.23 = (bf16[2,2,144,384]{3,2,0,1:T(8,128)(2,1)S(1)}, bf16[2,2,144,384]{3,2,0,1:T(8,128)(2,1)S(1)}, u32[]{:S(2)}, u32[]{:S(2)}) collective-permute-start(bf16[2,2,144,384]{3,2,0,1:T(8,128)(2,1)S(1)} %bitcast.224), channel_id=1, source_target_pairs={{0,4},{2,6},{4,0},{6,2},{8,12},{10,14},{12,8},{14,10},{16,20},{18,... | collective-permute-start | bytes 1327112 | tf_op jit(solution)/shard_map/ppermute | solution.py:83
  78.4 13.0 %collective-permute-start.24 = (bf16[2,2,144,384]{3,2,0,1:T(8,128)(2,1)S(1)}, bf16[2,2,144,384]{3,2,0,1:T(8,128)(2,1)S(1)}, u32[]{:S(2)}, u32[]{:S(2)}) collective-permute-start(bf16[2,2,144,384]{3,2,0,1:T(8,128)(2,1)S(1)} %bitcast.225), channel_id=1, source_target_pairs={{0,1},{1,0},{2,3},{3,2},{4,5},{5,4},{6,7},{7,6},{8,9},{9,8},{10,11... | collective-permute-start | bytes 1327112 | tf_op jit(solution)/shard_map/ppermute | solution.py:86
  79.2 16.2 %collective-permute-start.21 = (bf16[2,144,384]{2,1,0:T(8,128)(2,1)S(1)}, bf16[2,144,384]{2,1,0:T(8,128)(2,1)S(1)}, u32[]{:S(2)}, u32[]{:S(2)}) collective-permute-start(bf16[2,144,384]{2,1,0:T(8,128)(2,1)S(1)} %dynamic-slice_bitcast_fusion.3), channel_id=1, source_target_pairs={{0,1},{1,0},{2,3},{3,2},{4,5},{5,4},{6,7},{7,6},{8,9},{9,8},{10,11... | collective-permute-start | bytes 663560 | tf_op jit(solution)/shard_map/ppermute | solution.py:86
  80.8 14.6 %collective-permute-start.22 = (bf16[2,144,384]{2,1,0:T(8,128)(2,1)S(1)}, bf16[2,144,384]{2,1,0:T(8,128)(2,1)S(1)}, u32[]{:S(2)}, u32[]{:S(2)}) collective-permute-start(bf16[2,144,384]{2,1,0:T(8,128)(2,1)S(1)} %dynamic-slice_bitcast_fusion.2), channel_id=1, source_target_pairs={{0,4},{2,6},{4,0},{6,2},{8,12},{10,14},{12,8},{14,10},{16,20},{18,... | collective-permute-start | bytes 663560 | tf_op jit(solution)/shard_map/ppermute | solution.py:83
  96.0 10.6 %collective-permute-start.27 = (bf16[144,384]{1,0:T(8,128)(2,1)S(1)}, bf16[144,384]{1,0:T(8,128)(2,1)S(1)}, u32[]{:S(2)}, u32[]{:S(2)}) collective-permute-start(bf16[144,384]{1,0:T(8,128)(2,1)S(1)} %get-tuple-element.89), channel_id=1, source_target_pairs={{0,24},{2,26},{4,28},{6,30},{8,0},{10,2},{12,4},{14,6},{16,8},{18,... | collective-permute-start | bytes 331784 | tf_op jit(solution)/shard_map/ppermute | solution.py:89
  99.6 11.5 %collective-permute-start.28 = (bf16[144,384]{1,0:T(8,128)(2,1)S(1)}, bf16[144,384]{1,0:T(8,128)(2,1)S(1)}, u32[]{:S(2)}, u32[]{:S(2)}) collective-permute-start(bf16[144,384]{1,0:T(8,128)(2,1)S(1)} %get-tuple-element.90), channel_id=1, source_target_pairs={{0,16},{2,18},{4,20},{6,22},{8,24},{10,26},{12,28},{14,30},{16,0},... | collective-permute-start | bytes 331784 | tf_op jit(solution)/shard_map/ppermute | solution.py:89
  101.5 9.6 %collective-permute-start.29 = (bf16[144,384]{1,0:T(8,128)(2,1)S(1)}, bf16[144,384]{1,0:T(8,128)(2,1)S(1)}, u32[]{:S(2)}, u32[]{:S(2)}) collective-permute-start(bf16[144,384]{1,0:T(8,128)(2,1)S(1)} %get-tuple-element.91), channel_id=1, source_target_pairs={{0,8},{2,10},{4,12},{6,14},{8,16},{10,18},{12,20},{14,22},{16,24},... | collective-permute-start | bytes 331784 | tf_op jit(solution)/shard_map/ppermute | solution.py:89
  105.7 5.9 %collective-permute-start.25 = (bf16[2,144,384]{2,1,0:T(8,128)(2,1)S(1)}, bf16[2,144,384]{2,1,0:T(8,128)(2,1)S(1)}, u32[]{:S(2)}, u32[]{:S(2)}) collective-permute-start(bf16[2,144,384]{2,1,0:T(8,128)(2,1)S(1)} %dynamic-slice_bitcast_fusion.1), channel_id=1, source_target_pairs={{0,1},{1,0},{2,3},{3,2},{4,5},{5,4},{6,7},{7,6},{8,9},{9,8},{10,11... | collective-permute-start | bytes 663560 | tf_op jit(solution)/shard_map/ppermute | solution.py:86
  106.2 5.9 %collective-permute-start.26 = (bf16[2,144,384]{2,1,0:T(8,128)(2,1)S(1)}, bf16[2,144,384]{2,1,0:T(8,128)(2,1)S(1)}, u32[]{:S(2)}, u32[]{:S(2)}) collective-permute-start(bf16[2,144,384]{2,1,0:T(8,128)(2,1)S(1)} %dynamic-slice_bitcast_fusion), channel_id=1, source_target_pairs={{0,4},{2,6},{4,0},{6,2},{8,12},{10,14},{12,8},{14,10},{16,20},{18,... | collective-permute-start | bytes 663560 | tf_op jit(solution)/shard_map/ppermute | solution.py:83
  112.5 7.4 %collective-permute-start.34 = (bf16[144,384]{1,0:T(8,128)(2,1)S(1)}, bf16[144,384]{1,0:T(8,128)(2,1)S(1)}, u32[]{:S(2)}, u32[]{:S(2)}) collective-permute-start(bf16[144,384]{1,0:T(8,128)(2,1)S(1)} %get-tuple-element.103), channel_id=1, source_target_pairs={{0,8},{2,10},{4,12},{6,14},{8,16},{10,18},{12,20},{14,22},{16,24},... | collective-permute-start | bytes 331784 | tf_op jit(solution)/shard_map/ppermute | solution.py:89
  112.5 9.7 %collective-permute-start.33 = (bf16[144,384]{1,0:T(8,128)(2,1)S(1)}, bf16[144,384]{1,0:T(8,128)(2,1)S(1)}, u32[]{:S(2)}, u32[]{:S(2)}) collective-permute-start(bf16[144,384]{1,0:T(8,128)(2,1)S(1)} %get-tuple-element.102), channel_id=1, source_target_pairs={{0,16},{2,18},{4,20},{6,22},{8,24},{10,26},{12,28},{14,30},{16,0},... | collective-permute-start | bytes 331784 | tf_op jit(solution)/shard_map/ppermute | solution.py:89
  115.0 7.3 %collective-permute-start.32 = (bf16[144,384]{1,0:T(8,128)(2,1)S(1)}, bf16[144,384]{1,0:T(8,128)(2,1)S(1)}, u32[]{:S(2)}, u32[]{:S(2)}) collective-permute-start(bf16[144,384]{1,0:T(8,128)(2,1)S(1)} %get-tuple-element.101), channel_id=1, source_target_pairs={{0,24},{2,26},{4,28},{6,30},{8,0},{10,2},{12,4},{14,6},{16,8},{18,... | collective-permute-start | bytes 331784 | tf_op jit(solution)/shard_map/ppermute | solution.py:89
  116.4 8.0 %collective-permute-start.31 = (bf16[144,384]{1,0:T(8,128)(2,1)S(1)}, bf16[144,384]{1,0:T(8,128)(2,1)S(1)}, u32[]{:S(2)}, u32[]{:S(2)}) collective-permute-start(bf16[144,384]{1,0:T(8,128)(2,1)S(1)} %fusion.98), channel_id=1, source_target_pairs={{0,1},{1,0},{2,3},{3,2},{4,5},{5,4},{6,7},{7,6},{8,9},{9,8},{10,11... | collective-permute-start | bytes 331784 | tf_op jit(solution)/shard_map/ppermute | solution.py:86
  122.3 4.8 %collective-permute-start.35 = (bf16[144,384]{1,0:T(8,128)(2,1)S(1)}, bf16[144,384]{1,0:T(8,128)(2,1)S(1)}, u32[]{:S(2)}, u32[]{:S(2)}) collective-permute-start(bf16[144,384]{1,0:T(8,128)(2,1)S(1)} %fusion.96), channel_id=1, source_target_pairs={{0,1},{1,0},{2,3},{3,2},{4,5},{5,4},{6,7},{7,6},{8,9},{9,8},{10,11... | collective-permute-start | bytes 331784 | tf_op jit(solution)/shard_map/ppermute | solution.py:86
  (10 other events, 26.8 us)

commit v6 on v5

--- a/solution.py
+++ b/solution.py
@@ -237,14 +237,16 @@
         shifted(hidden, EDGE, rows).astype(F32)
         + jnp.dot(stack_second, second_mine, preferred_element_type=F32)
     ).astype(BF16)
-    sent = jnp.concatenate([tower_mine[1], grad_mine[1]], axis=0)
-    sent, grad_second = together(sent, grad_second)
+    sent, grad_second = together(grad_mine[1], grad_second)
+    tower_came = lax.ppermute(tower_mine[1], "dp", core_pairs)
     came = lax.ppermute(sent, "dp", core_pairs)
     came, *first_came = together(came, *first_came)
     half_first = first_sum(grad_first, *first_came)
     x_next, y_next = together(*first_out(grad_second))
     y_out, x_out = together(*second_out(*half_first))
-    y_in, x_in, x_come, y_come = together(by_y(y_out), by_x(x_out), by_x(x_next), by_y(y_next))
+    y_in, x_in, x_come, y_come, tower_came = together(
+        by_y(y_out), by_x(x_out), by_x(x_next), by_y(y_next), tower_came
+    )
     plane_first = second_sum(*half_first, y_in, x_in)
     half_second = first_sum(grad_second, x_come, y_come)
     y_out, x_out, *outs = together(*second_out(*half_second), *line_out(plane_first))
@@ -253,8 +255,8 @@
     plane_second = second_sum(*half_second, y_in, x_in)
     total_first, *outs = together(total_first, *line_out(plane_second))
     line_second = by_z(outs)
-    tower = by_core(tower_mine[0], came[:rows], 1)
-    grad_hidden = by_core(grad_mine[0], came[rows:], 1)
+    tower = by_core(tower_mine[0], tower_came, 1)
+    grad_hidden = by_core(grad_mine[0], came, 1)
 
     w_first_whole = by_core(first_mine, first_theirs, 1).reshape(3, channels, channels)
     spread = None

time: 130 us -> 128 us (0.985)
  waiting for transfers between devices: 50.7 us -> 47.6 us
    ppermute x8, starting transfers between devices: 7.49 us -> 8.94 us  [by_x(): return lax.ppermute(array, 'dp', x_pairs)]
    ppermute x8, waiting for transfers between devices: 9.63 us -> 8.19 us  [by_x(): return lax.ppermute(array, 'dp', x_pairs)]
    ppermute x12, waiting for transfers between devices: 14.1 us -> 12.8 us  [by_z(): lax.ppermute(out, 'dp', turn(step))]
  transfers between devices with their start and end apart: 37 -> 38, of which waited for: 20 -> 22; matrix products, arithmetic and copies ran while one was open for 20% -> 20% of each run, Pallas kernels for 0% -> 0%
where the time goes in v6:
time: 128 us
  waiting for transfers between devices  47.6 us (37%)
  starting transfers between devices  42.9 us (34%)
  matrix products  21.8 us (17%)
  other arithmetic  11.1 us (9%)
  local copies, waits for them, and re-layouts  3.06 us (2%)
    ppermute x9, waiting for transfers between devices, by_y(): return lax.ppermute(array, 'seq', y_pairs)  21.2 us
    ppermute x12, starting transfers between devices, by_z(): lax.ppermute(out, 'dp', turn(step))  21 us
    ppermute x12, waiting for transfers between devices, by_z(): lax.ppermute(out, 'dp', turn(step))  12.8 us
    ppermute x9, starting transfers between devices, by_y(): return lax.ppermute(array, 'seq', y_pairs)  10.3 us
    ppermute x8, starting transfers between devices, by_x(): return lax.ppermute(array, 'dp', x_pairs)  8.94 us
    dot_general x2, matrix products, gradient(): lax.dot_general(stacked.reshape(2 * rows, 3 * channels), upstream.reshape...  8.28 us
    ppermute x8, waiting for transfers between devices, by_x(): return lax.ppermute(array, 'dp', x_pairs)  8.19 us
    dot_general x1, matrix products, shards(): jnp.dot(stack_first, first_mine, preferred_element_type=F32)  4.18 us
  transfers between devices with their start and end apart: 38, of which 22 were waited for; matrix products, arithmetic and copies ran while one was open for 20% of the time, Pallas kernels for 0%

profile of v6, /device:TPU:0, one launch (start us, length us, event | category | flops | bytes accessed | tf_op | source)
XLA Modules:
  0.0 127.7 jit_solution(3083304406200550663)
XLA Ops:
  2.2 1.5 %pad_maximum_fusion.1 = bf16[512,1536]{1,0:T(8,128)(2,1)S(1)} fusion(bf16[512,768]{1,0:T(8,128)(2,1)} %bitcast.220, bf16[512,768]{1,0:T(8,128)(2,1)} %bitcast.221), kind=kLoop, calls=%fused_computation.92 | loop fusion | flops 3145728 | bytes 3145728 | tf_op jit(solution)/shard_map/concatenate | solution.py:69
  4.0 4.9 %collective-permute-start.3 = (bf16[144,384]{1,0:T(8,128)(2,1)S(1)}, bf16[144,384]{1,0:T(8,128)(2,1)S(1)}, u32[]{:S(2)}, u32[]{:S(2)}) collective-permute-start(bf16[144,384]{1,0:T(8,128)(2,1)S(1)} %dynamic-slice_bitcast_fusion.4), channel_id=1, source_target_pairs={{0,24},{2,26},{4,28},{6,30},{8,0},{10,2},{12,4},{14,6},{16,8},{18,... | collective-permute-start | bytes 331784 | tf_op jit(solution)/shard_map/ppermute | solution.py:89
  11.4 1.6 %collective-permute-start.1 = (bf16[16,1536]{1,0:T(8,128)(2,1)S(1)}, bf16[16,1536]{1,0:T(8,128)(2,1)S(1)}, u32[]{:S(2)}, u32[]{:S(2)}) collective-permute-start(bf16[16,1536]{1,0:T(8,128)(2,1)S(1)} %slice_select_fusion), channel_id=1, source_target_pairs={{0,1},{1,0},{2,3},{3,2},{4,5},{5,4},{6,7},{7,6},{8,9},{9,8},{10,11... | collective-permute-start | bytes 147464 | tf_op jit(solution)/shard_map/ppermute | solution.py:73
  13.0 2.6 %collective-permute-done.1 = bf16[16,1536]{1,0:T(8,128)(2,1)S(1)} collective-permute-done((bf16[16,1536]{1,0:T(8,128)(2,1)S(1)}, bf16[16,1536]{1,0:T(8,128)(2,1)S(1)}, u32[]{:S(2)}, u32[]{:S(2)}) %collective-permute-start.1) | collective-permute-done | bytes 49184 | tf_op jit(solution)/shard_map/ppermute | solution.py:73
  15.6 2.9 %collective-permute-start.9 = (bf16[144,384]{1,0:T(8,128)(2,1)S(1)}, bf16[144,384]{1,0:T(8,128)(2,1)S(1)}, u32[]{:S(2)}, u32[]{:S(2)}) collective-permute-start(bf16[144,384]{1,0:T(8,128)(2,1)S(1)} %dynamic-slice_bitcast_fusion.5), channel_id=1, source_target_pairs={{0,24},{2,26},{4,28},{6,30},{8,0},{10,2},{12,4},{14,6},{16,8},{18,... | collective-permute-start | bytes 331784 | tf_op jit(solution)/shard_map/ppermute | solution.py:89
  22.9 1.5 %collective-permute-start.8 = (bf16[3,144,384]{2,1,0:T(8,128)(2,1)S(1)}, bf16[3,144,384]{2,1,0:T(8,128)(2,1)S(1)}, u32[]{:S(2)}, u32[]{:S(2)}) collective-permute-start(bf16[3,144,384]{2,1,0:T(8,128)(2,1)S(1)} %pad_maximum_fusion.11), channel_id=1, source_target_pairs={{0,1},{1,0},{2,3},{3,2},{4,5},{5,4},{6,7},{7,6},{8,9},{9,8},{10,11... | collective-permute-start | bytes 995336 | tf_op jit(solution)/shard_map/ppermute | solution.py:86
  24.5 4.2 %collective-permute-done.10 = bf16[144,384]{1,0:T(8,128)(2,1)S(1)} collective-permute-done((bf16[144,384]{1,0:T(8,128)(2,1)S(1)}, bf16[144,384]{1,0:T(8,128)(2,1)S(1)}, u32[]{:S(2)}, u32[]{:S(2)}) %collective-permute-start.10) | collective-permute-done | bytes 110624 | tf_op jit(solution)/shard_map/ppermute | solution.py:89
  31.1 1.5 %collective-permute-start.14 = (bf16[3,144,384]{2,1,0:T(8,128)(2,1)S(1)}, bf16[3,144,384]{2,1,0:T(8,128)(2,1)S(1)}, u32[]{:S(2)}, u32[]{:S(2)}) collective-permute-start(bf16[3,144,384]{2,1,0:T(8,128)(2,1)S(1)} %pad_maximum_fusion.12), channel_id=1, source_target_pairs={{0,1},{1,0},{2,3},{3,2},{4,5},{5,4},{6,7},{7,6},{8,9},{9,8},{10,11... | collective-permute-start | bytes 995336 | tf_op jit(solution)/shard_map/ppermute | solution.py:86
  33.7 8.2 %collective-permute-done.14 = bf16[3,144,384]{2,1,0:T(8,128)(2,1)S(1)} collective-permute-done((bf16[3,144,384]{2,1,0:T(8,128)(2,1)S(1)}, bf16[3,144,384]{2,1,0:T(8,128)(2,1)S(1)}, u32[]{:S(2)}, u32[]{:S(2)}) %collective-permute-start.14) | collective-permute-done | bytes 331808 | tf_op jit(solution)/shard_map/ppermute | solution.py:86
  42.2 3.3 %collective-permute-done.12 = bf16[3,144,384]{2,1,0:T(8,128)(2,1)S(1)} collective-permute-done((bf16[3,144,384]{2,1,0:T(8,128)(2,1)S(1)}, bf16[3,144,384]{2,1,0:T(8,128)(2,1)S(1)}, u32[]{:S(2)}, u32[]{:S(2)}) %collective-permute-start.12) | collective-permute-done | bytes 331808 | tf_op jit(solution)/shard_map/ppermute | solution.py:86
  47.4 1.6 %collective-permute-done.16 = bf16[3,144,384]{2,1,0:T(8,128)(2,1)S(1)} collective-permute-done((bf16[3,144,384]{2,1,0:T(8,128)(2,1)S(1)}, bf16[3,144,384]{2,1,0:T(8,128)(2,1)S(1)}, u32[]{:S(2)}, u32[]{:S(2)}) %collective-permute-start.16) | collective-permute-done | bytes 331808 | tf_op jit(solution)/shard_map/ppermute | solution.py:83
  52.8 1.5 %collective-permute-done.17 = bf16[2304,384]{1,0:T(8,128)(2,1)S(1)} collective-permute-done((bf16[2304,384]{1,0:T(8,128)(2,1)S(1)}, bf16[2304,384]{1,0:T(8,128)(2,1)S(1)}, u32[]{:S(2)}, u32[]{:S(2)}) %collective-permute-start.17) | collective-permute-done | bytes 1769504 | tf_op jit(solution)/shard_map/ppermute | solution.py:147
  54.4 2.4 %fusion.34 = f32[2,544,1152]{2,1,0:T(8,128)S(1)} fusion(bf16[1152,384]{1,0:T(8,128)(2,1)S(1)} %bitcast.219, bf16[1152,384]{1,0:T(8,128)(2,1)S(1)} %bitcast.218, bf16[1,544,1536]{2,1,0:T(8,128)(2,1)S(1)} %bitcast.206, bf16[1,544,1536]{2,1,0:T(8,128)(2,1)S(1)} %bitcast.203), kind=kOutput, calls=%fused_computation.60 | convolution fusion | flops 1932066816 | bytes 10125312 | tf_op jit(solution)/shard_map/dot_general | solution.py:218
  56.8 4.2 %fusion.41 = (bf16[2,528,384]{2,1,0:T(8,128)(2,1)S(1)}, bf16[2,528,384]{2,1,0:T(8,128)(2,1)S(1)}, bf16[2,528,384]{2,1,0:T(8,128)(2,1)S(1)}) fusion(pred[528]{0:T(1024)(128)(4,1)S(1)} %fusion.115, f32[2,544,1152]{2,1,0:T(8,128)S(1)} %fusion.34, bf16[2,544,384]{2,1,0:T(8,128)(2,1)S(1)} %fusion.77, bf16[2304,384,1]{1,0,2:T(8,128)(2,1)S(1)} %bitcast.200, ...), kind=kOutput, calls=%fused_computation.69 | convolution fusion | flops 1892487168 | bytes 15557144 | tf_op jit(solution)/shard_map/dot_general | solution.py:143
  61.2 4.1 %fusion.21 = bf16[2304,384]{1,0:T(8,128)(2,1)S(1)} fusion(bf16[2,528,768]{2,1,0:T(8,128)(2,1)S(1)} %get-tuple-element.125, bf16[2,528,768]{2,1,0:T(8,128)(2,1)S(1)} %get-tuple-element.126, bf16[2,528,768]{2,1,0:T(8,128)(2,1)S(1)} %get-tuple-element.124, bf16[2,528,384]{2,1,0:T(8,128)(2,1)S(1)} %get-tuple-element.144), kind=kOutput, calls=%fused_computation.19 | convolution fusion | flops 1827864576 | bytes 7421952 | tf_op jit(solution)/shard_map/dot_general | solution.py:156
  66.5 1.5 %collective-permute-start.20 = (bf16[2,2,144,384]{3,2,0,1:T(8,128)(2,1)S(1)}, bf16[2,2,144,384]{3,2,0,1:T(8,128)(2,1)S(1)}, u32[]{:S(2)}, u32[]{:S(2)}) collective-permute-start(bf16[2,2,144,384]{3,2,0,1:T(8,128)(2,1)S(1)} %bitcast.223), channel_id=1, source_target_pairs={{0,1},{1,0},{2,3},{3,2},{4,5},{5,4},{6,7},{7,6},{8,9},{9,8},{10,11... | collective-permute-start | bytes 1327112 | tf_op jit(solution)/shard_map/ppermute | solution.py:86
  68.9 4.2 %fusion.20 = bf16[2304,384]{1,0:T(8,128)(2,1)S(1)} fusion(bf16[2,544,384]{2,1,0:T(8,128)(2,1)S(1)} %fusion.77, bf16[2,528,384]{2,1,0:T(8,128)(2,1)S(1)} %get-tuple-element.130, bf16[2,528,384]{2,1,0:T(8,128)(2,1)S(1)} %get-tuple-element.129, bf16[2,512,768]{2,1,0:T(8,128)(2,1)S(1)} %get-tuple-element.128, bf16[2,512,768]{2,1,0:T(8,128)(2,1)S(1)} %get-tuple-element.127), kind=kOutput, calls=%fused_computation.18 | convolution fusion | flops 1832583168 | bytes 7323648 | tf_op jit(solution)/shard_map/dot_general | solution.py:156
  75.6 3.0 %add_convert_fusion.1 = bf16[2,512,384]{2,1,0:T(8,128)(2,1)S(1)} fusion(bf16[2304,384,1]{1,0,2:T(8,128)(2,1)S(1)} %bitcast.209, bf16[2,528,384]{2,1,0:T(8,128)(2,1)S(1)} %get-tuple-element.175, bf16[2,528,384]{2,1,0:T(8,128)(2,1)S(1)} %get-tuple-element.130, bf16[2,528,384]{2,1,0:T(8,128)(2,1)S(1)} %get-tuple-element.129, ...), kind=kOutput, calls=%fused_computation.93 | convolution fusion | flops 1831993344 | bytes 8110080 | tf_op jit(solution)/shard_map/dot_general | solution.py:238
  79.6 1.8 %collective-permute-start.21 = (bf16[2,144,384]{2,1,0:T(8,128)(2,1)S(1)}, bf16[2,144,384]{2,1,0:T(8,128)(2,1)S(1)}, u32[]{:S(2)}, u32[]{:S(2)}) collective-permute-start(bf16[2,144,384]{2,1,0:T(8,128)(2,1)S(1)} %dynamic-slice_bitcast_fusion.3), channel_id=1, source_target_pairs={{0,1},{1,0},{2,3},{3,2},{4,5},{5,4},{6,7},{7,6},{8,9},{9,8},{10,11... | collective-permute-start | bytes 663560 | tf_op jit(solution)/shard_map/ppermute | solution.py:86
  84.6 3.8 %collective-permute-done.23 = bf16[2,2,144,384]{3,2,0,1:T(8,128)(2,1)S(1)} collective-permute-done((bf16[2,2,144,384]{3,2,0,1:T(8,128)(2,1)S(1)}, bf16[2,2,144,384]{3,2,0,1:T(8,128)(2,1)S(1)}, u32[]{:S(2)}, u32[]{:S(2)}) %collective-permute-start.23) | collective-permute-done | bytes 442400 | tf_op jit(solution)/shard_map/ppermute | solution.py:83
  88.7 4.1 %collective-permute-done.21 = bf16[2,144,384]{2,1,0:T(8,128)(2,1)S(1)} collective-permute-done((bf16[2,144,384]{2,1,0:T(8,128)(2,1)S(1)}, bf16[2,144,384]{2,1,0:T(8,128)(2,1)S(1)}, u32[]{:S(2)}, u32[]{:S(2)}) %collective-permute-start.21) | collective-permute-done | bytes 221216 | tf_op jit(solution)/shard_map/ppermute | solution.py:86
  93.5 3.4 %collective-permute-start.28 = (bf16[144,384]{1,0:T(8,128)(2,1)S(1)}, bf16[144,384]{1,0:T(8,128)(2,1)S(1)}, u32[]{:S(2)}, u32[]{:S(2)}) collective-permute-start(bf16[144,384]{1,0:T(8,128)(2,1)S(1)} %get-tuple-element.90), channel_id=1, source_target_pairs={{0,24},{2,26},{4,28},{6,30},{8,0},{10,2},{12,4},{14,6},{16,8},{18,... | collective-permute-start | bytes 331784 | tf_op jit(solution)/shard_map/ppermute | solution.py:89
  96.9 1.9 %collective-permute-start.29 = (bf16[144,384]{1,0:T(8,128)(2,1)S(1)}, bf16[144,384]{1,0:T(8,128)(2,1)S(1)}, u32[]{:S(2)}, u32[]{:S(2)}) collective-permute-start(bf16[144,384]{1,0:T(8,128)(2,1)S(1)} %get-tuple-element.91), channel_id=1, source_target_pairs={{0,16},{2,18},{4,20},{6,22},{8,24},{10,26},{12,28},{14,30},{16,0},... | collective-permute-start | bytes 331784 | tf_op jit(solution)/shard_map/ppermute | solution.py:89
  98.8 1.9 %collective-permute-start.30 = (bf16[144,384]{1,0:T(8,128)(2,1)S(1)}, bf16[144,384]{1,0:T(8,128)(2,1)S(1)}, u32[]{:S(2)}, u32[]{:S(2)}) collective-permute-start(bf16[144,384]{1,0:T(8,128)(2,1)S(1)} %get-tuple-element.92), channel_id=1, source_target_pairs={{0,8},{2,10},{4,12},{6,14},{8,16},{10,18},{12,20},{14,22},{16,24},... | collective-permute-start | bytes 331784 | tf_op jit(solution)/shard_map/ppermute | solution.py:89
  100.7 2.3 %fusion.61 = bf16[512,768]{1,0:T(8,128)(2,1)} fusion(f32[512,768]{1,0:T(8,128)S(1)} %fusion.70, f32[512,768]{1,0:T(8,128)S(1)} %fusion.67, bf16[2304,384]{1,0:T(8,128)(2,1)S(1)} %get-tuple-element.112, bf16[2304,384]{1,0:T(8,128)(2,1)S(1)} %get-tuple-element.113, bf16[528,384]{1,0:T(8,128)(2,1)S(1)} %get-tuple-element.131, ...), kind=kOutput, calls=%fused_computation.94 | convolution fusion | flops 614989824 | bytes 9879552 | tf_op jit(solution)/shard_map/dot_general | solution.py:265
  103.0 1.5 %collective-permute-start.26 = (bf16[2,144,384]{2,1,0:T(8,128)(2,1)S(1)}, bf16[2,144,384]{2,1,0:T(8,128)(2,1)S(1)}, u32[]{:S(2)}, u32[]{:S(2)}) collective-permute-start(bf16[2,144,384]{2,1,0:T(8,128)(2,1)S(1)} %dynamic-slice_bitcast_fusion.1), channel_id=1, source_target_pairs={{0,1},{1,0},{2,3},{3,2},{4,5},{5,4},{6,7},{7,6},{8,9},{9,8},{10,11... | collective-permute-start | bytes 663560 | tf_op jit(solution)/shard_map/ppermute | solution.py:86
  104.5 1.6 %collective-permute-start.27 = (bf16[2,144,384]{2,1,0:T(8,128)(2,1)S(1)}, bf16[2,144,384]{2,1,0:T(8,128)(2,1)S(1)}, u32[]{:S(2)}, u32[]{:S(2)}) collective-permute-start(bf16[2,144,384]{2,1,0:T(8,128)(2,1)S(1)} %dynamic-slice_bitcast_fusion), channel_id=1, source_target_pairs={{0,4},{2,6},{4,0},{6,2},{8,12},{10,14},{12,8},{14,10},{16,20},{18,... | collective-permute-start | bytes 663560 | tf_op jit(solution)/shard_map/ppermute | solution.py:83
  106.1 2.5 %collective-permute-done.29 = bf16[144,384]{1,0:T(8,128)(2,1)S(1)} collective-permute-done((bf16[144,384]{1,0:T(8,128)(2,1)S(1)}, bf16[144,384]{1,0:T(8,128)(2,1)S(1)}, u32[]{:S(2)}, u32[]{:S(2)}) %collective-permute-start.29) | collective-permute-done | bytes 110624 | tf_op jit(solution)/shard_map/ppermute | solution.py:89
  110.9 2.4 %collective-permute-start.34 = (bf16[144,384]{1,0:T(8,128)(2,1)S(1)}, bf16[144,384]{1,0:T(8,128)(2,1)S(1)}, u32[]{:S(2)}, u32[]{:S(2)}) collective-permute-start(bf16[144,384]{1,0:T(8,128)(2,1)S(1)} %get-tuple-element.104), channel_id=1, source_target_pairs={{0,16},{2,18},{4,20},{6,22},{8,24},{10,26},{12,28},{14,30},{16,0},... | collective-permute-start | bytes 331784 | tf_op jit(solution)/shard_map/ppermute | solution.py:89
  115.3 2.3 %collective-permute-done.35 = bf16[144,384]{1,0:T(8,128)(2,1)S(1)} collective-permute-done((bf16[144,384]{1,0:T(8,128)(2,1)S(1)}, bf16[144,384]{1,0:T(8,128)(2,1)S(1)}, u32[]{:S(2)}, u32[]{:S(2)}) %collective-permute-start.35) | collective-permute-done | bytes 110624 | tf_op jit(solution)/shard_map/ppermute | solution.py:89
  117.6 2.5 %collective-permute-done.34 = bf16[144,384]{1,0:T(8,128)(2,1)S(1)} collective-permute-done((bf16[144,384]{1,0:T(8,128)(2,1)S(1)}, bf16[144,384]{1,0:T(8,128)(2,1)S(1)}, u32[]{:S(2)}, u32[]{:S(2)}) %collective-permute-start.34) | collective-permute-done | bytes 110624 | tf_op jit(solution)/shard_map/ppermute | solution.py:89
  122.0 3.1 %collective-permute-done.36 = bf16[144,384]{1,0:T(8,128)(2,1)S(1)} collective-permute-done((bf16[144,384]{1,0:T(8,128)(2,1)S(1)}, bf16[144,384]{1,0:T(8,128)(2,1)S(1)}, u32[]{:S(2)}, u32[]{:S(2)}) %collective-permute-start.36) | collective-permute-done | bytes 110624 | tf_op jit(solution)/shard_map/ppermute | solution.py:86
  (134 shorter events, 36.6 us)
Async XLA Ops:
  4.0 14.5 %collective-permute-start.3 = (bf16[144,384]{1,0:T(8,128)(2,1)S(1)}, bf16[144,384]{1,0:T(8,128)(2,1)S(1)}, u32[]{:S(2)}, u32[]{:S(2)}) collective-permute-start(bf16[144,384]{1,0:T(8,128)(2,1)S(1)} %dynamic-slice_bitcast_fusion.4), channel_id=1, source_target_pairs={{0,24},{2,26},{4,28},{6,30},{8,0},{10,2},{12,4},{14,6},{16,8},{18,... | collective-permute-start | bytes 331784 | tf_op jit(solution)/shard_map/ppermute | solution.py:89
  8.9 12.0 %collective-permute-start.4 = (bf16[144,384]{1,0:T(8,128)(2,1)S(1)}, bf16[144,384]{1,0:T(8,128)(2,1)S(1)}, u32[]{:S(2)}, u32[]{:S(2)}) collective-permute-start(bf16[144,384]{1,0:T(8,128)(2,1)S(1)} %dynamic-slice_bitcast_fusion.4), channel_id=1, source_target_pairs={{0,16},{2,18},{4,20},{6,22},{8,24},{10,26},{12,28},{14,30},{16,0},... | collective-permute-start | bytes 331784 | tf_op jit(solution)/shard_map/ppermute | solution.py:89
  8.9 12.0 %collective-permute-start.5 = (bf16[144,384]{1,0:T(8,128)(2,1)S(1)}, bf16[144,384]{1,0:T(8,128)(2,1)S(1)}, u32[]{:S(2)}, u32[]{:S(2)}) collective-permute-start(bf16[144,384]{1,0:T(8,128)(2,1)S(1)} %dynamic-slice_bitcast_fusion.4), channel_id=1, source_target_pairs={{0,8},{2,10},{4,12},{6,14},{8,16},{10,18},{12,20},{14,22},{16,24},... | collective-permute-start | bytes 331784 | tf_op jit(solution)/shard_map/ppermute | solution.py:89
  9.9 11.5 %collective-permute-start.6 = (bf16[2,2,144,384]{3,2,1,0:T(8,128)(2,1)S(1)}, bf16[2,2,144,384]{3,2,1,0:T(8,128)(2,1)S(1)}, u32[]{:S(2)}, u32[]{:S(2)}) collective-permute-start(bf16[2,2,144,384]{3,2,1,0:T(8,128)(2,1)S(1)} %pad_maximum_fusion.10), channel_id=1, source_target_pairs={{0,4},{2,6},{4,0},{6,2},{8,12},{10,14},{12,8},{14,10},{16,20},{18,... | collective-permute-start | bytes 1327112 | tf_op jit(solution)/shard_map/ppermute | solution.py:83
  15.6 8.9 %collective-permute-start.9 = (bf16[144,384]{1,0:T(8,128)(2,1)S(1)}, bf16[144,384]{1,0:T(8,128)(2,1)S(1)}, u32[]{:S(2)}, u32[]{:S(2)}) collective-permute-start(bf16[144,384]{1,0:T(8,128)(2,1)S(1)} %dynamic-slice_bitcast_fusion.5), channel_id=1, source_target_pairs={{0,24},{2,26},{4,28},{6,30},{8,0},{10,2},{12,4},{14,6},{16,8},{18,... | collective-permute-start | bytes 331784 | tf_op jit(solution)/shard_map/ppermute | solution.py:89
  18.6 10.2 %collective-permute-start.10 = (bf16[144,384]{1,0:T(8,128)(2,1)S(1)}, bf16[144,384]{1,0:T(8,128)(2,1)S(1)}, u32[]{:S(2)}, u32[]{:S(2)}) collective-permute-start(bf16[144,384]{1,0:T(8,128)(2,1)S(1)} %dynamic-slice_bitcast_fusion.5), channel_id=1, source_target_pairs={{0,16},{2,18},{4,20},{6,22},{8,24},{10,26},{12,28},{14,30},{16,0},... | collective-permute-start | bytes 331784 | tf_op jit(solution)/shard_map/ppermute | solution.py:89
  20.9 7.9 %collective-permute-start.11 = (bf16[144,384]{1,0:T(8,128)(2,1)S(1)}, bf16[144,384]{1,0:T(8,128)(2,1)S(1)}, u32[]{:S(2)}, u32[]{:S(2)}) collective-permute-start(bf16[144,384]{1,0:T(8,128)(2,1)S(1)} %dynamic-slice_bitcast_fusion.5), channel_id=1, source_target_pairs={{0,8},{2,10},{4,12},{6,14},{8,16},{10,18},{12,20},{14,22},{16,24},... | collective-permute-start | bytes 331784 | tf_op jit(solution)/shard_map/ppermute | solution.py:89
  21.4 8.2 %collective-permute-start.7 = (bf16[3,144,384]{2,1,0:T(8,128)(2,1)S(1)}, bf16[3,144,384]{2,1,0:T(8,128)(2,1)S(1)}, u32[]{:S(2)}, u32[]{:S(2)}) collective-permute-start(bf16[3,144,384]{2,1,0:T(8,128)(2,1)S(1)} %pad_maximum_fusion.11), channel_id=1, source_target_pairs={{0,4},{2,6},{4,0},{6,2},{8,12},{10,14},{12,8},{14,10},{16,20},{18,... | collective-permute-start | bytes 995336 | tf_op jit(solution)/shard_map/ppermute | solution.py:83
  22.9 8.2 %collective-permute-start.8 = (bf16[3,144,384]{2,1,0:T(8,128)(2,1)S(1)}, bf16[3,144,384]{2,1,0:T(8,128)(2,1)S(1)}, u32[]{:S(2)}, u32[]{:S(2)}) collective-permute-start(bf16[3,144,384]{2,1,0:T(8,128)(2,1)S(1)} %pad_maximum_fusion.11), channel_id=1, source_target_pairs={{0,1},{1,0},{2,3},{3,2},{4,5},{5,4},{6,7},{7,6},{8,9},{9,8},{10,11... | collective-permute-start | bytes 995336 | tf_op jit(solution)/shard_map/ppermute | solution.py:86
  24.5 26.2 %collective-permute-start.2 = (bf16[544,1536]{1,0:T(8,128)(2,1)S(1)}, bf16[544,1536]{1,0:T(8,128)(2,1)S(1)}, u32[]{:S(2)}, u32[]{:S(2)}) collective-permute-start(bf16[544,1536]{1,0:T(8,128)(2,1)S(1)} %constant_dynamic-update-slice_fusion), channel_id=1, source_target_pairs={{0,2},{2,0},{4,6},{6,4},{8,10},{10,8},{12,14},{14,12},{16,18},{18,... | collective-permute-start | bytes 5013512 | tf_op jit(solution)/shard_map/ppermute | solution.py:119
  31.1 10.7 %collective-permute-start.14 = (bf16[3,144,384]{2,1,0:T(8,128)(2,1)S(1)}, bf16[3,144,384]{2,1,0:T(8,128)(2,1)S(1)}, u32[]{:S(2)}, u32[]{:S(2)}) collective-permute-start(bf16[3,144,384]{2,1,0:T(8,128)(2,1)S(1)} %pad_maximum_fusion.12), channel_id=1, source_target_pairs={{0,1},{1,0},{2,3},{3,2},{4,5},{5,4},{6,7},{7,6},{8,9},{9,8},{10,11... | collective-permute-start | bytes 995336 | tf_op jit(solution)/shard_map/ppermute | solution.py:86
  32.6 12.9 %collective-permute-start.12 = (bf16[3,144,384]{2,1,0:T(8,128)(2,1)S(1)}, bf16[3,144,384]{2,1,0:T(8,128)(2,1)S(1)}, u32[]{:S(2)}, u32[]{:S(2)}) collective-permute-start(bf16[3,144,384]{2,1,0:T(8,128)(2,1)S(1)} %collective-permute-done.7), channel_id=1, source_target_pairs={{0,1},{1,0},{2,3},{3,2},{4,5},{5,4},{6,7},{7,6},{8,9},{9,8},{10,11... | collective-permute-start | bytes 995336 | tf_op jit(solution)/shard_map/ppermute | solution.py:86
  33.2 14.2 %collective-permute-start.15 = (bf16[3,144,384]{2,1,0:T(8,128)(2,1)S(1)}, bf16[3,144,384]{2,1,0:T(8,128)(2,1)S(1)}, u32[]{:S(2)}, u32[]{:S(2)}) collective-permute-start(bf16[3,144,384]{2,1,0:T(8,128)(2,1)S(1)} %pad_maximum_fusion.12), channel_id=1, source_target_pairs={{0,4},{2,6},{4,0},{6,2},{8,12},{10,14},{12,8},{14,10},{16,20},{18,... | collective-permute-start | bytes 995336 | tf_op jit(solution)/shard_map/ppermute | solution.py:83
  41.9 7.1 %collective-permute-start.16 = (bf16[3,144,384]{2,1,0:T(8,128)(2,1)S(1)}, bf16[3,144,384]{2,1,0:T(8,128)(2,1)S(1)}, u32[]{:S(2)}, u32[]{:S(2)}) collective-permute-start(bf16[3,144,384]{2,1,0:T(8,128)(2,1)S(1)} %collective-permute-done.14), channel_id=1, source_target_pairs={{0,4},{2,6},{4,0},{6,2},{8,12},{10,14},{12,8},{14,10},{16,20},{18,... | collective-permute-start | bytes 995336 | tf_op jit(solution)/shard_map/ppermute | solution.py:83
  61.0 7.0 %collective-permute-start.13 = (bf16[2,528,384]{2,1,0:T(8,128)(2,1)S(1)}, bf16[2,528,384]{2,1,0:T(8,128)(2,1)S(1)}, u32[]{:S(2)}, u32[]{:S(2)}) collective-permute-start(bf16[2,528,384]{2,1,0:T(8,128)(2,1)S(1)} %get-tuple-element.143), channel_id=1, source_target_pairs={{0,2},{2,0},{4,6},{6,4},{8,10},{10,8},{12,14},{14,12},{16,18},{18,... | collective-permute-start | bytes 2433032 | tf_op jit(solution)/shard_map/ppermute | solution.py:148
  65.8 13.1 %collective-permute-start.19 = (bf16[2,2,144,384]{3,2,0,1:T(8,128)(2,1)S(1)}, bf16[2,2,144,384]{3,2,0,1:T(8,128)(2,1)S(1)}, u32[]{:S(2)}, u32[]{:S(2)}) collective-permute-start(bf16[2,2,144,384]{3,2,0,1:T(8,128)(2,1)S(1)} %bitcast.224), channel_id=1, source_target_pairs={{0,4},{2,6},{4,0},{6,2},{8,12},{10,14},{12,8},{14,10},{16,20},{18,... | collective-permute-start | bytes 1327112 | tf_op jit(solution)/shard_map/ppermute | solution.py:83
  66.5 12.8 %collective-permute-start.20 = (bf16[2,2,144,384]{3,2,0,1:T(8,128)(2,1)S(1)}, bf16[2,2,144,384]{3,2,0,1:T(8,128)(2,1)S(1)}, u32[]{:S(2)}, u32[]{:S(2)}) collective-permute-start(bf16[2,2,144,384]{3,2,0,1:T(8,128)(2,1)S(1)} %bitcast.223), channel_id=1, source_target_pairs={{0,1},{1,0},{2,3},{3,2},{4,5},{5,4},{6,7},{7,6},{8,9},{9,8},{10,11... | collective-permute-start | bytes 1327112 | tf_op jit(solution)/shard_map/ppermute | solution.py:86
  73.1 6.2 %collective-permute-start.18 = (bf16[528,384]{1,0:T(8,128)(2,1)S(1)}, bf16[528,384]{1,0:T(8,128)(2,1)S(1)}, u32[]{:S(2)}, u32[]{:S(2)}) collective-permute-start(bf16[528,384]{1,0:T(8,128)(2,1)S(1)} %slice_bitcast_fusion.1), channel_id=1, source_target_pairs={{0,2},{2,0},{4,6},{6,4},{8,10},{10,8},{12,14},{14,12},{16,18},{18,... | collective-permute-start | bytes 1216520 | tf_op jit(solution)/shard_map/ppermute | solution.py:242
  73.7 14.7 %collective-permute-start.23 = (bf16[2,2,144,384]{3,2,0,1:T(8,128)(2,1)S(1)}, bf16[2,2,144,384]{3,2,0,1:T(8,128)(2,1)S(1)}, u32[]{:S(2)}, u32[]{:S(2)}) collective-permute-start(bf16[2,2,144,384]{3,2,0,1:T(8,128)(2,1)S(1)} %bitcast.222), channel_id=1, source_target_pairs={{0,4},{2,6},{4,0},{6,2},{8,12},{10,14},{12,8},{14,10},{16,20},{18,... | collective-permute-start | bytes 1327112 | tf_op jit(solution)/shard_map/ppermute | solution.py:83
  75.1 13.6 %collective-permute-start.24 = (bf16[2,2,144,384]{3,2,0,1:T(8,128)(2,1)S(1)}, bf16[2,2,144,384]{3,2,0,1:T(8,128)(2,1)S(1)}, u32[]{:S(2)}, u32[]{:S(2)}) collective-permute-start(bf16[2,2,144,384]{3,2,0,1:T(8,128)(2,1)S(1)} %bitcast.225), channel_id=1, source_target_pairs={{0,1},{1,0},{2,3},{3,2},{4,5},{5,4},{6,7},{7,6},{8,9},{9,8},{10,11... | collective-permute-start | bytes 1327112 | tf_op jit(solution)/shard_map/ppermute | solution.py:86
  78.9 5.7 %collective-permute-start.25 = (bf16[512,384]{1,0:T(8,128)(2,1)S(1)}, bf16[512,384]{1,0:T(8,128)(2,1)S(1)}, u32[]{:S(2)}, u32[]{:S(2)}) collective-permute-start(bf16[512,384]{1,0:T(8,128)(2,1)S(1)} %slice_bitcast_fusion.2), channel_id=1, source_target_pairs={{0,2},{2,0},{4,6},{6,4},{8,10},{10,8},{12,14},{14,12},{16,18},{18,... | collective-permute-start | bytes 1179656 | tf_op jit(solution)/shard_map/ppermute | solution.py:241
  79.6 13.3 %collective-permute-start.21 = (bf16[2,144,384]{2,1,0:T(8,128)(2,1)S(1)}, bf16[2,144,384]{2,1,0:T(8,128)(2,1)S(1)}, u32[]{:S(2)}, u32[]{:S(2)}) collective-permute-start(bf16[2,144,384]{2,1,0:T(8,128)(2,1)S(1)} %dynamic-slice_bitcast_fusion.3), channel_id=1, source_target_pairs={{0,1},{1,0},{2,3},{3,2},{4,5},{5,4},{6,7},{7,6},{8,9},{9,8},{10,11... | collective-permute-start | bytes 663560 | tf_op jit(solution)/shard_map/ppermute | solution.py:86
  81.4 11.4 %collective-permute-start.22 = (bf16[2,144,384]{2,1,0:T(8,128)(2,1)S(1)}, bf16[2,144,384]{2,1,0:T(8,128)(2,1)S(1)}, u32[]{:S(2)}, u32[]{:S(2)}) collective-permute-start(bf16[2,144,384]{2,1,0:T(8,128)(2,1)S(1)} %dynamic-slice_bitcast_fusion.2), channel_id=1, source_target_pairs={{0,4},{2,6},{4,0},{6,2},{8,12},{10,14},{12,8},{14,10},{16,20},{18,... | collective-permute-start | bytes 663560 | tf_op jit(solution)/shard_map/ppermute | solution.py:83
  93.5 12.6 %collective-permute-start.28 = (bf16[144,384]{1,0:T(8,128)(2,1)S(1)}, bf16[144,384]{1,0:T(8,128)(2,1)S(1)}, u32[]{:S(2)}, u32[]{:S(2)}) collective-permute-start(bf16[144,384]{1,0:T(8,128)(2,1)S(1)} %get-tuple-element.90), channel_id=1, source_target_pairs={{0,24},{2,26},{4,28},{6,30},{8,0},{10,2},{12,4},{14,6},{16,8},{18,... | collective-permute-start | bytes 331784 | tf_op jit(solution)/shard_map/ppermute | solution.py:89
  96.9 11.8 %collective-permute-start.29 = (bf16[144,384]{1,0:T(8,128)(2,1)S(1)}, bf16[144,384]{1,0:T(8,128)(2,1)S(1)}, u32[]{:S(2)}, u32[]{:S(2)}) collective-permute-start(bf16[144,384]{1,0:T(8,128)(2,1)S(1)} %get-tuple-element.91), channel_id=1, source_target_pairs={{0,16},{2,18},{4,20},{6,22},{8,24},{10,26},{12,28},{14,30},{16,0},... | collective-permute-start | bytes 331784 | tf_op jit(solution)/shard_map/ppermute | solution.py:89
  98.8 9.9 %collective-permute-start.30 = (bf16[144,384]{1,0:T(8,128)(2,1)S(1)}, bf16[144,384]{1,0:T(8,128)(2,1)S(1)}, u32[]{:S(2)}, u32[]{:S(2)}) collective-permute-start(bf16[144,384]{1,0:T(8,128)(2,1)S(1)} %get-tuple-element.92), channel_id=1, source_target_pairs={{0,8},{2,10},{4,12},{6,14},{8,16},{10,18},{12,20},{14,22},{16,24},... | collective-permute-start | bytes 331784 | tf_op jit(solution)/shard_map/ppermute | solution.py:89
  103.0 6.1 %collective-permute-start.26 = (bf16[2,144,384]{2,1,0:T(8,128)(2,1)S(1)}, bf16[2,144,384]{2,1,0:T(8,128)(2,1)S(1)}, u32[]{:S(2)}, u32[]{:S(2)}) collective-permute-start(bf16[2,144,384]{2,1,0:T(8,128)(2,1)S(1)} %dynamic-slice_bitcast_fusion.1), channel_id=1, source_target_pairs={{0,1},{1,0},{2,3},{3,2},{4,5},{5,4},{6,7},{7,6},{8,9},{9,8},{10,11... | collective-permute-start | bytes 663560 | tf_op jit(solution)/shard_map/ppermute | solution.py:86
  104.5 5.9 %collective-permute-start.27 = (bf16[2,144,384]{2,1,0:T(8,128)(2,1)S(1)}, bf16[2,144,384]{2,1,0:T(8,128)(2,1)S(1)}, u32[]{:S(2)}, u32[]{:S(2)}) collective-permute-start(bf16[2,144,384]{2,1,0:T(8,128)(2,1)S(1)} %dynamic-slice_bitcast_fusion), channel_id=1, source_target_pairs={{0,4},{2,6},{4,0},{6,2},{8,12},{10,14},{12,8},{14,10},{16,20},{18,... | collective-permute-start | bytes 663560 | tf_op jit(solution)/shard_map/ppermute | solution.py:83
  110.8 6.8 %collective-permute-start.35 = (bf16[144,384]{1,0:T(8,128)(2,1)S(1)}, bf16[144,384]{1,0:T(8,128)(2,1)S(1)}, u32[]{:S(2)}, u32[]{:S(2)}) collective-permute-start(bf16[144,384]{1,0:T(8,128)(2,1)S(1)} %get-tuple-element.105), channel_id=1, source_target_pairs={{0,8},{2,10},{4,12},{6,14},{8,16},{10,18},{12,20},{14,22},{16,24},... | collective-permute-start | bytes 331784 | tf_op jit(solution)/shard_map/ppermute | solution.py:89
  110.9 9.3 %collective-permute-start.34 = (bf16[144,384]{1,0:T(8,128)(2,1)S(1)}, bf16[144,384]{1,0:T(8,128)(2,1)S(1)}, u32[]{:S(2)}, u32[]{:S(2)}) collective-permute-start(bf16[144,384]{1,0:T(8,128)(2,1)S(1)} %get-tuple-element.104), channel_id=1, source_target_pairs={{0,16},{2,18},{4,20},{6,22},{8,24},{10,26},{12,28},{14,30},{16,0},... | collective-permute-start | bytes 331784 | tf_op jit(solution)/shard_map/ppermute | solution.py:89
  113.3 6.8 %collective-permute-start.33 = (bf16[144,384]{1,0:T(8,128)(2,1)S(1)}, bf16[144,384]{1,0:T(8,128)(2,1)S(1)}, u32[]{:S(2)}, u32[]{:S(2)}) collective-permute-start(bf16[144,384]{1,0:T(8,128)(2,1)S(1)} %get-tuple-element.103), channel_id=1, source_target_pairs={{0,24},{2,26},{4,28},{6,30},{8,0},{10,2},{12,4},{14,6},{16,8},{18,... | collective-permute-start | bytes 331784 | tf_op jit(solution)/shard_map/ppermute | solution.py:89
  114.8 7.2 %collective-permute-start.32 = (bf16[144,384]{1,0:T(8,128)(2,1)S(1)}, bf16[144,384]{1,0:T(8,128)(2,1)S(1)}, u32[]{:S(2)}, u32[]{:S(2)}) collective-permute-start(bf16[144,384]{1,0:T(8,128)(2,1)S(1)} %fusion.98), channel_id=1, source_target_pairs={{0,1},{1,0},{2,3},{3,2},{4,5},{5,4},{6,7},{7,6},{8,9},{9,8},{10,11... | collective-permute-start | bytes 331784 | tf_op jit(solution)/shard_map/ppermute | solution.py:86
  (11 other events, 33.9 us)
